TPU v7x, 32 devices: a whole 2x2x4 slice. The times are simulated.
32 devices in a mesh: seq: 8 (over z, x), frame: 4 (over y, core).
Axes of the slice: x: 2, y: 2, z: 4, core: 2. Of those that a mesh axis runs over, the one named last changes fastest.
Arguments:
- media: bfloat16 [24, 4, 256, 1536], P('seq', 'frame'), may hold values from -6 to 6
- image_counts: int32 [24], P('seq'), may hold values from 0 to 4, as said below
- time_ids: int32 [24, 4], P('seq', 'frame'), may hold values from 0 to 3
- latents: bfloat16 [64, 1536], P(None, ('seq', 'frame')), may hold values from -6 to 6
- time_table: bfloat16 [4, 1536], P(None, ('seq', 'frame')), may hold values from -4 to 4
- media_gain: bfloat16 [1536], P(('seq', 'frame')), may hold values from 0.5 to 1.5
- latent_gain: bfloat16 [1536], P(('seq', 'frame')), may hold values from 0.5 to 1.5
- feed_gain: bfloat16 [1536], P(('seq', 'frame')), may hold values from 0.5 to 1.5
- query_weight: bfloat16 [1536, 1536], P(None, ('seq', 'frame')), may hold values from -0.15625 to 0.15625
- keyval_weight: bfloat16 [1536, 3072], P(None, ('seq', 'frame')), may hold values from -0.15625 to 0.15625
- output_weight: bfloat16 [1536, 1536], P(('seq', 'frame')), may hold values from -3.5 to 3.5
- up_weight: bfloat16 [1536, 6144], P('seq', 'frame'), may hold values from -0.15625 to 0.15625
- down_weight: bfloat16 [6144, 1536], P('frame', 'seq'), may hold values from -0.078125 to 0.078125
- cotangent: float32 [24, 64, 1536], P('seq', 'frame'), may hold values from -6 to 6
Outputs:
- new_latents: float32 [24, 64, 1536], P('seq', 'frame')
- media_grad: float32 [24, 4, 256, 1536], P('seq', 'frame')
- latents_grad: float32 [64, 1536], P(None, ('seq', 'frame'))
- table_grad: float32 [4, 1536], P(None, ('seq', 'frame'))
- media_gain_grad: float32 [1536], P(('seq', 'frame'))
- latent_gain_grad: float32 [1536], P(('seq', 'frame'))
- feed_gain_grad: float32 [1536], P(('seq', 'frame'))
- query_grad: float32 [1536, 1536], P(None, ('seq', 'frame'))
- keyval_grad: float32 [1536, 3072], P(None, ('seq', 'frame'))
- output_grad: float32 [1536, 1536], P(('seq', 'frame'))
- up_grad: float32 [1536, 6144], P('seq', 'frame')
- down_grad: float32 [6144, 1536], P('frame', 'seq')
Inputs may be any that keep to these rules, and one draw needn't show every extreme that they name: `image_counts`: in each aligned block of 3 sequences (those of one index of seq) one sequence has 4 images; a sequence with c images uses slots 0 to c - 1.
All inputs are finite; a program needn't handle non-finite values.
Results may differ from a plain program's by a relative error of at most 0.023.
Values may be sent and summed in bfloat16 or wider, within the bound.
No kernel may reach another device: no remote copies, remote signals or barrier semaphores. Data moves between devices by JAX's collectives and lax.ppermute only.
A program may use at most 320 MiB of HBM per device.

v0:
```python
import jax
import jax.numpy as jnp
from jax import lax
from jax.sharding import PartitionSpec as P

HEADS = 16


EPS = 1e-05
NEGATIVE = -1e30
HIGHEST = lax.Precision.HIGHEST


def merged(value, axis, join):
    pieces = jax.tree.map(lambda part: lax.all_gather(part, axis), value)
    head = jax.tree.map(lambda part: part[0], pieces)
    tail = jax.tree.map(lambda part: part[1:], pieces)
    running, _ = lax.scan(lambda running, share: (join(running, share), None), head, tail)
    return running


def normalize(values):
    center = values - jnp.mean(values, -1, keepdims=True)
    scale_inv = lax.rsqrt(jnp.mean(center * center, -1, keepdims=True) + EPS)
    return (center * scale_inv, scale_inv)


def norm_back(grad_hat, normed, scale_inv):
    return scale_inv * (
        grad_hat
        - jnp.mean(grad_hat, -1, keepdims=True)
        - normed * jnp.mean(grad_hat * normed, -1, keepdims=True)
    )


def matmul(first_op, second_op):
    return jnp.dot(first_op, second_op, preferred_element_type=jnp.float32)


def matmul_tn(first_op, second_op):
    return lax.dot_general(
        first_op, second_op, (((0,), (0,)), ((), ())), preferred_element_type=jnp.float32
    )


def matmul_nt(first_op, second_op):
    return lax.dot_general(
        first_op, second_op, (((1,), (1,)), ((), ())), preferred_element_type=jnp.float32
    )


def exact_gelu(values):
    return jax.nn.gelu(values, approximate=False)


def combine_stats(former, latter):
    top_score = jnp.maximum(former[0], latter[0])
    return (
        top_score,
        former[1] * jnp.exp(former[0] - top_score) + latter[1] * jnp.exp(latter[0] - top_score),
    )


def frame_major(values, axis_dim, seq_count, frame_count):
    shape = values.shape
    piece = shape[axis_dim] // (seq_count * frame_count)
    split = values.reshape(
        shape[:axis_dim] + (seq_count, frame_count, piece) + shape[axis_dim + 1 :]
    )
    return jnp.swapaxes(split, axis_dim, axis_dim + 1).reshape(shape)


def local(
    media,
    image_counts,
    time_ids,
    latents,
    time_table,
    media_gain,
    latent_gain,
    feed_gain,
    query_weight,
    keyval_weight,
    output_weight,
    up_weight,
    down_weight,
    cotangent,
):
    gathered = (
        lax.all_gather(latents, ("seq", "frame"), axis=1, tiled=True),
        lax.all_gather(time_table, ("seq", "frame"), axis=1, tiled=True),
        lax.all_gather(media_gain, ("seq", "frame"), axis=0, tiled=True),
        lax.all_gather(latent_gain, ("seq", "frame"), axis=0, tiled=True),
        lax.all_gather(feed_gain, ("seq", "frame"), axis=0, tiled=True),
        lax.all_gather(query_weight, ("seq", "frame"), axis=1, tiled=True),
        lax.all_gather(keyval_weight, ("seq", "frame"), axis=1, tiled=True),
        lax.all_gather(output_weight, ("seq", "frame"), axis=0, tiled=True),
    )
    lat_all, table_all, norm_media, norm_latent, norm_feed, query_full, keyval_full, output_full = (
        gathered
    )
    up_seq, down_seq = (
        lax.all_gather(up_weight, "seq", axis=0, tiled=True),
        lax.all_gather(down_weight, "seq", axis=1, tiled=True),
    )
    up_use, down_use = (
        lax.all_gather(up_seq, "frame", axis=1, tiled=True),
        lax.all_gather(down_seq, "frame", axis=0, tiled=True),
    )
    model_width = query_full.shape[0]
    head_dim = model_width // HEADS
    factor = head_dim ** (-0.5)
    frame_count = lax.axis_size("frame")
    seq_count = lax.axis_size("seq")
    slot_index = lax.axis_index("frame")
    seq_here = media.shape[0]
    patch_count = media.shape[2]
    lat_rows = lat_all.shape[0]
    own_rows = lat_rows // frame_count
    first_row = slot_index * own_rows
    is_valid = slot_index < image_counts
    onehot = (
        time_ids[:, 0][:, None] == jnp.arange(table_all.shape[0], dtype=jnp.int32)[None, :]
    ).astype(jnp.float32)
    embedding = jnp.dot(onehot, table_all.astype(jnp.float32), precision=HIGHEST)
    embedded = media[:, 0].astype(jnp.float32) + embedding[:, None, :]
    normed_media, inv_media = normalize(embedded.reshape(seq_here * patch_count, model_width))
    media_scale = norm_media.astype(jnp.float32)
    hidden_media = (normed_media * media_scale).astype(jnp.bfloat16)
    media_kv = matmul(hidden_media, keyval_full).astype(jnp.bfloat16)
    media_keys = media_kv[:, :model_width].reshape(seq_here, patch_count, HEADS, head_dim)
    media_vals = media_kv[:, model_width:].reshape(seq_here, patch_count, HEADS, head_dim)
    lat_float = lat_all.astype(jnp.float32)
    normed_lat, inv_lat = normalize(lat_float)
    latent_scale = norm_latent.astype(jnp.float32)
    hidden_lat = (normed_lat * latent_scale).astype(jnp.bfloat16)
    queries = matmul(hidden_lat, query_full).astype(jnp.bfloat16).reshape(lat_rows, HEADS, head_dim)
    hidden_own = lax.dynamic_slice_in_dim(hidden_lat, first_row, own_rows, 0)
    own_kv = matmul(hidden_own, keyval_full).astype(jnp.bfloat16)
    own_keys = own_kv[:, :model_width].reshape(own_rows, HEADS, head_dim)
    own_vals = own_kv[:, model_width:].reshape(own_rows, HEADS, head_dim)
    media_scores = (
        jnp.einsum("lhe,sphe->shlp", queries, media_keys, preferred_element_type=jnp.float32)
        * factor
    )
    media_scores = jnp.where(is_valid[:, None, None, None], media_scores, NEGATIVE)
    own_scores = (
        jnp.einsum("lhe,rhe->hlr", queries, own_keys, preferred_element_type=jnp.float32)[None]
        * factor
    )
    local_top = jnp.maximum(jnp.max(media_scores, -1), jnp.max(own_scores, -1))
    local_sum = jnp.sum(jnp.exp(media_scores - local_top[..., None]), -1) + jnp.sum(
        jnp.exp(own_scores - local_top[..., None]), -1
    )
    top_score, sum_total = merged((local_top, local_sum), "frame", combine_stats)
    log_total = (top_score + jnp.log(sum_total))[..., None]
    media_probs = jnp.exp(media_scores - log_total)
    own_probs = jnp.exp(own_scores - log_total)
    media_low = media_probs.astype(jnp.bfloat16)
    own_low = own_probs.astype(jnp.bfloat16)
    partial_value = jnp.einsum(
        "shlp,sphe->slhe", media_low, media_vals, preferred_element_type=jnp.float32
    )
    partial_value = partial_value + jnp.einsum(
        "shlr,rhe->slhe", own_low, own_vals, preferred_element_type=jnp.float32
    )
    context = lax.psum_scatter(
        partial_value.reshape(seq_here, lat_rows, model_width).astype(jnp.bfloat16),
        "frame",
        scatter_dimension=1,
        tiled=True,
    )
    context_low = context.reshape(seq_here * own_rows, model_width)
    lat_own = lax.dynamic_slice_in_dim(lat_float, first_row, own_rows, 0)
    mixed = jnp.tile(lat_own, (seq_here, 1)) + matmul(context_low, output_full)
    normed_feed, inv_feed = normalize(mixed)
    feed_scale = norm_feed.astype(jnp.float32)
    hidden_feed = (normed_feed * feed_scale).astype(jnp.bfloat16)
    grad_out = cotangent.reshape(seq_here * own_rows, model_width)
    grad_low = grad_out.astype(jnp.bfloat16)
    feed_rows, grad_rows = (hidden_feed, grad_low)
    up_pre = matmul(feed_rows, up_use)
    hidden_act = exact_gelu(up_pre).astype(jnp.bfloat16)
    down_out = matmul(hidden_act, down_use)
    grad_act = matmul_nt(grad_rows, down_use)
    unused, gelu_pullback = jax.vjp(exact_gelu, up_pre)
    grad_up = gelu_pullback(grad_act)[0].astype(jnp.bfloat16)
    grad_feed = matmul_nt(grad_up, up_use)
    down_part = matmul_tn(hidden_act, grad_rows)
    up_part = matmul_tn(feed_rows, grad_up)
    new_latents = (mixed + down_out).reshape(seq_here, own_rows, model_width)
    up_part, down_part = (
        lax.psum_scatter(
            up_part.astype(jnp.bfloat16), "frame", scatter_dimension=1, tiled=True
        ).astype(jnp.float32),
        lax.psum_scatter(
            down_part.astype(jnp.bfloat16), "frame", scatter_dimension=0, tiled=True
        ).astype(jnp.float32),
    )
    up_grad, down_grad = (
        lax.psum_scatter(
            up_part.astype(jnp.bfloat16), "seq", scatter_dimension=0, tiled=True
        ).astype(jnp.float32),
        lax.psum_scatter(
            down_part.astype(jnp.bfloat16), "seq", scatter_dimension=1, tiled=True
        ).astype(jnp.float32),
    )
    feed_gain_part = jnp.sum(grad_feed * normed_feed, 0)
    grad_mixed = grad_out + norm_back(grad_feed * feed_scale, normed_feed, inv_feed)
    grad_mixed_low = grad_mixed.astype(jnp.bfloat16)
    output_part = matmul_tn(context_low, grad_mixed_low)
    grad_context = (
        matmul_nt(grad_mixed_low, output_full)
        .astype(jnp.bfloat16)
        .reshape(seq_here, own_rows, model_width)
    )
    grad_full = lax.all_gather(grad_context, "frame", axis=1, tiled=True).reshape(
        seq_here, lat_rows, HEADS, head_dim
    )
    media_dots = jnp.einsum(
        "slhe,sphe->shlp", grad_full, media_vals, preferred_element_type=jnp.float32
    )
    own_dots = jnp.einsum("slhe,rhe->shlr", grad_full, own_vals, preferred_element_type=jnp.float32)
    row_part = jnp.sum(media_probs * media_dots, -1) + jnp.sum(own_probs * own_dots, -1)
    row_total = lax.psum(row_part, "frame")[..., None]
    media_ds = (media_probs * (media_dots - row_total)).astype(jnp.bfloat16)
    own_ds = (own_probs * (own_dots - row_total)).astype(jnp.bfloat16)
    query_part = jnp.einsum(
        "shlp,sphe->lhe", media_ds, media_keys, preferred_element_type=jnp.float32
    )
    query_part = (
        query_part
        + jnp.einsum("shlr,rhe->lhe", own_ds, own_keys, preferred_element_type=jnp.float32)
    ) * factor
    media_dk = (
        jnp.einsum("shlp,lhe->sphe", media_ds, queries, preferred_element_type=jnp.float32) * factor
    )
    media_dv = jnp.einsum(
        "shlp,slhe->sphe", media_low, grad_full, preferred_element_type=jnp.float32
    )
    grad_media_kv = jnp.concatenate(
        [
            media_dk.reshape(seq_here * patch_count, model_width),
            media_dv.reshape(seq_here * patch_count, model_width),
        ],
        1,
    ).astype(jnp.bfloat16)
    keyval_part = matmul_tn(hidden_media, grad_media_kv)
    grad_hidden_media = matmul_nt(grad_media_kv, keyval_full)
    media_gain_part = jnp.sum(grad_hidden_media * normed_media, 0)
    grad_embedded = norm_back(grad_hidden_media * media_scale, normed_media, inv_media).reshape(
        seq_here, patch_count, model_width
    )
    table_part = jnp.dot(onehot.T, jnp.sum(grad_embedded, 1), precision=HIGHEST)
    own_dk = (
        jnp.einsum("shlr,lhe->rhe", own_ds, queries, preferred_element_type=jnp.float32) * factor
    )
    own_dv = jnp.einsum("shlr,slhe->rhe", own_low, grad_full, preferred_element_type=jnp.float32)
    own_grad = jnp.concatenate(
        [own_dk.reshape(own_rows, model_width), own_dv.reshape(own_rows, model_width)], 1
    )
    keyval_rows = lax.dynamic_update_slice_in_dim(
        jnp.zeros((lat_rows, 2 * model_width), jnp.float32), own_grad, first_row, 0
    )
    query_cols, keyval_cols = (
        lax.psum_scatter(
            query_part.reshape(lat_rows, model_width),
            ("seq", "frame"),
            scatter_dimension=1,
            tiled=True,
        ),
        lax.psum_scatter(keyval_rows, ("seq", "frame"), scatter_dimension=1, tiled=True),
    )
    query_low = query_cols.astype(jnp.bfloat16)
    keyval_low = keyval_cols.astype(jnp.bfloat16)
    query_grad = matmul_tn(hidden_lat, query_low)
    keyval_latent = matmul_tn(hidden_lat, keyval_low)
    grad_hidden_lat = matmul_nt(query_low, query_weight) + matmul_nt(keyval_low, keyval_weight)
    latent_gain_part = jnp.sum(grad_hidden_lat * normed_lat, 0)
    residual_rows = jnp.sum(grad_mixed.reshape(seq_here, own_rows, model_width), 0)
    latents_part = norm_back(grad_hidden_lat * latent_scale, normed_lat, inv_lat)
    latents_part = latents_part + lax.dynamic_update_slice_in_dim(
        jnp.zeros((lat_rows, model_width), jnp.float32), residual_rows, first_row, 0
    )
    terms = (
        latents_part,
        table_part,
        media_gain_part,
        latent_gain_part,
        feed_gain_part,
        keyval_part,
        output_part,
    )
    term_dims = (1, 1, 0, 0, 0, 1, 0)
    reordered = tuple(
        (
            frame_major(item, item_dim, seq_count, frame_count)
            for item, item_dim in zip(terms, term_dims)
        )
    )
    framed = (
        lax.psum_scatter(
            reordered[0].astype(jnp.bfloat16), "frame", scatter_dimension=1, tiled=True
        ).astype(jnp.float32),
        lax.psum_scatter(
            reordered[1].astype(jnp.bfloat16), "frame", scatter_dimension=1, tiled=True
        ).astype(jnp.float32),
        lax.psum_scatter(
            reordered[2].astype(jnp.bfloat16), "frame", scatter_dimension=0, tiled=True
        ).astype(jnp.float32),
        lax.psum_scatter(
            reordered[3].astype(jnp.bfloat16), "frame", scatter_dimension=0, tiled=True
        ).astype(jnp.float32),
        lax.psum_scatter(
            reordered[4].astype(jnp.bfloat16), "frame", scatter_dimension=0, tiled=True
        ).astype(jnp.float32),
        lax.psum_scatter(
            reordered[5].astype(jnp.bfloat16), "frame", scatter_dimension=1, tiled=True
        ).astype(jnp.float32),
        lax.psum_scatter(
            reordered[6].astype(jnp.bfloat16), "frame", scatter_dimension=0, tiled=True
        ).astype(jnp.float32),
    )
    summed = (
        lax.psum_scatter(
            framed[0].astype(jnp.bfloat16), "seq", scatter_dimension=1, tiled=True
        ).astype(jnp.float32),
        lax.psum_scatter(
            framed[1].astype(jnp.bfloat16), "seq", scatter_dimension=1, tiled=True
        ).astype(jnp.float32),
        lax.psum_scatter(
            framed[2].astype(jnp.bfloat16), "seq", scatter_dimension=0, tiled=True
        ).astype(jnp.float32),
        lax.psum_scatter(
            framed[3].astype(jnp.bfloat16), "seq", scatter_dimension=0, tiled=True
        ).astype(jnp.float32),
        lax.psum_scatter(
            framed[4].astype(jnp.bfloat16), "seq", scatter_dimension=0, tiled=True
        ).astype(jnp.float32),
        lax.psum_scatter(
            framed[5].astype(jnp.bfloat16), "seq", scatter_dimension=1, tiled=True
        ).astype(jnp.float32),
        lax.psum_scatter(
            framed[6].astype(jnp.bfloat16), "seq", scatter_dimension=0, tiled=True
        ).astype(jnp.float32),
    )
    (
        latents_grad,
        table_grad,
        media_gain_grad,
        latent_gain_grad,
        feed_gain_grad,
        keyval_media,
        output_grad,
    ) = summed
    keyval_grad = keyval_media + keyval_latent
    media_grad = grad_embedded[:, None]
    return (
        new_latents,
        media_grad,
        latents_grad,
        table_grad,
        media_gain_grad,
        latent_gain_grad,
        feed_gain_grad,
        query_grad,
        keyval_grad,
        output_grad,
        up_grad,
        down_grad,
    )


def solution(mesh):
    return jax.shard_map(
        local,
        mesh=mesh,
        in_specs=(
            P("seq", "frame", None, None),
            P("seq"),
            P("seq", "frame"),
            P(None, ("seq", "frame")),
            P(None, ("seq", "frame")),
            P(("seq", "frame")),
            P(("seq", "frame")),
            P(("seq", "frame")),
            P(None, ("seq", "frame")),
            P(None, ("seq", "frame")),
            P(("seq", "frame"), None),
            P("seq", "frame"),
            P("frame", "seq"),
            P("seq", "frame", None),
        ),
        out_specs=(
            P("seq", "frame", None),
            P("seq", "frame", None, None),
            P(None, ("seq", "frame")),
            P(None, ("seq", "frame")),
            P(("seq", "frame")),
            P(("seq", "frame")),
            P(("seq", "frame")),
            P(None, ("seq", "frame")),
            P(None, ("seq", "frame")),
            P(("seq", "frame"), None),
            P("seq", "frame"),
            P("frame", "seq"),
        ),
        check_vma=False,
    )
```

profile of v0, /device:TPU:0, one launch (start us, length us, event | category | flops | bytes accessed | tf_op | source)
XLA Modules:
  0.0 1854.8 jit_solution(15838547174743569386)
XLA Ops:
  10.7 43.6 %all-gather.1 = bf16[32,48,4]{1,2,0:T(4,128)(2,1)S(1)} all-gather(bf16[1,48,4]{1,2,0:T(4,128)(2,1)} %bitcast.259), channel_id=1, replica_groups=mesh['seq'=8,'frame'=4] {'seq','frame'}, dimensions={0}, use_global_device_ids=true | all-gather | bytes 12672 | tf_op jit(solution)/shard_map/all_gather | solution.py:91
  57.5 38.6 %all_gather.47 = bf16[64,1536]{0,1:T(8,128)(2,1)S(1)} all-gather(bf16[64,48]{0,1:T(8,128)(2,1)S(1)} %copy-done.46), channel_id=1, replica_groups=mesh['seq'=8,'frame'=4] {'seq','frame'}, dimensions={1}, use_global_device_ids=true | all-gather | bytes 202752 | tf_op jit(solution)/shard_map/all_gather | solution.py:90
  97.1 38.1 %all-reduce.9 = (bf16[1536]{0:T(1024)(128)(2,1)S(1)}, bf16[1536]{0:T(1024)(128)(2,1)S(1)}, bf16[1536]{0:T(1024)(128)(2,1)}) all-reduce(bf16[1536]{0:T(1024)(128)(2,1)S(1)} %dynamic-update-slice.1, bf16[1536]{0:T(1024)(128)(2,1)S(1)} %dynamic-update-slice.2, ...), channel_id=1, replica_groups=mesh['seq'=8,'frame'=4] {'seq','frame'}, use_global_device_ids=true, to_apply=%add | all-reduce | flops 4608 | bytes 18432
  144.4 19.2 %all-gather.10.cloned.1.call-done = bf16[1536,3072]{0,1:T(8,128)(2,1)} async-done(((bf16[1536,96]{0,1:T(8,128)(2,1)}), bf16[1536,3072]{0,1:T(8,128)(2,1)}) %all-gather.10.cloned.1.call-update) | async-done | bytes 9437200 | tf_op jit(solution)/shard_map/all_gather | solution.py:96
  227.6 16.6 all-gather.16.cloned.1.call-done
  244.2 80.0 %all-gather.20.cloned.1.call-done = bf16[1536,1536]{0,1:T(8,128)(2,1)} async-done(((bf16[1536,192]{0,1:T(8,128)(2,1)}), bf16[1536,1536]{0,1:T(8,128)(2,1)}) %all-gather.20.cloned.1.call-update) | async-done | bytes 4718608 | tf_op jit(solution)/shard_map/all_gather | solution.py:104
  326.1 62.7 %all-gather.14.cloned.1.call-done = bf16[1536,1536]{1,0:T(8,128)(2,1)} async-done(((bf16[48,1536]{1,0:T(8,128)(2,1)}), bf16[1536,1536]{1,0:T(8,128)(2,1)}) %all-gather.14.cloned.1.call-update) | async-done | bytes 4718608 | tf_op jit(solution)/shard_map/all_gather | solution.py:97
  388.7 23.8 %reduce-scatter.30.cloned.1.call-done = bf16[3,16,1536]{2,1,0:T(8,128)(2,1)} async-done(((bf16[3,64,1536]{2,1,0:T(8,128)(2,1)}), bf16[3,16,1536]{2,1,0:T(8,128)(2,1)}) %reduce-scatter.30.cloned.1.call-update) | async-done | bytes 147472 | tf_op jit(solution)/shard_map/reduce_scatter | solution.py:167
  416.3 117.9 %all-gather.18.cloned.1.call-done = bf16[1536,6144]{1,0:T(8,128)(2,1)} async-done(((bf16[1536,1536]{1,0:T(8,128)(2,1)}), bf16[1536,6144]{1,0:T(8,128)(2,1)}) %all-gather.18.cloned.1.call-update) | async-done | bytes 18874384 | tf_op jit(solution)/shard_map/all_gather | solution.py:107
  545.0 110.8 %all-gather.22.cloned.1.call-done = bf16[6144,1536]{0,1:T(8,128)(2,1)} async-done(((bf16[1536,1536]{0,1:T(8,128)(2,1)}), bf16[6144,1536]{0,1:T(8,128)(2,1)}) %all-gather.22.cloned.1.call-update) | async-done | bytes 18874384 | tf_op jit(solution)/shard_map/all_gather | solution.py:108
  669.4 13.8 multiply_reduce_fusion.10
  796.5 28.9 %reduce-scatter.46.cloned.1.call-done = f32[48,64]{1,0:T(8,128)} async-done(((f32[1536,64]{1,0:T(8,128)}), f32[48,64]{1,0:T(8,128)}) %reduce-scatter.46.cloned.1.call-update) | async-done | bytes 12304
  828.1 98.5 %reduce-scatter.48.cloned.1.call-done = f32[96,64]{1,0:T(8,128)} async-done(((f32[3072,64]{1,0:T(8,128)}), f32[96,64]{1,0:T(8,128)}) %reduce-scatter.48.cloned.1.call-update) | async-done | bytes 24592
  992.3 30.3 %reduce-scatter.36.cloned.1.call-done = bf16[384,1536]{1,0:T(8,128)(2,1)} async-done(((bf16[1536,1536]{1,0:T(8,128)(2,1)}), bf16[384,1536]{1,0:T(8,128)(2,1)}) %reduce-scatter.36.cloned.1.call-update) | async-done | bytes 1179664 | tf_op jit(solution)/shard_map/reduce_scatter | solution.py:320
  1022.7 81.0 %reduce-scatter.32.cloned.1.call-done = bf16[1536,768]{0,1:T(8,128)(2,1)} async-done(((bf16[1536,3072]{0,1:T(8,128)(2,1)}), bf16[1536,768]{0,1:T(8,128)(2,1)}) %reduce-scatter.32.cloned.1.call-update) | async-done | bytes 2359312 | tf_op jit(solution)/shard_map/reduce_scatter | solution.py:317
  1103.8 142.0 %reduce-scatter.44.cloned.1.call-done = bf16[1536,1536]{1,0:T(8,128)(2,1)} async-done(((bf16[6144,1536]{1,0:T(8,128)(2,1)}), bf16[1536,1536]{1,0:T(8,128)(2,1)}) %reduce-scatter.44.cloned.1.call-update) | async-done | bytes 4718608 | tf_op jit(solution)/shard_map/reduce_scatter | solution.py:196
  1252.7 135.1 %reduce-scatter.40.cloned.1.call-done = bf16[1536,1536]{1,0:T(8,128)(2,1)} async-done(((bf16[1536,6144]{1,0:T(8,128)(2,1)}), bf16[1536,1536]{1,0:T(8,128)(2,1)}) %reduce-scatter.40.cloned.1.call-update) | async-done | bytes 4718608 | tf_op jit(solution)/shard_map/reduce_scatter | solution.py:193
  1403.6 45.3 %reduce-scatter.56.cloned.1.call-done = bf16[48,4]{1,0:T(8,128)(2,1)} async-done(((bf16[384,4]{1,0:T(8,128)(2,1)}), bf16[48,4]{1,0:T(8,128)(2,1)}) %reduce-scatter.56.cloned.1.call-update) | async-done | bytes 400
  1461.8 19.5 %all-reduce.10 = (bf16[384]{0:T(512)(128)(2,1)S(1)}, bf16[384]{0:T(512)(128)(2,1)S(1)}, bf16[384]{0:T(512)(128)(2,1)S(1)}) all-reduce(bf16[384]{0:T(512)(128)(2,1)S(1)} %dynamic-slice.2, bf16[384]{0:T(512)(128)(2,1)S(1)} %dynamic-slice.6, bf16[384]{0:T(512)(128)(2,1)S(1)} %dynamic-slice.10), channel_id=11, replica_groups=mesh['seq'=8,'frame'=4] {'seq'}, use_global_device_ids=true, to_apply=%region_33.34.clone | all-reduce | flops 1152 | bytes 4608
  1483.0 26.2 %reduce-scatter.52.cloned.1.call-done = bf16[48,64]{1,0:T(8,128)(2,1)} async-done(((bf16[384,64]{1,0:T(8,128)(2,1)}), bf16[48,64]{1,0:T(8,128)(2,1)}) %reduce-scatter.52.cloned.1.call-update) | async-done | bytes 6160
  1510.7 65.4 %reduce-scatter.38.cloned.1.call-done = bf16[48,1536]{1,0:T(8,128)(2,1)} async-done(((bf16[384,1536]{1,0:T(8,128)(2,1)}), bf16[48,1536]{1,0:T(8,128)(2,1)}) %reduce-scatter.38.cloned.1.call-update) | async-done | bytes 147472 | tf_op jit(solution)/shard_map/reduce_scatter | solution.py:343
  1577.8 70.3 %reduce-scatter.34.cloned.1.call-done = bf16[1536,96]{0,1:T(8,128)(2,1)} async-done(((bf16[1536,768]{0,1:T(8,128)(2,1)}), bf16[1536,96]{0,1:T(8,128)(2,1)}) %reduce-scatter.34.cloned.1.call-update) | async-done | bytes 294928 | tf_op jit(solution)/shard_map/reduce_scatter | solution.py:340
  1650.1 96.4 %reduce-scatter.58.cloned.1.call-done = bf16[192,1536]{1,0:T(8,128)(2,1)} async-done(((bf16[1536,1536]{1,0:T(8,128)(2,1)}), bf16[192,1536]{1,0:T(8,128)(2,1)}) %reduce-scatter.58.cloned.1.call-update) | async-done | bytes 589840
  1749.1 96.5 %reduce-scatter.42.cloned.1.call-done = bf16[192,1536]{1,0:T(8,128)(2,1)} async-done(((bf16[1536,1536]{1,0:T(8,128)(2,1)}), bf16[192,1536]{1,0:T(8,128)(2,1)}) %reduce-scatter.42.cloned.1.call-update) | async-done | bytes 589840 | tf_op jit(solution)/shard_map/reduce_scatter | solution.py:201
  (328 shorter events, 340.1 us)
Async XLA Ops:
  7.2 132.3 %all-gather.12.cloned.1.call-start = ((), (), s32[]{:S(2)}) async-start(), calls=%async_computation.16 | async-start | bytes 4866048 | tf_op jit(solution)/shard_map/all_gather | solution.py:95
  8.0 155.6 %all-gather.10.cloned.1.call-start = ((), (), s32[]{:S(2)}) async-start(), calls=%async_computation.15 | async-start | bytes 9732096 | tf_op jit(solution)/shard_map/all_gather | solution.py:96
  8.7 235.4 %all-gather.16.cloned.1.call-start = ((), (), s32[]{:S(2)}) async-start(), calls=%async_computation.19 | async-start | bytes 5308416 | tf_op jit(solution)/shard_map/all_gather | solution.py:103
  9.4 314.8 %all-gather.20.cloned.1.call-start = ((), (), s32[]{:S(2)}) async-start(), calls=%async_computation.21 | async-start | bytes 5308416 | tf_op jit(solution)/shard_map/all_gather | solution.py:104
  10.0 378.7 %all-gather.14.cloned.1.call-start = ((), (), s32[]{:S(2)}) async-start(), calls=%async_computation.18 | async-start | bytes 4866048 | tf_op jit(solution)/shard_map/all_gather | solution.py:97
  10.6 402.0 %reduce-scatter.30.cloned.1.call-start = ((), (), s32[]{:S(2)}) async-start(), calls=%async_computation.17 | async-start | bytes 737280 | tf_op jit(solution)/shard_map/reduce_scatter | solution.py:167
  227.5 306.7 %all-gather.18.cloned.1.call-start = ((), (), s32[]{:S(2)}) async-start(), calls=%async_computation.20 | async-start | bytes 23592960 | tf_op jit(solution)/shard_map/all_gather | solution.py:107
  244.2 411.6 %all-gather.22.cloned.1.call-start = ((), (), s32[]{:S(2)}) async-start(), calls=%async_computation.22 | async-start | bytes 23592960 | tf_op jit(solution)/shard_map/all_gather | solution.py:108
  324.3 501.2 %reduce-scatter.46.cloned.1.call-start = ((), (), s32[]{:S(2)}) async-start(), calls=%async_computation.30 | async-start | bytes 811008
  416.1 267.2 %copy-start.38 = (f32[48]{0:T(128)}, f32[48]{0:T(128)S(1)}, u32[]{:S(2)}) copy-start(f32[48]{0:T(128)S(1)} %broadcast_multiply_fusion.5) | copy-start | bytes 580
  416.3 266.9 %copy-start.40 = (f32[48]{0:T(128)}, f32[48]{0:T(128)S(1)}, u32[]{:S(2)}) copy-start(f32[48]{0:T(128)S(1)} %add_rsqrt_fusion.1) | copy-start | bytes 580
  728.8 197.8 %reduce-scatter.48.cloned.1.call-start = ((), (), s32[]{:S(2)}) async-start(), calls=%async_computation.31 | async-start | bytes 1622016
  759.3 231.9 %reduce-scatter.54.cloned.1.call-start = ((), (), s32[]{:S(2)}) async-start(), calls=%async_computation.34 | async-start | bytes 491520
  796.5 195.3 %reduce-scatter.50.cloned.1.call-start = ((), (), s32[]{:S(2)}) async-start(), calls=%async_computation.32 | async-start | bytes 491520
  933.7 88.9 %reduce-scatter.36.cloned.1.call-start = ((), (), s32[]{:S(2)}) async-start(), calls=%async_computation.25 | async-start | bytes 5898240 | tf_op jit(solution)/shard_map/reduce_scatter | solution.py:320
  939.6 164.2 %reduce-scatter.32.cloned.1.call-start = ((), (), s32[]{:S(2)}) async-start(), calls=%async_computation.23 | async-start | bytes 11796480 | tf_op jit(solution)/shard_map/reduce_scatter | solution.py:317
  969.6 276.3 %reduce-scatter.44.cloned.1.call-start = ((), (), s32[]{:S(2)}) async-start(), calls=%async_computation.29 | async-start | bytes 23592960 | tf_op jit(solution)/shard_map/reduce_scatter | solution.py:196
  980.7 407.1 %reduce-scatter.40.cloned.1.call-start = ((), (), s32[]{:S(2)}) async-start(), calls=%async_computation.27 | async-start | bytes 23592960 | tf_op jit(solution)/shard_map/reduce_scatter | solution.py:193
  991.1 457.8 %reduce-scatter.56.cloned.1.call-start = ((), (), s32[]{:S(2)}) async-start(), calls=%async_computation.35 | async-start | bytes 110592
  991.7 517.5 %reduce-scatter.52.cloned.1.call-start = ((), (), s32[]{:S(2)}) async-start(), calls=%async_computation.33 | async-start | bytes 110592
  992.3 583.8 %reduce-scatter.38.cloned.1.call-start = ((), (), s32[]{:S(2)}) async-start(), calls=%async_computation.26 | async-start | bytes 1327104 | tf_op jit(solution)/shard_map/reduce_scatter | solution.py:343
  1022.6 625.4 %reduce-scatter.34.cloned.1.call-start = ((), (), s32[]{:S(2)}) async-start(), calls=%async_computation.24 | async-start | bytes 2654208 | tf_op jit(solution)/shard_map/reduce_scatter | solution.py:340
  1103.7 642.7 %reduce-scatter.58.cloned.1.call-start = ((), (), s32[]{:S(2)}) async-start(), calls=%async_computation.36 | async-start | bytes 5308416
  1252.5 593.1 %reduce-scatter.42.cloned.1.call-start = ((), (), s32[]{:S(2)}) async-start(), calls=%async_computation.28 | async-start | bytes 5308416 | tf_op jit(solution)/shard_map/reduce_scatter | solution.py:201
  (57 other events, 2260.7 us)
Sparse Core Ops, SparseCore 0:
  11.0 67.5 all-gather.11
  81.5 81.9 all-gather.9
  165.7 78.3 all-gather.15
  246.2 78.0 all-gather.19
  327.0 61.7 all-gather.13
  391.7 20.8 reduce-scatter.29
  414.2 120.0 all-gather.17
  535.8 119.9 all-gather.21
  728.9 96.4 reduce-scatter.45
  830.5 96.0 reduce-scatter.47
  929.1 19.8 reduce-scatter.53
  951.4 20.8 reduce-scatter.49
  974.8 47.8 reduce-scatter.35
  1025.2 78.4 reduce-scatter.31
  1106.3 139.4 reduce-scatter.43
  1248.3 139.5 reduce-scatter.39
  1391.3 57.5 reduce-scatter.55
  1452.3 56.7 reduce-scatter.51
  1513.0 63.1 reduce-scatter.37
  1579.9 68.1 reduce-scatter.33
  1652.1 94.2 reduce-scatter.57
  1750.5 95.0 reduce-scatter.41
where the time goes:
time: 1860 us; the launch traced here: 1850 us
  waiting for transfers between devices  1350 us (73%)
  blocking collectives  180 us (10%)
  matrix products  158 us (8%)
  local copies, waits for them, and re-layouts  110 us (6%)
  other arithmetic  36.1 us (2%)
    unnamed x29, waiting for transfers between devices  300 us
    reduce_scatter x1, waiting for transfers between devices, local(): lax.psum_scatter(down_part.astype(jnp.bfloat16), 'frame', scatter_dimensi...  142 us
    reduce_scatter x1, waiting for transfers between devices, local(): lax.psum_scatter(up_part.astype(jnp.bfloat16), 'frame', scatter_dimension...  135 us
    all_gather x1, waiting for transfers between devices, local(): lax.all_gather(up_seq, 'frame', axis=1, tiled=True)  118 us
    all_gather x1, waiting for transfers between devices, local(): lax.all_gather(down_seq, 'frame', axis=0, tiled=True)  111 us
    reduce_scatter x1, waiting for transfers between devices, local(): lax.psum_scatter(up_part.astype(jnp.bfloat16), 'seq', scatter_dimension=0...  96.5 us
    reduce_scatter x1, waiting for transfers between devices, local(): lax.psum_scatter(reordered[5].astype(jnp.bfloat16), 'frame', scatter_dime...  81 us
    all_gather x1, waiting for transfers between devices, local(): lax.all_gather(down_weight, 'seq', axis=1, tiled=True)  80 us
  transfers between devices with their start and end apart: 22, of which 19 were waited for; matrix products, arithmetic and copies ran while one was open for 13% of the time, Pallas kernels for 0%

commit v1 on v0

v1 whole, which is shorter than its diff:
```python
import jax
import jax.numpy as jnp
from jax import lax
from jax.sharding import PartitionSpec as P

HEADS = 16
EPS = 1e-05
NEGATIVE = -1e30
HIGHEST = lax.Precision.HIGHEST
BF = jnp.bfloat16
F32 = jnp.float32
BOTH = ("seq", "frame")


def normalize(values):
    center = values - jnp.mean(values, -1, keepdims=True)
    scale_inv = lax.rsqrt(jnp.mean(center * center, -1, keepdims=True) + EPS)
    return (center * scale_inv, scale_inv)


def norm_back(grad_hat, normed, scale_inv):
    return scale_inv * (
        grad_hat
        - jnp.mean(grad_hat, -1, keepdims=True)
        - normed * jnp.mean(grad_hat * normed, -1, keepdims=True)
    )


def mm(a, b):
    return jnp.dot(a, b, preferred_element_type=F32)


def mm_tn(a, b):
    return lax.dot_general(a, b, (((0,), (0,)), ((), ())), preferred_element_type=F32)


def mm_nt(a, b):
    return lax.dot_general(a, b, (((1,), (1,)), ((), ())), preferred_element_type=F32)


def ein(spec, a, b):
    return jnp.einsum(spec, a, b, preferred_element_type=F32)


def exact_gelu(values):
    return jax.nn.gelu(values, approximate=False)


class Grid:
    def __init__(self, seq_count, frame_count):
        self.seq, self.frame = seq_count, frame_count
        self.core = 2
        self.side = frame_count // 2
        self.depth = seq_count // self.side
        self.count = seq_count * frame_count

    def split(self, lin):
        seq, frame = lin // self.frame, lin % self.frame
        return seq // self.side, seq % self.side, frame // 2, frame % 2

    def join(self, z, x, y, c):
        return ((z * self.side + x) * self.side + y) * 2 + c

    def send(self, value, move):
        perm = [(i, self.join(*move(*self.split(i)))) for i in range(self.count)]
        return lax.ppermute(value, BOTH, perm)

    def to_core(self, v):
        return self.send(v, lambda z, x, y, c: (z, x, y, 1 - c))

    def to_z(self, v, k):
        return self.send(v, lambda z, x, y, c: (z ^ k, x, y, c))

    def to_a(self, v, k):
        return self.send(v, lambda z, x, y, c: (z, x, y ^ k, c) if c else (z, x ^ k, y, c))

    def to_b(self, v, k):
        return self.send(v, lambda z, x, y, c: (z, x ^ k, y, c) if c else (z, x, y ^ k, c))

    def to_frame(self, v, k):
        def move(z, x, y, c):
            f = (y * 2 + c) ^ k
            return z, x, f // 2, f % 2

        return self.send(v, move)

    def to_seq(self, v, k):
        def move(z, x, y, c):
            s = (z * self.side + x) ^ k
            return s // self.side, s % self.side, y, c

        return self.send(v, move)

    def own(self):
        return lax.axis_index("seq") * self.frame + lax.axis_index("frame")

    def rel_of_abs(self):
        z, x, y, c = self.split(self.own())
        oz, ox, oy, oc = self.split(jnp.arange(self.count, dtype=jnp.int32))
        rz, rx, ry, rc = oz ^ z, ox ^ x, oy ^ y, oc ^ c
        b = jnp.where(oc == 0, ry, rx)
        a = jnp.where(oc == 0, rx, ry)
        return ((rc * self.side + b) * self.side + a) * self.depth + rz

    def abs_of_rel(self):
        z, x, y, c = self.split(self.own())
        r = jnp.arange(self.count, dtype=jnp.int32)
        rz = r % self.depth
        a = r // self.depth % self.side
        b = r // (self.depth * self.side) % self.side
        oc = (r // (self.depth * self.side * self.side)) ^ c
        rx = jnp.where(oc == 0, a, b)
        ry = jnp.where(oc == 0, b, a)
        return self.join(rz ^ z, rx ^ x, ry ^ y, oc)

    def gather(self, w):
        v = jnp.stack([w] + [self.to_z(w, k) for k in range(1, self.depth)])
        v = jnp.stack([v] + [self.to_a(v, k) for k in range(1, self.side)])
        v = jnp.stack([v] + [self.to_b(v, k) for k in range(1, self.side)])
        v = jnp.stack([v, self.to_core(v)])
        return v.reshape((self.count,) + w.shape)

    def scatter(self, v):
        v = v.reshape((2, self.side, self.side, self.depth) + v.shape[1:])
        t = v[0].astype(F32) + self.to_core(v[1].astype(BF)).astype(F32)
        s = t[0]
        for k in range(1, self.side):
            s = s + self.to_b(t[k].astype(BF), k).astype(F32)
        t = s
        s = t[0]
        for k in range(1, self.side):
            s = s + self.to_a(t[k].astype(BF), k).astype(F32)
        t = s
        s = t[0]
        for k in range(1, self.depth):
            s = s + self.to_z(t[k].astype(BF), k).astype(F32)
        return s


def local(
    grid,
    media,
    image_counts,
    time_ids,
    latents,
    time_table,
    media_gain,
    latent_gain,
    feed_gain,
    query_weight,
    keyval_weight,
    output_weight,
    up_weight,
    down_weight,
    cotangent,
):
    width = output_weight.shape[1]
    head_dim = width // HEADS
    factor = head_dim ** (-0.5)
    lat_rows = latents.shape[0]
    times = time_table.shape[0]
    seq_here, patches = media.shape[0], media.shape[2]
    own_rows = lat_rows // grid.frame
    rows = seq_here * own_rows
    part = width // grid.count
    slot = lax.axis_index("frame")
    seq_pos = lax.axis_index("seq")
    first_row = slot * own_rows
    rel_of_abs = grid.rel_of_abs()
    abs_of_rel = grid.abs_of_rel()

    def gather_sorted(w):
        return jnp.take(grid.gather(w), rel_of_abs, axis=0)

    def scatter_sorted(v):
        return grid.scatter(jnp.take(v, abs_of_rel, axis=0))

    pad = (-(lat_rows + times + 3)) % 8
    packed = jnp.concatenate(
        [latents, time_table, media_gain[None], latent_gain[None], feed_gain[None], jnp.zeros((pad, part), BF)]
    )
    small = gather_sorted(packed.T).reshape(width, -1).T.astype(F32)
    lat_float = small[:lat_rows]
    table_all = small[lat_rows : lat_rows + times]
    media_scale, latent_scale, feed_scale = (small[lat_rows + times + i] for i in range(3))

    keyval_all = gather_sorted(keyval_weight.T).reshape(2, HEADS, head_dim, width)
    key_w, value_w = keyval_all[0], keyval_all[1]
    output_all = gather_sorted(output_weight).reshape(HEADS, head_dim, width)

    hid_f = up_weight.shape[1]
    hid = hid_f // grid.seq
    d_part = up_weight.shape[0]
    up_blocks = up_weight.reshape(d_part, grid.seq, hid).transpose(1, 2, 0)
    down_blocks = down_weight.reshape(grid.seq, hid, d_part)
    both_blocks = jnp.stack([up_blocks, down_blocks], 1)
    seq_ids = jnp.arange(grid.seq, dtype=jnp.int32) ^ seq_pos
    rel_blocks = jnp.take(both_blocks, seq_ids, axis=0)
    got = jnp.stack([rel_blocks[0]] + [grid.to_seq(rel_blocks[k], k) for k in range(1, grid.seq)])
    got = jnp.take(got, seq_ids, axis=0)
    got = got.transpose(1, 2, 0, 3).reshape(2, hid, width)
    up_t, down_w = got[0], got[1]

    is_valid = slot < image_counts
    onehot = (time_ids[:, 0][:, None] == jnp.arange(times, dtype=jnp.int32)[None, :]).astype(F32)
    embedding = jnp.dot(onehot, table_all, precision=HIGHEST)
    embedded = media[:, 0].astype(F32) + embedding[:, None, :]
    normed_media, inv_media = normalize(embedded)
    hidden_media = (normed_media * media_scale).astype(BF)

    normed_lat, inv_lat = normalize(lat_float)
    hidden_lat = (normed_lat * latent_scale).astype(BF)
    hidden_own = lax.dynamic_slice_in_dim(hidden_lat, first_row, own_rows, 0)
    query_own = mm_tn(query_weight, hidden_lat.T).astype(BF)
    query_t = gather_sorted(query_own).reshape(HEADS, head_dim, lat_rows)
    folded = (ein("hel,hed->hld", query_t, key_w) * factor).astype(BF).reshape(HEADS * lat_rows, width)

    media_scores = ein("rd,spd->srp", folded, hidden_media)
    media_scores = jnp.where(is_valid[:, None, None], media_scores, NEGATIVE)
    own_scores = mm_nt(folded, hidden_own)
    top = jnp.maximum(jnp.max(media_scores, -1), jnp.max(own_scores, -1))
    media_exp = jnp.exp(media_scores - top[..., None])
    own_exp = jnp.exp(own_scores - top[..., None])
    total = jnp.sum(media_exp, -1) + jnp.sum(own_exp, -1)
    mix = ein("srp,spd->srd", media_exp.astype(BF), hidden_media) + ein("srk,kd->srd", own_exp.astype(BF), hidden_own)
    mix = (mix / total[..., None]).astype(BF).reshape(seq_here, HEADS, lat_rows, width)
    part_context = ein("shld,hed->shle", mix, value_w).astype(BF)
    pieces = part_context.reshape(seq_here, HEADS, grid.frame, own_rows, head_dim).transpose(2, 0, 1, 3, 4)
    frame_ids = jnp.arange(grid.frame, dtype=jnp.int32) ^ slot
    pieces = jnp.take(pieces, frame_ids, axis=0)
    stats = jnp.stack([top, total]).reshape(2, seq_here, HEADS, lat_rows)
    pieces = [pieces[0]] + [grid.to_frame(pieces[k], k) for k in range(1, grid.frame)]
    all_stats = jnp.stack([stats] + [grid.to_frame(stats, k) for k in range(1, grid.frame)])
    top_all = jnp.max(all_stats[:, 0], 0)
    weights = all_stats[:, 1] * jnp.exp(all_stats[:, 0] - top_all)
    total_all = jnp.sum(weights, 0)
    log_total = top_all + jnp.log(total_all)
    own_weights = lax.dynamic_slice_in_dim(weights / total_all, first_row, own_rows, 3)
    context = sum(p.astype(F32) * own_weights[i][..., None] for i, p in enumerate(pieces))
    context_low = context.astype(BF)

    lat_own = lax.dynamic_slice_in_dim(lat_float, first_row, own_rows, 0)
    mixed = lat_own[None] + ein("shle,hed->sld", context_low, output_all)
    mixed = mixed.reshape(rows, width)
    normed_feed, inv_feed = normalize(mixed)
    hidden_feed = (normed_feed * feed_scale).astype(BF)
    grad_out = cotangent.reshape(rows, width)

    feed_rows = grid.gather(hidden_feed).reshape(-1, width)
    grad_rows = grid.gather(grad_out.astype(BF)).reshape(-1, width)
    up_pre = mm_nt(feed_rows, up_t)
    hidden_act = exact_gelu(up_pre).astype(BF)
    grad_act = mm_nt(grad_rows, down_w)
    _, pullback = jax.vjp(exact_gelu, up_pre)
    grad_up = pullback(grad_act)[0].astype(BF)
    grad_feed = grid.scatter(mm(grad_up, up_t).astype(BF).reshape(grid.count, rows, width))
    down_out = grid.scatter(mm(hidden_act, down_w).astype(BF).reshape(grid.count, rows, width))
    up_part = mm_tn(grad_up, feed_rows).astype(BF)
    down_part = mm_tn(hidden_act, grad_rows).astype(BF)
    new_latents = (mixed + down_out).reshape(seq_here, own_rows, width)
    back_blocks = jnp.stack([up_part, down_part]).reshape(2, hid, grid.seq, d_part).transpose(2, 0, 1, 3)
    back_blocks = jnp.take(back_blocks, seq_ids, axis=0)
    back = jnp.stack([back_blocks[0]] + [grid.to_seq(back_blocks[k], k) for k in range(1, grid.seq)])
    back = jnp.take(back, seq_ids, axis=0).astype(F32)
    up_grad = back[:, 0].reshape(hid_f, d_part).T
    down_grad = back[:, 1].reshape(hid_f, d_part)

    feed_gain_part = jnp.sum(grad_feed * normed_feed, 0)
    grad_mixed = grad_out + norm_back(grad_feed * feed_scale, normed_feed, inv_feed)
    grad_mixed_low = grad_mixed.astype(BF)
    mixed_3 = grad_mixed_low.reshape(seq_here, own_rows, width)
    output_part = ein("shle,sld->hed", context_low, mixed_3).astype(BF)
    output_grad = scatter_sorted(output_part.reshape(grid.count, part, width))
    grad_context = ein("sld,hed->shle", mixed_3, output_all).astype(BF)
    row_own = jnp.sum(grad_context.astype(F32) * context, -1)
    got_grad = jnp.stack([grad_context] + [grid.to_frame(grad_context, k) for k in range(1, grid.frame)])
    got_row = jnp.stack([row_own] + [grid.to_frame(row_own, k) for k in range(1, grid.frame)])
    got_grad = jnp.take(got_grad, frame_ids, axis=0)
    got_row = jnp.take(got_row, frame_ids, axis=0)
    grad_all = got_grad.transpose(1, 2, 0, 3, 4).reshape(seq_here, HEADS, lat_rows, head_dim)
    row_term = got_row.transpose(1, 2, 0, 3).reshape(seq_here, HEADS * lat_rows, 1)

    log_rows = log_total.reshape(seq_here, HEADS * lat_rows, 1)
    grad_folded = ein("shle,hed->shld", grad_all, value_w).astype(BF).reshape(seq_here, HEADS * lat_rows, width)
    media_probs = jnp.exp(media_scores - log_rows)
    own_probs = jnp.exp(own_scores - log_rows)
    media_low, own_low = media_probs.astype(BF), own_probs.astype(BF)
    media_ds = (media_probs * (ein("srd,spd->srp", grad_folded, hidden_media) - row_term)).astype(BF)
    own_ds = (own_probs * (ein("srd,kd->srk", grad_folded, hidden_own) - row_term)).astype(BF)
    key_mix = ein("srp,spd->rd", media_ds, hidden_media) + ein("srk,kd->rd", own_ds, hidden_own)
    key_mix = key_mix.astype(BF).reshape(HEADS, lat_rows, width)
    value_mix = ein("srp,spd->srd", media_low, hidden_media) + ein("srk,kd->srd", own_low, hidden_own)
    value_mix = value_mix.astype(BF).reshape(seq_here, HEADS, lat_rows, width)
    value_part = ein("shle,shld->hed", grad_all, value_mix).astype(BF)
    key_part = (ein("hel,hld->hed", query_t, key_mix) * factor).astype(BF)
    query_part = (ein("hld,hed->hel", key_mix, key_w) * factor).astype(BF)
    keyval_part = jnp.concatenate([key_part, value_part]).reshape(grid.count, 2 * part, width)
    keyval_grad = scatter_sorted(keyval_part).T
    query_sum = scatter_sorted(query_part.reshape(grid.count, part, lat_rows)).T.astype(BF)

    grad_hidden = ein("srp,rd->spd", media_ds, folded) + ein("srp,srd->spd", media_low, grad_folded)
    grad_hidden_own = ein("srk,rd->kd", own_ds, folded) + ein("srk,srd->kd", own_low, grad_folded)
    media_gain_part = jnp.sum(grad_hidden * normed_media, (0, 1))
    grad_embedded = norm_back(grad_hidden * media_scale, normed_media, inv_media)
    table_part = jnp.dot(onehot.T, jnp.sum(grad_embedded, 1), precision=HIGHEST)

    query_grad = mm_tn(hidden_lat, query_sum)
    grad_lat = mm_nt(query_sum, query_weight)
    grad_lat = grad_lat + lax.dynamic_update_slice_in_dim(jnp.zeros_like(grad_lat), grad_hidden_own, first_row, 0)
    latent_gain_part = jnp.sum(grad_lat * normed_lat, 0)
    residual = jnp.sum(grad_mixed.reshape(seq_here, own_rows, width), 0)
    latents_part = norm_back(grad_lat * latent_scale, normed_lat, inv_lat)
    latents_part = latents_part + lax.dynamic_update_slice_in_dim(
        jnp.zeros_like(latents_part), residual, first_row, 0
    )
    smalls = jnp.concatenate(
        [
            latents_part,
            table_part,
            media_gain_part[None],
            latent_gain_part[None],
            feed_gain_part[None],
            jnp.zeros((pad, width), F32),
        ]
    ).astype(BF)
    small_sum = scatter_sorted(smalls.T.reshape(grid.count, part, -1)).T
    latents_grad = small_sum[:lat_rows]
    table_grad = small_sum[lat_rows : lat_rows + times]
    media_gain_grad, latent_gain_grad, feed_gain_grad = (small_sum[lat_rows + times + i] for i in range(3))
    return (
        new_latents,
        grad_embedded[:, None],
        latents_grad,
        table_grad,
        media_gain_grad,
        latent_gain_grad,
        feed_gain_grad,
        query_grad,
        keyval_grad,
        output_grad,
        up_grad,
        down_grad,
    )


def solution(mesh):
    grid = Grid(mesh.shape["seq"], mesh.shape["frame"])

    def run(*args):
        return local(grid, *args)

    return jax.shard_map(
        run,
        mesh=mesh,
        in_specs=(
            P("seq", "frame", None, None),
            P("seq"),
            P("seq", "frame"),
            P(None, BOTH),
            P(None, BOTH),
            P(BOTH),
            P(BOTH),
            P(BOTH),
            P(None, BOTH),
            P(None, BOTH),
            P(BOTH, None),
            P("seq", "frame"),
            P("frame", "seq"),
            P("seq", "frame", None),
        ),
        out_specs=(
            P("seq", "frame", None),
            P("seq", "frame", None, None),
            P(None, BOTH),
            P(None, BOTH),
            P(BOTH),
            P(BOTH),
            P(BOTH),
            P(None, BOTH),
            P(None, BOTH),
            P(BOTH, None),
            P("seq", "frame"),
            P("frame", "seq"),
        ),
        check_vma=False,
    )
```

time: 1860 us -> 758 us (0.41)
  waiting for transfers between devices: 1350 us -> 234 us
  blocking collectives: 180 us -> 0 us
  starting transfers between devices: 1.66 us -> 130 us
  other arithmetic: 36.1 us -> 125 us
  matrix products: 158 us -> 129 us
    reduce_scatter x8 -> x0, waiting for transfers between devices: 644 us -> none  [the longest x1 142 us: local(): lax.psum_scatter(down_part.astype(jnp.bfloat16), 'frame', scatter_dimensi...]
    all_gather x7 -> x0, waiting for transfers between devices: 407 us -> none  [the longest x1 118 us: local(): lax.all_gather(up_seq, 'frame', axis=1, tiled=True)]
    unnamed x29 -> x0, waiting for transfers between devices: 300 us -> none
    ppermute x0 -> x98, waiting for transfers between devices: none -> 234 us  [send(): return lax.ppermute(value, BOTH, perm)]
    ppermute x0 -> x98, starting transfers between devices: none -> 130 us  [send(): return lax.ppermute(value, BOTH, perm)]
    all_gather x5 -> x0, blocking collectives: 101 us -> none  [the longest x1 43.6 us: local(): lax.all_gather(time_table, ('seq', 'frame'), axis=1, tiled=True)]
    unnamed x3 -> x0, blocking collectives: 67.7 us -> none
    another operation x0 -> x36, other arithmetic: none -> 52.5 us  [the longest x12 36.4 us: gather(): v = jnp.stack([v, self.to_core(v)])]
  transfers between devices with their start and end apart: 22 -> 98, of which waited for: 19 -> 40; matrix products, arithmetic and copies ran while one was open for 13% -> 48% of each run, Pallas kernels for 0% -> 0%
where the time goes in v1:
time: 758 us; the launch traced here: 748 us
  waiting for transfers between devices  234 us (31%)
  starting transfers between devices  130 us (17%)
  matrix products  129 us (17%)
  local copies, waits for them, and re-layouts  127 us (17%)
  other arithmetic  125 us (16%)
    ppermute x98, waiting for transfers between devices, send(): return lax.ppermute(value, BOTH, perm)  234 us
    ppermute x98, starting transfers between devices, send(): return lax.ppermute(value, BOTH, perm)  130 us
    dot_general x22, matrix products, ein(): return jnp.einsum(spec, a, b, preferred_element_type=F32)  113 us
    another operation x12, other arithmetic, gather(): v = jnp.stack([v, self.to_core(v)])  36.4 us
    unnamed x199, local copies, waits for them, and re-layouts  19.7 us
    gather x4, local copies, waits for them, and re-layouts, scatter_sorted(): return grid.scatter(jnp.take(v, abs_of_rel, axis=0))  18 us
    gather x4, local copies, waits for them, and re-layouts, gather_sorted(): return jnp.take(grid.gather(w), rel_of_abs, axis=0)  17.4 us
  transfers between devices with their start and end apart: 98, of which 40 were waited for; matrix products, arithmetic and copies ran while one was open for 48% of the time, Pallas kernels for 0%

profile of v1, /device:TPU:0, one launch (start us, length us, event | category | flops | bytes accessed | tf_op | source)
XLA Modules:
  0.0 747.6 jit_solution(16487508046175247322)
XLA Ops:
  21.8 12.0 %collective-permute-start = (bf16[48,72]{1,0:T(8,128)(2,1)S(1)}, bf16[48,72]{1,0:T(8,128)(2,1)S(1)}, u32[]{:S(2)}, u32[]{:S(2)}) collective-permute-start(bf16[48,72]{1,0:T(8,128)(2,1)S(1)} %bitcast.743), channel_id=1, source_target_pairs={{0,8},{1,9},{2,10},{3,11},{4,12},{5,13},{6,14},{7,15},{8,0},{9,1},... | collective-permute-start | bytes 20744 | tf_op jit(solution)/shard_map/ppermute | solution.py:66
  49.9 10.2 %collective-permute-done.3 = bf16[4,48,72]{2,1,0:T(8,128)(2,1)S(1)} collective-permute-done((bf16[4,48,72]{2,1,0:T(8,128)(2,1)S(1)}, bf16[4,48,72]{2,1,0:T(8,128)(2,1)S(1)}, u32[]{:S(2)}, u32[]{:S(2)}) %collective-permute-start.3) | collective-permute-done | bytes 27680 | tf_op jit(solution)/shard_map/ppermute | solution.py:66
  97.3 21.0 %collective-permute-done.10 = bf16[2,4,96,1536]{3,2,1,0:T(8,128)(2,1)} collective-permute-done((bf16[2,4,96,1536]{3,2,1,0:T(8,128)(2,1)}, bf16[2,4,96,1536]{3,2,1,0:T(8,128)(2,1)}, u32[]{:S(2)}, u32[]{:S(2)}) %collective-permute-start.10) | collective-permute-done | bytes 2359328 | tf_op jit(solution)/shard_map/ppermute | solution.py:66
  146.0 13.8 %collective-permute-done.16 = bf16[2,4,48,64]{3,2,1,0:T(8,128)(2,1)S(1)} collective-permute-done((bf16[2,4,48,64]{3,2,1,0:T(8,128)(2,1)S(1)}, bf16[2,4,48,64]{3,2,1,0:T(8,128)(2,1)S(1)}, u32[]{:S(2)}, u32[]{:S(2)}) %collective-permute-start.16) | collective-permute-done | bytes 49184 | tf_op jit(solution)/shard_map/ppermute | solution.py:66
  182.2 8.3 %pad_maximum_fusion = bf16[2,2,2,4,96,1536]{5,4,3,2,1,0:T(8,128)(2,1)} fusion(bf16[1,2,2,4,96,1536]{5,4,3,2,1,0:T(8,128)(2,1)} %bitcast.27, bf16[1,2,2,4,96,1536]{5,4,3,2,1,0:T(8,128)(2,1)} %get-tuple-element.123), kind=kLoop, calls=%fused_computation.17 | loop fusion | flops 4718592 | bytes 18874368 | tf_op jit(solution)/shard_map/stack | solution.py:120
  190.5 9.8 %gather_fusion.2 = bf16[32,96,1536]{2,1,0:T(8,128)(2,1)} fusion(bf16[32,96,1536]{2,1,0:T(8,128)(2,1)} %bitcast.658, s32[1024]{0:T(1024)} %copy-done.61), kind=kCustom, calls=%fused_computation.1.clone | custom fusion | bytes 18874496 | tf_op jit(solution)/shard_map/jit(_take)/gather | solution.py:173
  200.3 8.3 %broadcast_select_fusion.1 = bf16[32,96,1536]{2,1,0:T(8,128)(2,1)} fusion(bf16[32,96,1536]{2,1,0:T(8,128)(2,1)} %gather_fusion.2, pred[32]{0:T(512)(128)(4,1)S(1)} %copy-done.56), kind=kLoop, calls=%fused_computation.27 | loop fusion | flops 4718592 | bytes 18874400 | tf_op jit(solution)/shard_map/jit(_take)/select_n | solution.py:173
  216.5 10.2 %fusion.46 = f32[3,1024,1536]{2,1,0:T(8,128)} fusion(f32[3,256,1024]{2,1,0:T(8,128)S(1)} %get-tuple-element.217, f32[3,1024]{1,0:T(4,128)S(1)} %broadcast_maximum_fusion.2, pred[3]{0:T(512)(128)(4,1)S(1)} %copy-done.49, bf16[3,1,256,1536]{3,2,1,0:T(8,128)(2,1)S(1)} %copy-done.1, f32[1536]{0:T(1024)} %copy-done.29, f32[3,256]{1,0:T(4,128)} %copy-done.35, ...), kind=kOutput, calls=%fused_computation.112 | convolution fusion | flops 2425356288 | bytes 24422404 | tf_op jit(solution)/shard_map/srp,spd->srd/dot_general | solution.py:42
  229.6 10.6 %divide_convert_fusion = bf16[3,1024,1536]{2,1,0:T(8,128)(2,1)} fusion(f32[3,1024,1536]{2,1,0:T(8,128)} %fusion.46, f32[3,1024]{1,0:T(4,128)S(1)} %add.395, f32[3,1024]{1,0:T(4,128)S(1)} %broadcast_maximum_fusion.2, f32[1024,16]{0,1:T(8,128)S(1)} %get-tuple-element.219, bf16[64,1536]{1,0:T(8,128)(2,1)S(1)} %get-tuple-element.182, s32[]{:T(128)S(6)} %select_n.201), kind=kOutput, calls=%fused_computation.16 | convolution fusion | flops 165249024 | bytes 28459012 | tf_op jit(solution)/shard_map/srk,kd->srd/dot_general | solution.py:42
  279.8 8.8 %collective-permute-done.31 = bf16[48,1536]{1,0:T(8,128)(2,1)S(1)} collective-permute-done((bf16[48,1536]{1,0:T(8,128)(2,1)S(1)}, bf16[48,1536]{1,0:T(8,128)(2,1)S(1)}, u32[]{:S(2)}, u32[]{:S(2)}) %collective-permute-start.31) | collective-permute-done | bytes 147488 | tf_op jit(solution)/shard_map/ppermute | solution.py:66
  403.2 12.0 %collective-permute-done.95 = bf16[2,192,192]{2,1,0:T(8,128)(2,1)S(1)} collective-permute-done((bf16[2,192,192]{2,1,0:T(8,128)(2,1)S(1)}, bf16[2,192,192]{2,1,0:T(8,128)(2,1)S(1)}, u32[]{:S(2)}, u32[]{:S(2)}) %collective-permute-start.95) | collective-permute-done | bytes 147488 | tf_op jit(solution)/shard_map/ppermute | solution.py:66
  422.1 12.5 %collective-permute-done.56 = bf16[2,4,48,1536]{3,2,1,0:T(8,128)(2,1)S(1)} collective-permute-done((bf16[2,4,48,1536]{3,2,1,0:T(8,128)(2,1)S(1)}, bf16[2,4,48,1536]{3,2,1,0:T(8,128)(2,1)S(1)}, u32[]{:S(2)}, u32[]{:S(2)}) %collective-permute-start.56) | collective-permute-done | bytes 1179680 | tf_op jit(solution)/shard_map/ppermute | solution.py:66
  436.5 17.1 %collective-permute-done.44 = bf16[2,4,48,1536]{3,2,1,0:T(8,128)(2,1)S(1)} collective-permute-done((bf16[2,4,48,1536]{3,2,1,0:T(8,128)(2,1)S(1)}, bf16[2,4,48,1536]{3,2,1,0:T(8,128)(2,1)S(1)}, u32[]{:S(2)}, u32[]{:S(2)}) %collective-permute-start.44) | collective-permute-done | bytes 1179680 | tf_op jit(solution)/shard_map/ppermute | solution.py:66
  466.6 8.7 %collective-permute-done.59 = bf16[48,1536]{1,0:T(8,128)(2,1)S(1)} collective-permute-done((bf16[48,1536]{1,0:T(8,128)(2,1)S(1)}, bf16[48,1536]{1,0:T(8,128)(2,1)S(1)}, u32[]{:S(2)}, u32[]{:S(2)}) %collective-permute-start.59) | collective-permute-done | bytes 147488 | tf_op jit(solution)/shard_map/ppermute | solution.py:66
  513.6 8.7 %convert_bitcast_fusion = bf16[3,16,64,1536]{3,2,0,1:T(8,128)(2,1)} fusion(bf16[32,96,1536]{2,1,0:T(8,128)(2,1)} %broadcast_select_fusion.1, bf16[3,16,64,96]{3,2,1,0:T(8,128)(2,1)S(1)} %bitcast.669), kind=kOutput, calls=%fused_computation.25 | convolution fusion | flops 910688256 | bytes 14745600 | tf_op jit(solution)/shard_map/shle,hed->shld/dot_general | solution.py:42
  522.2 8.3 %copy.206 = bf16[3,16,64,1536]{3,2,1,0:T(8,128)(2,1)} copy(bf16[3,16,64,1536]{3,2,0,1:T(8,128)(2,1)} %convert_bitcast_fusion) | data formatting | bytes 18874368 | tf_op jit(solution)/shard_map/convert_element_type | solution.py:284
  530.5 9.6 %fusion.175 = f32[3,256,1536]{2,1,0:T(8,128)} fusion(bf16[3,1024,1536]{2,1,0:T(8,128)(2,1)} %bitcast.643, f32[3,256,1024]{2,1,0:T(8,128)} %copy-done.3, f32[3,1024]{1,0:T(4,128)S(1)} %add.412, pred[3]{0:T(512)(128)(4,1)S(1)} %copy-done.50), kind=kOutput, calls=%fused_computation.454 | convolution fusion | flops 2418278400 | bytes 17313796 | tf_op jit(solution)/shard_map/srp,srd->spd/dot_general | solution.py:42
  540.2 8.5 %multiply_convert_fusion.2 = bf16[3,1024,256]{1,2,0:T(8,128)(2,1)} fusion(f32[3,256,1024]{2,1,0:T(8,128)} %copy-done.3, bf16[3,1024,1536]{2,1,0:T(8,128)(2,1)} %bitcast.644, f32[3,1024]{1,0:T(4,128)S(1)} %sub.219, f32[3,1024]{1,0:T(4,128)S(1)} %add.412, pred[3]{0:T(512)(128)(4,1)S(1)} %copy-done.50, bf16[3,1,256,1536]{3,2,1,0:T(8,128)(2,1)S(1)} %copy-done.2, ...), kind=kOutput, calls=%fused_computation.76 | convolution fusion | flops 2426929152 | bytes 16570371 | tf_op jit(solution)/shard_map/srd,spd->srp/dot_general | solution.py:42
  587.9 9.4 %gather_fusion.11 = bf16[32,96,1536]{2,1,0:T(8,128)(2,1)} fusion(bf16[32,96,1536]{2,1,0:T(8,128)(2,1)} %pad_maximum_fusion.1, s32[1024]{0:T(1024)} %pad_clamp_fusion), kind=kCustom, calls=%fused_computation.7.clone | custom fusion | bytes 18874496 | tf_op jit(solution)/shard_map/jit(_take)/gather | solution.py:176
  597.3 8.3 %broadcast_select_fusion = bf16[32,96,1536]{2,1,0:T(8,128)(2,1)} fusion(bf16[32,96,1536]{2,1,0:T(8,128)(2,1)} %gather_fusion.11, pred[32]{0:T(512)(128)(4,1)S(1)} %copy-done.53), kind=kLoop, calls=%fused_computation.26 | loop fusion | flops 4718592 | bytes 18874400 | tf_op jit(solution)/shard_map/jit(_take)/select_n | solution.py:176
  605.6 8.5 %fusion.205 = (bf16[16,96,1536]{2,1,0:T(8,128)(2,1)}, bf16[16,96,1536]{2,1,0:T(8,128)(2,1)}) fusion(bf16[32,96,1536]{2,1,0:T(8,128)(2,1)} %broadcast_select_fusion), kind=kLoop, calls=%fused_computation.470 | loop fusion | bytes 18874368 | tf_op jit(solution)/shard_map/slice | solution.py:125
  676.9 23.3 %collective-permute-done.80 = bf16[2,4,96,1536]{3,2,1,0:T(8,128)(2,1)} collective-permute-done((bf16[2,4,96,1536]{3,2,1,0:T(8,128)(2,1)}, bf16[2,4,96,1536]{3,2,1,0:T(8,128)(2,1)}, u32[]{:S(2)}, u32[]{:S(2)}) %collective-permute-start.80) | collective-permute-done | bytes 2359328 | tf_op jit(solution)/shard_map/ppermute | solution.py:66
  709.5 11.0 %collective-permute-done.81 = bf16[4,96,1536]{2,1,0:T(8,128)(2,1)S(1)} collective-permute-done((bf16[4,96,1536]{2,1,0:T(8,128)(2,1)S(1)}, bf16[4,96,1536]{2,1,0:T(8,128)(2,1)S(1)}, u32[]{:S(2)}, u32[]{:S(2)}) %collective-permute-start.81) | collective-permute-done | bytes 1179680 | tf_op jit(solution)/shard_map/ppermute | solution.py:66
  732.8 13.5 %collective-permute-done.83 = bf16[96,1536]{1,0:T(8,128)(2,1)S(1)} collective-permute-done((bf16[96,1536]{1,0:T(8,128)(2,1)S(1)}, bf16[96,1536]{1,0:T(8,128)(2,1)S(1)}, u32[]{:S(2)}, u32[]{:S(2)}) %collective-permute-start.83) | collective-permute-done | bytes 294944 | tf_op jit(solution)/shard_map/ppermute | solution.py:66
  (628 shorter events, 472.0 us)
Async XLA Ops:
  4.6 41.9 %collective-permute-start.2 = (bf16[48,72]{1,0:T(8,128)(2,1)S(1)}, bf16[48,72]{1,0:T(8,128)(2,1)S(1)}, u32[]{:S(2)}, u32[]{:S(2)}) collective-permute-start(bf16[48,72]{1,0:T(8,128)(2,1)S(1)} %bitcast.741), channel_id=1, source_target_pairs={{0,24},{1,25},{2,26},{3,27},{4,28},{5,29},{6,30},{7,31},{8,16},{9,... | collective-permute-start | bytes 20744 | tf_op jit(solution)/shard_map/ppermute | solution.py:66
  9.7 36.8 %collective-permute-start.1 = (bf16[48,72]{1,0:T(8,128)(2,1)S(1)}, bf16[48,72]{1,0:T(8,128)(2,1)S(1)}, u32[]{:S(2)}, u32[]{:S(2)}) collective-permute-start(bf16[48,72]{1,0:T(8,128)(2,1)S(1)} %bitcast.742), channel_id=1, source_target_pairs={{0,16},{1,17},{2,18},{3,19},{4,20},{5,21},{6,22},{7,23},{8,24},{9,... | collective-permute-start | bytes 20744 | tf_op jit(solution)/shard_map/ppermute | solution.py:66
  11.6 27.1 %collective-permute-start.7 = (bf16[96,1536]{1,0:T(8,128)(2,1)}, bf16[96,1536]{1,0:T(8,128)(2,1)}, u32[]{:S(2)}, u32[]{:S(2)}) collective-permute-start(bf16[96,1536]{1,0:T(8,128)(2,1)} %bitcast.711), channel_id=1, source_target_pairs={{0,16},{1,17},{2,18},{3,19},{4,20},{5,21},{6,22},{7,23},{8,24},{9,... | collective-permute-start | bytes 884744 | tf_op jit(solution)/shard_map/ppermute | solution.py:66
  12.6 28.4 %collective-permute-start.6 = (bf16[96,1536]{1,0:T(8,128)(2,1)}, bf16[96,1536]{1,0:T(8,128)(2,1)}, u32[]{:S(2)}, u32[]{:S(2)}) collective-permute-start(bf16[96,1536]{1,0:T(8,128)(2,1)} %bitcast.712), channel_id=1, source_target_pairs={{0,8},{1,9},{2,10},{3,11},{4,12},{5,13},{6,14},{7,15},{8,0},{9,1},... | collective-permute-start | bytes 884744 | tf_op jit(solution)/shard_map/ppermute | solution.py:66
  21.8 26.8 %collective-permute-start = (bf16[48,72]{1,0:T(8,128)(2,1)S(1)}, bf16[48,72]{1,0:T(8,128)(2,1)S(1)}, u32[]{:S(2)}, u32[]{:S(2)}) collective-permute-start(bf16[48,72]{1,0:T(8,128)(2,1)S(1)} %bitcast.743), channel_id=1, source_target_pairs={{0,8},{1,9},{2,10},{3,11},{4,12},{5,13},{6,14},{7,15},{8,0},{9,1},... | collective-permute-start | bytes 20744 | tf_op jit(solution)/shard_map/ppermute | solution.py:66
  38.7 28.4 %collective-permute-start.26 = (bf16[48,1536]{1,0:T(8,128)(2,1)}, bf16[48,1536]{1,0:T(8,128)(2,1)S(1)}, u32[]{:S(2)}, u32[]{:S(2)}) collective-permute-start(bf16[48,1536]{1,0:T(8,128)(2,1)} %param.36), channel_id=1, source_target_pairs={{0,24},{1,25},{2,26},{3,27},{4,28},{5,29},{6,30},{7,31},{8,16},{9,... | collective-permute-start | bytes 442376 | tf_op jit(solution)/shard_map/ppermute | solution.py:66
  43.3 30.3 %collective-permute-start.9 = (bf16[4,96,1536]{2,1,0:T(8,128)(2,1)S(1)}, bf16[4,96,1536]{2,1,0:T(8,128)(2,1)S(1)}, u32[]{:S(2)}, u32[]{:S(2)}) collective-permute-start(bf16[4,96,1536]{2,1,0:T(8,128)(2,1)S(1)} %get-tuple-element.159), channel_id=1, source_target_pairs={{0,4},{1,3},{2,6},{3,1},{4,0},{5,7},{6,2},{7,5},{8,12},{9,11},{10,... | collective-permute-start | bytes 3538952 | tf_op jit(solution)/shard_map/ppermute | solution.py:66
  78.6 39.7 %collective-permute-start.10 = (bf16[2,4,96,1536]{3,2,1,0:T(8,128)(2,1)}, bf16[2,4,96,1536]{3,2,1,0:T(8,128)(2,1)}, u32[]{:S(2)}, u32[]{:S(2)}) collective-permute-start(bf16[2,4,96,1536]{3,2,1,0:T(8,128)(2,1)} %get-tuple-element.130), channel_id=1, source_target_pairs={{0,2},{1,5},{2,0},{3,7},{4,6},{5,1},{6,4},{7,3},{8,10},{9,13},{10,... | collective-permute-start | bytes 7077896 | tf_op jit(solution)/shard_map/ppermute | solution.py:66
  81.3 58.4 %collective-permute-start.52 = (bf16[4,48,1536]{2,1,0:T(8,128)(2,1)}, bf16[4,48,1536]{2,1,0:T(8,128)(2,1)}, u32[]{:S(2)}, u32[]{:S(2)}) collective-permute-start(bf16[4,48,1536]{2,1,0:T(8,128)(2,1)} %get-tuple-element.181), channel_id=1, source_target_pairs={{0,4},{1,3},{2,6},{3,1},{4,0},{5,7},{6,2},{7,5},{8,12},{9,11},{10,... | collective-permute-start | bytes 1769480 | tf_op jit(solution)/shard_map/ppermute | solution.py:66
  95.7 35.1 %collective-permute-start.28 = (bf16[2,4,48,1536]{3,2,1,0:T(8,128)(2,1)S(1)}, bf16[2,4,48,1536]{3,2,1,0:T(8,128)(2,1)S(1)}, u32[]{:S(2)}, u32[]{:S(2)}) collective-permute-start(bf16[2,4,48,1536]{3,2,1,0:T(8,128)(2,1)S(1)} %get-tuple-element.161), channel_id=1, source_target_pairs={{0,2},{1,5},{2,0},{3,7},{4,6},{5,1},{6,4},{7,3},{8,10},{9,13},{10,... | collective-permute-start | bytes 3538952 | tf_op jit(solution)/shard_map/ppermute | solution.py:66
  124.1 58.0 %collective-permute-start.11 = (bf16[2,2,4,96,1536]{4,3,2,1,0:T(8,128)(2,1)}, bf16[2,2,4,96,1536]{4,3,2,1,0:T(8,128)(2,1)}, u32[]{:S(2)}, u32[]{:S(2)}) collective-permute-start(bf16[2,2,4,96,1536]{4,3,2,1,0:T(8,128)(2,1)} %get-tuple-element.124), channel_id=1, source_target_pairs={{0,1},{1,0},{2,3},{3,2},{4,5},{5,4},{6,7},{7,6},{8,9},{9,8},{10,11... | collective-permute-start | bytes 14155784 | tf_op jit(solution)/shard_map/ppermute | solution.py:66
  133.3 34.1 %collective-permute-start.29 = (bf16[2,2,4,48,1536]{4,3,2,1,0:T(8,128)(2,1)}, bf16[2,2,4,48,1536]{4,3,2,1,0:T(8,128)(2,1)}, u32[]{:S(2)}, u32[]{:S(2)}) collective-permute-start(bf16[2,2,4,48,1536]{4,3,2,1,0:T(8,128)(2,1)} %get-tuple-element.132), channel_id=1, source_target_pairs={{0,1},{1,0},{2,3},{3,2},{4,5},{5,4},{6,7},{7,6},{8,9},{9,8},{10,11... | collective-permute-start | bytes 7077896 | tf_op jit(solution)/shard_map/ppermute | solution.py:66
  135.2 153.5 %collective-permute-start.37 = (bf16[2,192,192]{2,1,0:T(8,128)(2,1)}, bf16[2,192,192]{2,1,0:T(8,128)(2,1)}, u32[]{:S(2)}, u32[]{:S(2)}) collective-permute-start(bf16[2,192,192]{2,1,0:T(8,128)(2,1)} %get-tuple-element.150), channel_id=1, source_target_pairs={{0,8},{1,9},{2,10},{3,11},{4,12},{5,13},{6,14},{7,15},{8,0},{9,1},... | collective-permute-start | bytes 442376 | tf_op jit(solution)/shard_map/ppermute | solution.py:66
  161.3 129.7 %collective-permute-start.38 = (bf16[2,192,192]{2,1,0:T(8,128)(2,1)}, bf16[2,192,192]{2,1,0:T(8,128)(2,1)}, u32[]{:S(2)}, u32[]{:S(2)}) collective-permute-start(bf16[2,192,192]{2,1,0:T(8,128)(2,1)} %get-tuple-element.149), channel_id=1, source_target_pairs={{0,12},{1,13},{2,14},{3,15},{4,8},{5,9},{6,10},{7,11},{8,4},{9,5},... | collective-permute-start | bytes 442376 | tf_op jit(solution)/shard_map/ppermute | solution.py:66
  288.6 35.0 %collective-permute-start.54 = (bf16[2,2,4,48,1536]{4,3,2,1,0:T(8,128)(2,1)}, bf16[2,2,4,48,1536]{4,3,2,1,0:T(8,128)(2,1)}, u32[]{:S(2)}, u32[]{:S(2)}) collective-permute-start(bf16[2,2,4,48,1536]{4,3,2,1,0:T(8,128)(2,1)} %get-tuple-element.134), channel_id=1, source_target_pairs={{0,1},{1,0},{2,3},{3,2},{4,5},{5,4},{6,7},{7,6},{8,9},{9,8},{10,11... | collective-permute-start | bytes 7077896 | tf_op jit(solution)/shard_map/ppermute | solution.py:66
  354.6 61.3 %collective-permute-start.55 = (bf16[2,2,4,48,1536]{4,3,2,1,0:T(8,128)(2,1)}, bf16[2,2,4,48,1536]{4,3,2,1,0:T(8,128)(2,1)}, u32[]{:S(2)}, u32[]{:S(2)}) collective-permute-start(bf16[2,2,4,48,1536]{4,3,2,1,0:T(8,128)(2,1)} %bitcast.142), channel_id=1, source_target_pairs={{0,1},{1,0},{2,3},{3,2},{4,5},{5,4},{6,7},{7,6},{8,9},{9,8},{10,11... | collective-permute-start | bytes 7077896 | tf_op jit(solution)/shard_map/ppermute | solution.py:66
  376.9 42.2 %collective-permute-start.43 = (bf16[2,2,4,48,1536]{4,3,2,1,0:T(8,128)(2,1)S(1)}, bf16[2,2,4,48,1536]{4,3,2,1,0:T(8,128)(2,1)S(1)}, u32[]{:S(2)}, u32[]{:S(2)}) collective-permute-start(bf16[2,2,4,48,1536]{4,3,2,1,0:T(8,128)(2,1)S(1)} %bitcast.686), channel_id=1, source_target_pairs={{0,1},{1,0},{2,3},{3,2},{4,5},{5,4},{6,7},{7,6},{8,9},{9,8},{10,11... | collective-permute-start | bytes 7077896 | tf_op jit(solution)/shard_map/ppermute | solution.py:66
  397.0 24.4 %collective-permute-start.96 = (bf16[2,192,192]{2,1,0:T(8,128)(2,1)S(1)}, bf16[2,192,192]{2,1,0:T(8,128)(2,1)S(1)}, u32[]{:S(2)}, u32[]{:S(2)}) collective-permute-start(bf16[2,192,192]{2,1,0:T(8,128)(2,1)S(1)} %get-tuple-element.136), channel_id=1, source_target_pairs={{0,24},{1,25},{2,26},{3,27},{4,28},{5,29},{6,30},{7,31},{8,16},{9,... | collective-permute-start | bytes 442376 | tf_op jit(solution)/shard_map/ppermute | solution.py:66
  399.2 236.4 %collective-permute-start.97 = (bf16[2,192,192]{2,1,0:T(8,128)(2,1)}, bf16[2,192,192]{2,1,0:T(8,128)(2,1)}, u32[]{:S(2)}, u32[]{:S(2)}) collective-permute-start(bf16[2,192,192]{2,1,0:T(8,128)(2,1)} %get-tuple-element.135), channel_id=1, source_target_pairs={{0,28},{1,29},{2,30},{3,31},{4,24},{5,25},{6,26},{7,27},{8,20},{9,... | collective-permute-start | bytes 442376 | tf_op jit(solution)/shard_map/ppermute | solution.py:66
  420.0 33.6 %collective-permute-start.44 = (bf16[2,4,48,1536]{3,2,1,0:T(8,128)(2,1)S(1)}, bf16[2,4,48,1536]{3,2,1,0:T(8,128)(2,1)S(1)}, u32[]{:S(2)}, u32[]{:S(2)}) collective-permute-start(bf16[2,4,48,1536]{3,2,1,0:T(8,128)(2,1)S(1)} %fusion.58), channel_id=1, source_target_pairs={{0,2},{1,5},{2,0},{3,7},{4,6},{5,1},{6,4},{7,3},{8,10},{9,13},{10,... | collective-permute-start | bytes 3538952 | tf_op jit(solution)/shard_map/ppermute | solution.py:66
  506.4 141.8 %collective-permute-start.85 = (bf16[2,2,4,48,1536]{4,3,2,1,0:T(8,128)(2,1)}, bf16[2,2,4,48,1536]{4,3,2,1,0:T(8,128)(2,1)}, u32[]{:S(2)}, u32[]{:S(2)}) collective-permute-start(bf16[2,2,4,48,1536]{4,3,2,1,0:T(8,128)(2,1)} %bitcast.220), channel_id=1, source_target_pairs={{0,1},{1,0},{2,3},{3,2},{4,5},{5,4},{6,7},{7,6},{8,9},{9,8},{10,11... | collective-permute-start | bytes 7077896 | tf_op jit(solution)/shard_map/ppermute | solution.py:66
  578.1 36.1 %collective-permute-start.67 = (bf16[2,2,4,48,64]{4,3,2,1,0:T(8,128)(2,1)}, bf16[2,2,4,48,64]{4,3,2,1,0:T(8,128)(2,1)}, u32[]{:S(2)}, u32[]{:S(2)}) collective-permute-start(bf16[2,2,4,48,64]{4,3,2,1,0:T(8,128)(2,1)} %bitcast.175), channel_id=1, source_target_pairs={{0,1},{1,0},{2,3},{3,2},{4,5},{5,4},{6,7},{7,6},{8,9},{9,8},{10,11... | collective-permute-start | bytes 294920 | tf_op jit(solution)/shard_map/ppermute | solution.py:66
  659.1 41.2 %collective-permute-start.80 = (bf16[2,4,96,1536]{3,2,1,0:T(8,128)(2,1)}, bf16[2,4,96,1536]{3,2,1,0:T(8,128)(2,1)}, u32[]{:S(2)}, u32[]{:S(2)}) collective-permute-start(bf16[2,4,96,1536]{3,2,1,0:T(8,128)(2,1)} %fusion.32), channel_id=1, source_target_pairs={{0,2},{1,5},{2,0},{3,7},{4,6},{5,1},{6,4},{7,3},{8,10},{9,13},{10,... | collective-permute-start | bytes 7077896 | tf_op jit(solution)/shard_map/ppermute | solution.py:66
  676.8 27.9 %collective-permute-start.87 = (bf16[4,48,1536]{2,1,0:T(8,128)(2,1)S(1)}, bf16[4,48,1536]{2,1,0:T(8,128)(2,1)S(1)}, u32[]{:S(2)}, u32[]{:S(2)}) collective-permute-start(bf16[4,48,1536]{2,1,0:T(8,128)(2,1)S(1)} %fusion.77), channel_id=1, source_target_pairs={{0,4},{1,3},{2,6},{3,1},{4,0},{5,7},{6,2},{7,5},{8,12},{9,11},{10,... | collective-permute-start | bytes 1769480 | tf_op jit(solution)/shard_map/ppermute | solution.py:66
  (165 other events, 2637.1 us)

commit v2 on v1

v2 whole, which is shorter than its diff:
```python
import functools

import jax
import jax.numpy as jnp
from jax import lax
from jax.experimental import pallas as pl
from jax.experimental.pallas import tpu as pltpu
from jax.sharding import PartitionSpec as P

HEADS = 16
EPS = 1e-05
NEGATIVE = -1e30
HIGHEST = lax.Precision.HIGHEST
BF = jnp.bfloat16
F32 = jnp.float32
BOTH = ("seq", "frame")


def normalize(values):
    center = values - jnp.mean(values, -1, keepdims=True)
    scale_inv = lax.rsqrt(jnp.mean(center * center, -1, keepdims=True) + EPS)
    return (center * scale_inv, scale_inv)


def norm_back(grad_hat, normed, scale_inv):
    return scale_inv * (
        grad_hat
        - jnp.mean(grad_hat, -1, keepdims=True)
        - normed * jnp.mean(grad_hat * normed, -1, keepdims=True)
    )


def mm(a, b):
    return jnp.dot(a, b, preferred_element_type=F32)


def mm_tn(a, b):
    return lax.dot_general(a, b, (((0,), (0,)), ((), ())), preferred_element_type=F32)


def mm_nt(a, b):
    return lax.dot_general(a, b, (((1,), (1,)), ((), ())), preferred_element_type=F32)


def ein(spec, a, b):
    return jnp.einsum(spec, a, b, preferred_element_type=F32)


def exact_gelu(values):
    return jax.nn.gelu(values, approximate=False)


def bits(n):
    return n.bit_length() - 1


class Grid:
    def __init__(self, seq_count, frame_count):
        self.seq, self.frame = seq_count, frame_count
        self.side = frame_count // 2
        self.depth = seq_count // self.side
        self.count = seq_count * frame_count

    def split(self, lin):
        side = bits(self.side)
        return lin >> (2 * side + 1), (lin >> (side + 1)) & (self.side - 1), (lin >> 1) & (self.side - 1), lin & 1

    def join(self, z, x, y, c):
        return ((z * self.side + x) * self.side + y) * 2 + c

    def send(self, value, move):
        perm = [(i, self.join(*move(*self.split(i)))) for i in range(self.count)]
        return lax.ppermute(value, BOTH, perm)

    def to_z(self, v, k):
        return self.send(v, lambda z, x, y, c: (z ^ k, x, y, c))

    def to_a(self, v, k):
        return self.send(v, lambda z, x, y, c: (z, x, y ^ k, c) if c else (z, x ^ k, y, c))

    def to_b(self, v, k):
        return self.send(v, lambda z, x, y, c: (z, x ^ k, y, c) if c else (z, x, y ^ k, c))

    def to_x(self, v, k):
        return self.send(v, lambda z, x, y, c: (z, x ^ k, y, c))

    def to_core(self, v):
        return self.send(v, lambda z, x, y, c: (z, x, y, 1 - c))

    def to_frame(self, v, k):
        def move(z, x, y, c):
            f = (y * 2 + c) ^ k
            return z, x, f // 2, f % 2

        return self.send(v, move)

    def own(self):
        return lax.axis_index("seq") * self.frame + lax.axis_index("frame")

    def scatter_core_last(self, v):
        for send, size in ((self.to_z, self.depth), (self.to_b, self.side), (self.to_a, self.side)):
            for k in reversed(self.strides(size)):
                half = v.shape[0] // 2
                v = v[:half].astype(F32) + send(v[half:].astype(BF), k).astype(F32)
        return v[0] + self.to_core(v[1].astype(BF)).astype(F32)

    def strides(self, size):
        return [1 << t for t in reversed(range(bits(size)))]

    def places(self, steps="zabc"):
        z, x, y, c = self.split(self.own())
        oz, ox, oy, oc = self.split(jnp.arange(self.count, dtype=jnp.int32))
        way = oc if steps[-1] == "c" else c
        rx, ry = ox ^ x, oy ^ y
        fields = {
            "z": (oz ^ z, self.depth),
            "a": (jnp.where(way == 0, rx, ry), self.side),
            "b": (jnp.where(way == 0, ry, rx), self.side),
            "c": (oc ^ c, 2),
        }
        place, bit = 0, 0
        for step in steps:
            value, size = fields[step]
            for k in self.strides(size):
                place = place + ((value & k != 0).astype(jnp.int32) << bit)
                bit += 1
        return place

    def owners(self, steps="zabc"):
        order = jnp.arange(self.count, dtype=jnp.int32)
        return jnp.zeros_like(order).at[self.places(steps)].set(order, unique_indices=True)

    def step(self, v, kind, k):
        send = {"z": self.to_z, "a": self.to_a, "b": self.to_b, "c": lambda p, _: self.to_core(p)}[kind]
        return jnp.concatenate([v, send(v, k)])

    def gather(self, v, steps):
        for kind in steps:
            for k in self.strides({"z": self.depth, "c": 2}.get(kind, self.side)):
                v = self.step(v, kind, k)
        return v

    def gather_ab(self, v, *others):
        v = [v]
        for k in self.strides(self.side):
            v = v + [self.to_a(p, k) for p in v]
        for k in self.strides(self.side):
            own = self.to_b(v[0], k)
            v = v + [own] + [self.to_b(after(p, own, others), k) for p in v[1:]]
        return v

    def gather_core(self, v, *others):
        return v + [self.to_core(p) for p in v[:-1]] + [self.to_core(after(v[-1], others))]


class Scatter:
    def __init__(self, grid, send, *others):
        self.grid = grid
        self.size = send.shape[0]
        half = self.size // 2
        send = after(send, others)
        self.high, self.arrays = [grid.to_core(send[half:])], [grid.to_core(send[:half])]

    def keep(self, keep):
        half = self.size // 2
        self.high.append(keep[half:])
        self.arrays.append(keep)

    def sum(self, lo, hi):
        arrays = self.arrays
        if hi > self.arrays[0].shape[0]:
            arrays, lo, hi = self.high, 0, hi - lo
        return sum(p[lo:hi].astype(F32) for p in arrays)

    def step(self, send, size, *others):
        for k in reversed(self.grid.strides(size)):
            half = self.size // 2
            self.arrays.append(send(after(self.sum(half, self.size).astype(BF), others), k))
            self.size = half

    def to_b(self, *others):
        self.step(self.grid.to_b, self.grid.side, *others)

    def to_a(self, *others):
        self.step(self.grid.to_a, self.grid.side, *others)

    def to_z(self, *others):
        self.step(self.grid.to_z, self.grid.depth, *others)

    def last(self):
        return self.arrays[-1]

    def result(self):
        return self.sum(0, 1)[0]


def after(value, *others):
    return lax.optimization_barrier((value, others))[0]


def load_blocks(order_ref, part_refs, store_ref, sem_ref):
    rows = store_ref.shape[1]
    copies = []
    for part in part_refs:
        for k in range(part.shape[0]):
            n = len(copies)
            block = part.at[k] if part.shape[1] == rows else part.at[k, pl.ds(0, rows)]
            copies.append(pltpu.make_async_copy(block, store_ref.at[order_ref[n]], sem_ref.at[n]))
    return copies


def place_copy(place_ref, block, source_ref, keep_ref, send_ref, sem_ref):
    half = keep_ref.shape[0]
    place = place_ref[block]

    @pl.when(place < half)
    def _():
        pltpu.make_async_copy(source_ref, keep_ref.at[place], sem_ref).start()

    @pl.when(place >= half)
    def _():
        pltpu.make_async_copy(source_ref, send_ref.at[place - half], sem_ref).start()


def dot(a, b):
    return lax.dot_general(a, b, (((1,), (0,)), ((), ())), preferred_element_type=F32)


def pieces_of(value):
    high = value.astype(BF).astype(F32)
    middle = (value - high).astype(BF).astype(F32)
    return high, middle, value - high - middle


def whole(shape):
    return pl.BlockSpec(shape, lambda *_: (0,) * len(shape))


SMEM = pl.BlockSpec(memory_space=pltpu.SMEM)
ANYWHERE = pl.BlockSpec(memory_space=pltpu.HBM)
LANES = 128


def params(mib):
    return pltpu.CompilerParams(vmem_limit_bytes=mib * 1024 * 1024)


def cost(flops, moved):
    return pl.CostEstimate(flops=int(flops), bytes_accessed=int(moved), transcendentals=0)


def attend_kernel(sizes, order_ref, valid_ref, query_ref, media_ref, own_ref, *refs):
    heads, group, seqs, lat, factor, part_count = sizes
    parts = refs[:part_count]
    folded_ref, score_ref, own_score_ref, context_ref, weight_ref, mix_ref, sem_ref = refs[part_count:]
    step = pl.program_id(0)
    head_dim = weight_ref.shape[1]

    @pl.when(step == 0)
    def _():
        copies = load_blocks(order_ref, parts, weight_ref, sem_ref)
        for c in copies:
            c.start()
        for c in copies:
            c.wait()

    for j in range(group):
        h = step * group + j
        folded = mm_tn(query_ref[h], weight_ref[h]) * factor
        folded_ref[j * lat : (j + 1) * lat, :] = folded.astype(BF)
    queries = folded_ref[...]
    own = own_ref[...]
    own_scores = mm_nt(queries, own)
    own_score_ref[...] = own_scores
    own_top = jnp.max(own_scores, -1, keepdims=True)
    lanes = lax.broadcasted_iota(jnp.int32, (group * lat, LANES), 1)
    for s in range(seqs):
        media = media_ref[s]
        scores = mm_nt(queries, media)
        scores = jnp.where(valid_ref[s] > 0, scores, NEGATIVE)
        score_ref[s] = scores
        top = jnp.maximum(jnp.max(scores, -1, keepdims=True), own_top)
        media_exp = jnp.exp(scores - top)
        own_exp = jnp.exp(own_scores - top)
        total = jnp.sum(media_exp, -1, keepdims=True) + jnp.sum(own_exp, -1, keepdims=True)
        mix = dot(media_exp.astype(BF), media) + dot(own_exp.astype(BF), own)
        mix = (mix * (1.0 / total)).astype(BF)
        stats = jnp.zeros(lanes.shape, F32)
        for i, piece in enumerate(pieces_of(top) + pieces_of(total)):
            stats = jnp.where(lanes == head_dim + i, piece, stats)
        for j in range(group):
            mix_ref[j, s * lat : (s + 1) * lat, :] = mix[j * lat : (j + 1) * lat, :]
            context_ref[j, s * lat : (s + 1) * lat, head_dim:] = stats[j * lat : (j + 1) * lat, head_dim:]
    for j in range(group):
        h = step * group + j
        context_ref[j, :, :head_dim] = mm_nt(mix_ref[j], weight_ref[heads + h])


def attend(order, valid, query_t, hidden_media, hidden_own, parts, factor):
    heads, head_dim, lat = query_t.shape
    seqs, patches, width = hidden_media.shape
    group = 4
    own = hidden_own.shape[0]
    rows = group * lat
    return pl.pallas_call(
        functools.partial(attend_kernel, (heads, group, seqs, lat, factor, len(parts))),
        grid=(heads // group,),
        in_specs=[SMEM, SMEM, whole(query_t.shape), whole(hidden_media.shape), whole(hidden_own.shape)]
        + [ANYWHERE] * len(parts),
        out_specs=[
            pl.BlockSpec((rows, width), lambda i: (i, 0)),
            pl.BlockSpec((seqs, rows, patches), lambda i: (0, i, 0)),
            pl.BlockSpec((rows, own), lambda i: (i, 0)),
            pl.BlockSpec((group, seqs * lat, LANES), lambda i: (i, 0, 0)),
        ],
        out_shape=[
            jax.ShapeDtypeStruct((heads * lat, width), BF),
            jax.ShapeDtypeStruct((seqs, heads * lat, patches), F32),
            jax.ShapeDtypeStruct((heads * lat, own), F32),
            jax.ShapeDtypeStruct((heads, seqs * lat, LANES), F32),
        ],
        scratch_shapes=[
            pltpu.VMEM((2 * heads, head_dim, width), BF),
            pltpu.VMEM((group, seqs * lat, width), BF),
            pltpu.SemaphoreType.DMA((2 * heads,)),
        ],
        compiler_params=params(56),
        cost_estimate=cost(15e9, 25e6),
        name="attend",
    )(order, valid, query_t, hidden_media, hidden_own, *parts)


def mixer_kernel(sizes, order_ref, latent_ref, gain_ref, *refs):
    heads, head_dim, seqs, piece_count, part_count = sizes
    pieces = refs[:piece_count]
    parts = refs[piece_count : piece_count + part_count]
    mixed_ref, normed_ref, hidden_ref, context_ref, low_ref, weight_ref, sem_ref = refs[piece_count + part_count :]
    copies = load_blocks(order_ref, parts, weight_ref, sem_ref)
    for c in copies:
        c.start()
    values = [p[...].astype(F32) for p in pieces]
    at = head_dim
    tops = [v[..., at : at + 1] + v[..., at + 1 : at + 2] + v[..., at + 2 : at + 3] for v in values]
    totals = [v[..., at + 3 : at + 4] + v[..., at + 4 : at + 5] + v[..., at + 5 : at + 6] for v in values]
    top = functools.reduce(jnp.maximum, tops)
    shares = [t * jnp.exp(p - top) for t, p in zip(totals, tops)]
    total = functools.reduce(lambda p, q: p + q, shares)
    context = functools.reduce(lambda p, q: p + q, [v * (w / total) for v, w in zip(values, shares)])
    lanes = lax.broadcasted_iota(jnp.int32, context.shape, 2)
    context_ref[...] = jnp.where(lanes == head_dim, top + jnp.log(total), context)
    for h in range(heads):
        low_ref[:, h * head_dim : (h + 1) * head_dim] = context[h, :, :head_dim].astype(BF)
    for c in copies:
        c.wait()
    weight = weight_ref[...].reshape(heads * head_dim, -1)
    mixed = jnp.concatenate([latent_ref[...]] * seqs) + dot(low_ref[...], weight)
    mixed_ref[...] = mixed
    center = mixed - jnp.mean(mixed, -1, keepdims=True)
    normed = center * lax.rsqrt(jnp.mean(center * center, -1, keepdims=True) + EPS)
    normed_ref[...] = normed
    hidden_ref[...] = (normed * gain_ref[...]).astype(BF)


def mixer(order, latent_own, gain, pieces, parts, head_dim):
    heads, rows, _ = pieces[0].shape
    own_rows, width = latent_own.shape
    count = sum(p.shape[0] for p in parts)
    block = heads * head_dim // count
    sizes = (heads, head_dim, rows // own_rows, len(pieces), len(parts))
    return pl.pallas_call(
        functools.partial(mixer_kernel, sizes),
        in_specs=[SMEM, whole(latent_own.shape), whole(gain.shape)]
        + [whole(p.shape) for p in pieces]
        + [ANYWHERE] * len(parts),
        out_specs=[whole((rows, width))] * 3 + [whole((heads, rows, LANES)), whole((rows, heads * head_dim))],
        out_shape=[
            jax.ShapeDtypeStruct((rows, width), F32),
            jax.ShapeDtypeStruct((rows, width), F32),
            jax.ShapeDtypeStruct((rows, width), BF),
            jax.ShapeDtypeStruct((heads, rows, LANES), F32),
            jax.ShapeDtypeStruct((rows, heads * head_dim), BF),
        ],
        scratch_shapes=[pltpu.VMEM((count, block, width), BF), pltpu.SemaphoreType.DMA((count,))],
        compiler_params=params(32),
        cost_estimate=cost(2e9, 8e6),
        name="mixer",
    )(order, latent_own, gain, *pieces, *parts)


def unmix_kernel(sizes, order_ref, grad_feed_ref, grad_out_ref, mixed_ref, normed_ref, gain_ref, context_ref, *refs):
    heads, head_dim, seqs, part_count = sizes
    parts = refs[:part_count]
    message_ref, grad_mixed_ref, low_ref, gain_grad_ref, residual_ref, weight_ref, sem_ref = refs[part_count:]
    copies = load_blocks(order_ref, parts, weight_ref, sem_ref)
    for c in copies:
        c.start()
    mixed = mixed_ref[...]
    center = mixed - jnp.mean(mixed, -1, keepdims=True)
    scale_inv = lax.rsqrt(jnp.mean(center * center, -1, keepdims=True) + EPS)
    normed = normed_ref[...]
    grad_feed = grad_feed_ref[...]
    gain_grad_ref[...] = jnp.sum(grad_feed * normed, 0, keepdims=True)
    grad_mixed = grad_out_ref[...] + norm_back(grad_feed * gain_ref[...], normed, scale_inv)
    grad_mixed_ref[...] = grad_mixed
    own = residual_ref.shape[0]
    residual_ref[...] = sum(grad_mixed[s * own : (s + 1) * own] for s in range(seqs))
    low = grad_mixed.astype(BF)
    low_ref[...] = low
    for c in copies:
        c.wait()
    grads = mm_nt(low, weight_ref[...].reshape(heads * head_dim, -1)).astype(BF)
    lanes = lax.broadcasted_iota(jnp.int32, (low.shape[0], LANES), 1)
    for h in range(heads):
        grad = grads[:, h * head_dim : (h + 1) * head_dim]
        context = context_ref[h]
        row = jnp.sum(grad.astype(F32) * context[:, :head_dim], -1, keepdims=True)
        log_total = context[:, head_dim : head_dim + 1]
        message = jnp.zeros(lanes.shape, F32)
        for i, piece in enumerate(pieces_of(row) + pieces_of(log_total)):
            message = jnp.where(lanes == head_dim + i, piece, message)
        message_ref[h] = message.astype(BF)
        message_ref[h, :, :head_dim] = grad


def unmix(order, grad_feed, grad_out, mixed, normed, gain, context, parts, head_dim, own_rows):
    heads, rows, _ = context.shape
    width = mixed.shape[1]
    count = sum(p.shape[0] for p in parts)
    block = heads * head_dim // count
    sizes = (heads, head_dim, rows // own_rows, len(parts))
    arrays = (grad_feed, grad_out, mixed, normed, gain, context)
    shapes = [((heads, rows, LANES), BF), ((rows, width), F32), ((rows, width), BF), ((1, width), F32), ((own_rows, width), F32)]
    return pl.pallas_call(
        functools.partial(unmix_kernel, sizes),
        in_specs=[SMEM] + [whole(a.shape) for a in arrays] + [ANYWHERE] * len(parts),
        out_specs=[whole(shape) for shape, _ in shapes],
        out_shape=[jax.ShapeDtypeStruct(*item) for item in shapes],
        scratch_shapes=[pltpu.VMEM((count, block, width), BF), pltpu.SemaphoreType.DMA((count,))],
        compiler_params=params(32),
        cost_estimate=cost(2e9, 8e6),
        name="unmix",
    )(order, *arrays, *parts)


def output_part_kernel(groups, place_ref, context_ref, low_ref, *refs):
    keep_ref, send_ref, out_ref, sem_ref = refs[-4:]
    low = low_ref[...]
    per = out_ref.shape[0] // groups
    part = context_ref.shape[1] // groups
    rows = out_ref.shape[1]
    last = pl.ds(keep_ref.shape[1] - rows, rows)
    keep_rows, send_rows = keep_ref.at[:, last], send_ref.at[:, last]
    for g in range(groups):
        value = mm_tn(context_ref[:, g * part : (g + 1) * part], low).astype(BF)
        out_ref[g * per : (g + 1) * per] = value.reshape((per,) + out_ref.shape[1:])
        for i in range(g * per, (g + 1) * per):
            place_copy(place_ref, i, out_ref.at[i], keep_rows, send_rows, sem_ref.at[i])
    for i in range(out_ref.shape[0]):
        pltpu.make_async_copy(out_ref.at[i], keep_rows.at[0], sem_ref.at[i]).wait()


def output_part_of(place, context, low, *halves):
    width = low.shape[1]
    count = place.shape[0]
    block = context.shape[1] // count
    shapes = [h.shape for h in halves] or [(count // 2, block, width)] * 2
    return pl.pallas_call(
        functools.partial(output_part_kernel, 4),
        in_specs=[SMEM, whole(context.shape), whole(low.shape)] + [ANYWHERE] * len(halves),
        out_specs=[ANYWHERE, ANYWHERE],
        out_shape=[jax.ShapeDtypeStruct(shape, BF) for shape in shapes],
        input_output_aliases={3: 0, 4: 1} if halves else {},
        scratch_shapes=[pltpu.VMEM((count, block, width), BF), pltpu.SemaphoreType.DMA((count,))],
        compiler_params=params(32),
        cost_estimate=cost(2e9, 8e6),
        name="output_part",
    )(place, context, low, *halves)


def unpack_feed_kernel(got_ref, up_ref, down_ref):
    part = got_ref.shape[-1] // 2
    for s in range(got_ref.shape[0]):
        up_ref[:, s * part : (s + 1) * part] = got_ref[s, :, :part]
        down_ref[:, s * part : (s + 1) * part] = got_ref[s, :, part:]


def unpack_feed(got):
    count, hid, part = got.shape
    out = (hid, count * part // 2)
    return pl.pallas_call(
        unpack_feed_kernel,
        in_specs=[whole(got.shape)],
        out_specs=[whole(out)] * 2,
        out_shape=[jax.ShapeDtypeStruct(out, BF)] * 2,
        cost_estimate=cost(0, 3e6),
        name="unpack_feed",
    )(got)


def pack_back_kernel(far_up_ref, far_down_ref, near_up_ref, near_down_ref, out_ref):
    part = out_ref.shape[-1] // 2
    for s in range(out_ref.shape[0]):
        at = slice(s * part, (s + 1) * part)
        out_ref[s, :, :part] = (far_up_ref[:, at] + near_up_ref[:, at]).astype(BF)
        out_ref[s, :, part:] = (far_down_ref[:, at] + near_down_ref[:, at]).astype(BF)


def pack_back(count, *grads):
    hid, width = grads[0].shape
    out = (count, hid, 2 * width // count)
    return pl.pallas_call(
        pack_back_kernel,
        in_specs=[whole(g.shape) for g in grads],
        out_specs=whole(out),
        out_shape=jax.ShapeDtypeStruct(out, BF),
        cost_estimate=cost(0, 6e6),
        name="pack_back",
    )(*grads)


def unpack_back_kernel(got_ref, up_ref, down_ref):
    hid, part = got_ref.shape[1], got_ref.shape[2] // 2
    for s in range(got_ref.shape[0]):
        up_ref[s * hid : (s + 1) * hid, :] = got_ref[s, :, :part].astype(F32)
        down_ref[s * hid : (s + 1) * hid, :] = got_ref[s, :, part:].astype(F32)


def unpack_back(got):
    count, hid, part = got.shape
    out = (count * hid, part // 2)
    return pl.pallas_call(
        unpack_back_kernel,
        in_specs=[whole(got.shape)],
        out_specs=[whole(out)] * 2,
        out_shape=[jax.ShapeDtypeStruct(out, F32)] * 2,
        cost_estimate=cost(0, 5e6),
        name="unpack_back",
    )(got)


ROOT_HALF = 0.5**0.5
DENSITY = 1 / (2 * 3.141592653589793) ** 0.5


def loads(parts, rows, store_ref, sem_ref):
    out, n = [], 0
    for part in parts:
        skip = part.shape[1] - rows
        copies = []
        for k in range(part.shape[0]):
            block = part.at[k, pl.ds(skip, rows)] if skip else part.at[k]
            copies.append(pltpu.make_async_copy(block, store_ref.at[n], sem_ref.at[n]))
            n += 1
        out.append(copies)
    return out


def start(copies):
    for c in copies:
        c.start()


def wait(copies):
    for c in copies:
        c.wait()


def feed_kernel(part_count, up_ref, down_ref, *refs):
    feed, grad = refs[:part_count], refs[part_count : 2 * part_count]
    act_ref, grad_up_ref, out_ref, feed_st, grad_st, out_st, feed_sem, grad_sem, out_sem = refs[2 * part_count :]
    n, per, width = feed[0].shape
    chunk = n * per
    feeds, grads = loads(feed, per, feed_st, feed_sem), loads(grad, per, grad_st, grad_sem)
    for i in range(part_count):
        start(feeds[i])
        start(grads[i])
    up, down = up_ref[...], down_ref[...]
    outs = []
    for i in range(part_count):
        at = slice(i * n, (i + 1) * n)
        wait(feeds[i])
        pre = mm_nt(feed_st[at].reshape(chunk, width), up)
        wait(grads[i])
        grad_act = mm_nt(grad_st[at].reshape(chunk, width), down)
        cdf = 0.5 * (1.0 + lax.erf(pre * ROOT_HALF))
        slope = cdf + pre * (jnp.exp(-0.5 * pre * pre) * DENSITY)
        act_ref[i * chunk : (i + 1) * chunk, :] = (pre * cdf).astype(BF)
        grad_up = (grad_act * slope).astype(BF)
        grad_up_ref[i * chunk : (i + 1) * chunk, :] = grad_up
        out_st[at] = dot(grad_up, up).astype(BF).reshape(n, per, width)
        outs.append(pltpu.make_async_copy(out_st.at[pl.ds(i * n, n)], out_ref.at[pl.ds(i * n, n)], out_sem.at[i]))
        outs[i].start()
    wait(outs)


def feed(up, down, feed_parts, grad_parts):
    hid, width = up.shape
    count = len(feed_parts)
    n, per, _ = feed_parts[0].shape
    rows = count * n * per
    store = pltpu.VMEM((count * n, per, width), BF)
    sems = pltpu.SemaphoreType.DMA((count * n,))
    return pl.pallas_call(
        functools.partial(feed_kernel, count),
        in_specs=[whole(up.shape), whole(down.shape)] + [ANYWHERE] * (2 * count),
        out_specs=[whole((rows, hid))] * 2 + [ANYWHERE],
        out_shape=[jax.ShapeDtypeStruct((rows, hid), BF)] * 2 + [jax.ShapeDtypeStruct((count * n, per, width), BF)],
        scratch_shapes=[store] * 3 + [sems] * 3,
        compiler_params=params(48),
        cost_estimate=cost(5e9, 8e6),
        name="feed",
    )(up, down, *feed_parts, *grad_parts)


def feed_rest_kernel(part_count, down_ref, act_ref, grad_up_ref, *refs):
    feed, grad = refs[:part_count], refs[part_count : 2 * part_count]
    up_grad_ref, down_grad_ref, out_ref, feed_st, grad_st, out_st, feed_sem, grad_sem, out_sem = refs[2 * part_count :]
    n, per, width = feed[0].shape
    chunk = n * per
    feeds, grads = loads(feed, per, feed_st, feed_sem), loads(grad, per, grad_st, grad_sem)
    for i in range(part_count):
        start(feeds[i])
        start(grads[i])
    down = down_ref[...]
    first = pl.ds(0, per)
    outs = []
    for i in range(part_count):
        at = slice(i * n, (i + 1) * n)
        act = act_ref[i * chunk : (i + 1) * chunk, :]
        out_st[at] = dot(act, down).astype(BF).reshape(n, per, width)
        outs.append(pltpu.make_async_copy(out_st.at[pl.ds(i * n, n)], out_ref.at[pl.ds(i * n, n), first], out_sem.at[i]))
        outs[i].start()
    for i in range(part_count):
        wait(feeds[i])
        wait(grads[i])
    up_grad_ref[...] = mm_tn(grad_up_ref[...], feed_st[...].reshape(part_count * chunk, width))
    down_grad_ref[...] = mm_tn(act_ref[...], grad_st[...].reshape(part_count * chunk, width))
    wait(outs)


def feed_rest(down, act, grad_up, feed_parts, grad_parts, spare):
    hid, width = down.shape
    count = len(feed_parts)
    n, per, _ = feed_parts[0].shape
    store = pltpu.VMEM((count * n, per, width), BF)
    sems = pltpu.SemaphoreType.DMA((count * n,))
    return pl.pallas_call(
        functools.partial(feed_rest_kernel, count),
        in_specs=[whole(down.shape), whole(act.shape), whole(grad_up.shape)] + [ANYWHERE] * (2 * count),
        out_specs=[whole((hid, width))] * 2 + [ANYWHERE],
        out_shape=[jax.ShapeDtypeStruct((hid, width), F32)] * 2
        + [jax.ShapeDtypeStruct((count * n, per + spare, width), BF)],
        scratch_shapes=[store] * 3 + [sems] * 3,
        compiler_params=params(48),
        cost_estimate=cost(5e9, 8e6),
        name="feed_rest",
    )(down, act, grad_up, *feed_parts, *grad_parts)


def attend_back_kernel(sizes, order_ref, place_ref, slot_ref, query_ref, media_ref, own_ref, *refs):
    heads, group, seqs, lat, factor, piece_count, part_count, first, count = sizes
    pieces = refs[:piece_count]
    folded_ref, score_ref, own_score_ref = refs[piece_count : piece_count + 3]
    parts = refs[piece_count + 3 : piece_count + 3 + part_count]
    refs = refs[piece_count + 3 + part_count :]
    (
        keep_ref,
        send_ref,
        query_part_ref,
        grad_media_ref,
        grad_own_ref,
        weight_ref,
        mix_ref,
        gp_ref,
        grad_ref,
        out_ref,
        key_mix_ref,
        sem_ref,
        out_sem_ref,
    ) = refs[-13:]
    step = pl.program_id(0)
    head_dim = weight_ref.shape[1]
    own_rows = own_ref.shape[0]

    def out_wait():
        for slot in range(2 * group):
            pltpu.make_async_copy(out_ref.at[slot], keep_ref.at[0], out_sem_ref.at[slot]).wait()

    @pl.when(step == 0)
    def _():
        loads_here = []
        for part in parts:
            for k in range(part.shape[0]):
                n = len(loads_here)
                block = order_ref[n]
                head = block & (heads - 1)
                here = (head >= first) & (head < first + count)
                to = jnp.where(here, head - first + jnp.where(block >= heads, count, 0), 0)
                loads_here.append((here, pltpu.make_async_copy(part.at[k], weight_ref.at[to], sem_ref.at[n])))
        for here, c in loads_here:
            pl.when(here)(c.start)
        grad_media_ref[...] = jnp.zeros_like(grad_media_ref)
        grad_own_ref[...] = jnp.zeros_like(grad_own_ref)
        query_part_ref[...] = jnp.zeros_like(query_part_ref)
        for here, c in loads_here:
            pl.when(here)(c.wait)

    columns = []
    for j in range(group):
        h = step * group + j
        for s in range(seqs):
            for k in range(piece_count):
                at = s * lat + k * own_rows
                grad_ref[j, at : at + own_rows, :] = pieces[k][first + h, s * own_rows : (s + 1) * own_rows, :]
        message = grad_ref[j].astype(F32)
        column = [message[:, head_dim + i : head_dim + i + 1] for i in range(6)]
        columns.append((column[0] + column[1] + column[2], column[3] + column[4] + column[5]))
        lifted = dot(grad_ref[j, :, :head_dim], weight_ref[count + h]).astype(BF)
        for s in range(seqs):
            gp_ref[s, j * lat : (j + 1) * lat, :] = lifted[s * lat : (s + 1) * lat, :]
    queries = folded_ref[...]
    own = own_ref[...]
    own_scores = own_score_ref[...]
    key_mix = jnp.zeros(queries.shape, F32)
    for s in range(seqs):
        media = media_ref[s]
        lifted = gp_ref[s]
        row_term, log_total = (
            jnp.concatenate([columns[j][i][s * lat : (s + 1) * lat] for j in range(group)]) for i in range(2)
        )
        probs = jnp.exp(score_ref[s] - log_total)
        own_probs = jnp.exp(own_scores - log_total)
        ds = (probs * (mm_nt(lifted, media) - row_term)).astype(BF)
        own_ds = (own_probs * (mm_nt(lifted, own) - row_term)).astype(BF)
        probs, own_probs = probs.astype(BF), own_probs.astype(BF)
        key_mix = key_mix + dot(ds, media) + dot(own_ds, own)
        mix = (dot(probs, media) + dot(own_probs, own)).astype(BF)
        for j in range(group):
            mix_ref[j, s * lat : (s + 1) * lat, :] = mix[j * lat : (j + 1) * lat, :]
        grad_media_ref[s] += mm_tn(ds, queries) + mm_tn(probs, lifted)
        grad_own_ref[...] += mm_tn(own_ds, queries) + mm_tn(own_probs, lifted)
    key_mix_ref[...] = (key_mix * factor).astype(BF)
    per = query_part_ref.shape[0] // heads
    pl.when(step > 0)(out_wait)
    for j in range(group):
        h = step * group + j
        mixed = key_mix_ref[j * lat : (j + 1) * lat, :]
        sorted_rows = [
            key_mix_ref[pl.ds(pl.multiple_of(j * lat + (k ^ slot_ref[0]) * own_rows, own_rows), own_rows), :]
            for k in range(piece_count)
        ]
        part = mm_nt(weight_ref[h], jnp.concatenate(sorted_rows)).astype(BF)
        for i in range(per):
            rows = head_dim // per
            query_part_ref[place_ref[(first + h) * per + i]] = part[i * rows : (i + 1) * rows]
        out_ref[2 * j] = dot(query_ref[first + h], mixed).astype(BF)
        out_ref[2 * j + 1] = mm_tn(grad_ref[j, :, :head_dim], mix_ref[j]).astype(BF)
        for i in range(2):
            slot = 2 * j + i
            place_copy(place_ref, first + h + i * heads, out_ref.at[slot], keep_ref, send_ref, out_sem_ref.at[slot])
    pl.when(step == pl.num_programs(0) - 1)(out_wait)


def attend_back(order, place, slot, query_t, hidden_media, hidden_own, pieces, folded, scores, own_scores, parts, factor, first, count, *halves):
    heads, head_dim, lat = query_t.shape
    seqs, patches, width = hidden_media.shape
    group = 4
    own = hidden_own.shape[0]
    block = group * lat
    sizes = (heads, group, seqs, lat, factor, len(pieces), len(parts), first, count)
    skip = first // group
    position = 9 + len(pieces) + len(parts)
    return pl.pallas_call(
        functools.partial(attend_back_kernel, sizes),
        grid=(count // group,),
        in_specs=[SMEM, SMEM, SMEM, whole(query_t.shape), whole(hidden_media.shape), whole(hidden_own.shape)]
        + [whole(p.shape) for p in pieces]
        + [
            pl.BlockSpec((block, width), lambda i: (i + skip, 0)),
            pl.BlockSpec((seqs, block, patches), lambda i: (0, i + skip, 0)),
            pl.BlockSpec((block, own), lambda i: (i + skip, 0)),
        ]
        + [ANYWHERE] * (len(parts) + len(halves)),
        out_specs=[
            ANYWHERE,
            ANYWHERE,
            whole((2 * heads, head_dim // 2, lat)),
            whole(hidden_media.shape),
            whole(hidden_own.shape),
        ],
        out_shape=[
            jax.ShapeDtypeStruct((heads, head_dim, width), BF),
            jax.ShapeDtypeStruct((heads, head_dim, width), BF),
            jax.ShapeDtypeStruct((2 * heads, head_dim // 2, lat), BF),
            jax.ShapeDtypeStruct(hidden_media.shape, F32),
            jax.ShapeDtypeStruct(hidden_own.shape, F32),
        ],
        scratch_shapes=[
            pltpu.VMEM((2 * count, head_dim, width), BF),
            pltpu.VMEM((group, seqs * lat, width), BF),
            pltpu.VMEM((seqs, block, width), BF),
            pltpu.VMEM((group, seqs * lat, LANES), BF),
            pltpu.VMEM((2 * group, head_dim, width), BF),
            pltpu.VMEM((block, width), BF),
            pltpu.SemaphoreType.DMA((2 * heads,)),
            pltpu.SemaphoreType.DMA((2 * group,)),
        ],
        input_output_aliases={position: 0, position + 1: 1} if halves else {},
        compiler_params=params(60),
        cost_estimate=cost(12e9, 20e6),
        name="attend_back",
    )(order, place, slot, query_t, hidden_media, hidden_own, *pieces, folded, scores, own_scores, *parts, *halves)


def local(
    grid,
    media,
    image_counts,
    time_ids,
    latents,
    time_table,
    media_gain,
    latent_gain,
    feed_gain,
    query_weight,
    keyval_weight,
    output_weight,
    up_weight,
    down_weight,
    cotangent,
):
    width = output_weight.shape[1]
    head_dim = width // HEADS
    factor = head_dim ** (-0.5)
    lat_rows = latents.shape[0]
    times = time_table.shape[0]
    seq_here, patches = media.shape[0], media.shape[2]
    own_rows = lat_rows // grid.frame
    rows = seq_here * own_rows
    part = width // grid.count
    slot = lax.axis_index("frame")
    first_row = slot * own_rows
    places, owners = grid.places(), grid.owners()
    aligned = grid.count == 2 * HEADS
    if aligned:
        order, place = owners, places
    else:
        order = place = jnp.arange(2 * HEADS, dtype=jnp.int32)

    def scatter_order(keep, send):
        if aligned:
            return keep, send
        v = jnp.concatenate([keep, send]).reshape(grid.count, -1, keep.shape[-1])
        v = v.at[owners].get(mode="promise_in_bounds")
        return v[: grid.count // 2], v[grid.count // 2 :]

    def aligned_parts(parts):
        if aligned:
            return parts
        flat = jnp.concatenate(parts).at[places].get(mode="promise_in_bounds")
        return [flat.reshape(2 * HEADS, -1, width)]

    pad = (-(lat_rows + times + 3)) % 8
    packed = jnp.concatenate(
        [latents, time_table, media_gain[None], latent_gain[None], feed_gain[None], jnp.zeros((pad, part), BF)]
    )
    small = grid.gather(packed.T[None], "z")
    first, *rest = grid.strides(grid.depth)
    keyval_z = grid.step(after(keyval_weight.T, small)[None], "z", first)
    small = after(small, keyval_z)
    for k in rest:
        keyval_z = grid.step(keyval_z, "z", k)
    small = grid.gather(small, "abc").at[places].get(mode="promise_in_bounds")
    small = small.reshape(width, -1).T.astype(F32)
    lat_float = small[:lat_rows]
    table_all = small[lat_rows : lat_rows + times]
    media_scale, latent_scale, feed_scale = (small[lat_rows + times + i][None] for i in range(3))

    grad_out = cotangent.reshape(rows, width)
    hid_f = up_weight.shape[1]
    hid = hid_f // grid.seq
    d_part = up_weight.shape[0]
    blocks = (grid.seq, hid, d_part)
    feed_got = jnp.concatenate([up_weight.T.reshape(blocks), down_weight.reshape(blocks)], -1)
    is_valid = (slot < image_counts).astype(jnp.int32)
    onehot = (time_ids[:, 0][:, None] == jnp.arange(times, dtype=jnp.int32)[None, :]).astype(F32)
    embedding = jnp.dot(onehot, table_all, precision=HIGHEST)
    embedded = media[:, 0].astype(F32) + embedding[:, None, :]
    normed_media, inv_media = normalize(embedded)
    hidden_media = (normed_media * media_scale).astype(BF)

    normed_lat, inv_lat = normalize(lat_float)
    hidden_lat = (normed_lat * latent_scale).astype(BF)
    hidden_own = lax.dynamic_slice_in_dim(hidden_lat, first_row, own_rows, 0)
    lat_own = lax.dynamic_slice_in_dim(lat_float, first_row, own_rows, 0)
    query_own = mm_tn(query_weight, hidden_lat.T).astype(BF)
    frame_ids = jnp.arange(grid.frame, dtype=jnp.int32) ^ slot
    query_t = after(grid.gather(query_own[None], "cab"), keyval_z)
    query_t = grid.gather(query_t, "z")
    first, *rest = grid.strides(grid.depth)
    mixed_first = grid.step(after(jnp.concatenate([output_weight, grad_out.astype(BF)]), query_t)[None], "z", first)
    mixed_z = mixed_first
    for k in rest:
        mixed_z = grid.step(mixed_z, "z", k)
    query_t = query_t.reshape(grid.count, part, grid.frame, own_rows)
    query_places = grid.places("cabz")
    query_t = query_t.at[query_places[:, None], :, frame_ids[None, :]].get(mode="promise_in_bounds")
    query_t = query_t.transpose(0, 2, 1, 3).reshape(HEADS, head_dim, lat_rows)
    keyval_ab = grid.gather_ab(keyval_z, query_t, mixed_first)
    keyval_parts = aligned_parts(grid.gather_core(keyval_ab, mixed_z))
    mixed_z = after(mixed_z, keyval_ab)
    feed_got = lax.all_to_all(after(feed_got, mixed_z), "seq", 0, 0)
    folded, media_scores, own_scores, context_parts = attend(
        order, is_valid, query_t, hidden_media, hidden_own, keyval_parts, factor
    )
    context_parts = context_parts.reshape(HEADS, seq_here, grid.frame, own_rows, LANES)
    pieces = [context_parts[:, :, k].reshape(HEADS, rows, LANES).astype(BF) for k in range(grid.frame)]
    pieces = after(pieces, feed_got)
    pieces = [pieces[0]] + [grid.to_frame(pieces[k], k) for k in range(1, grid.frame)]
    mixed_parts = grid.gather_core(grid.gather_ab(mixed_z, folded))
    if aligned:
        output_parts, grad_parts = mixed_parts, mixed_parts
    else:
        output_parts = aligned_parts([p[:, :part] for p in mixed_parts])
        grad_parts = [p[:, part:] for p in mixed_parts]
    mixed, normed_feed, hidden_feed, context, context_low = mixer(
        order, lat_own, feed_scale, pieces, output_parts, head_dim
    )

    up_t, down_w = unpack_feed(feed_got)
    feed_parts = grid.gather_core(grid.gather_ab(grid.gather(hidden_feed[None], "z"), up_t))
    half = len(feed_parts) // 2
    far, near = (feed_parts[half:], grad_parts[half:]), (feed_parts[:half], grad_parts[:half])
    far_act, far_grad_up, send = feed(up_t, down_w, *far)
    grad_sum = Scatter(grid, send)
    near_act, near_grad_up, keep = feed(up_t, down_w, *after(near, send))
    grad_sum.keep(keep)
    grad_sum.to_b()
    spare = part if aligned else 0
    far_up, far_down, send = feed_rest(down_w, far_act, after(far_grad_up, keep), *far, spare)
    near_up, near_down, keep = feed_rest(down_w, near_act, after(near_grad_up, send), *near, spare)
    grad_sum.to_a(send)
    grad_sum.to_z(keep)
    back = pack_back(grid.seq, far_up, far_down, near_up, near_down)
    grad_feed = after(grad_sum.result(), back)
    message, grad_mixed, grad_mixed_low, feed_gain_part, residual = unmix(
        order, grad_feed, grad_out, mixed, normed_feed, feed_scale, context, output_parts, head_dim, own_rows
    )
    messages = [message] + [grid.to_frame(message, k) for k in range(1, grid.frame)]
    back = lax.all_to_all(after(back, message), "seq", 0, 0)
    if aligned:
        keep, send = output_part_of(place, after(context_low, messages), grad_mixed_low, keep, send)
    else:
        out_keep, out_send = scatter_order(*output_part_of(place, context_low, grad_mixed_low))
        keep, send = jnp.concatenate([keep, out_keep], 1), jnp.concatenate([send, out_send], 1)
    mixed_sum = Scatter(grid, send)
    mixed_sum.keep(keep)
    messages = after(messages, keep)

    def back_half(messages, first, *halves):
        return attend_back(
            order, place, slot.reshape(1), query_t, hidden_media, hidden_own, messages, folded, media_scores, own_scores,
            keyval_parts, factor, first, HEADS // 2, *halves,
        )

    keep, send, query_near, grad_hidden_near, grad_own_near = back_half(messages, 0)
    keep, send = after((keep, send), mixed_sum.arrays[0])
    mixed_sum.to_b(send, back)
    keep, send, query_far, grad_hidden_far, grad_own_far = back_half(messages, HEADS // 2, keep, send)
    keep, send = scatter_order(keep, send)
    keyval_sum = Scatter(grid, send)
    keyval_sum.keep(keep)
    half = grid.count // 2
    query_part = query_near + query_far
    if not aligned:
        query_part = query_part.reshape(grid.count, part, lat_rows).at[owners].get(mode="promise_in_bounds")
    query_part = after(query_part, mixed_sum.last())
    query_sum = Scatter(grid, query_part[half:])
    query_sum.keep(query_part[:half])
    mixed_sum.to_a(send)
    query_sum.to_b()
    query_sum.to_a()
    keyval_sum.to_b(query_sum.last(), mixed_sum.last())
    keyval_b = keyval_sum.last()
    query_sum.to_z(keyval_sum.arrays[0])
    query_sum = query_sum.result().T.astype(BF)
    mixed_sum.to_z(query_sum)
    grad_hidden_near = after(grad_hidden_near, keyval_sum.arrays[0])
    back = after(back, keyval_b)
    grad_hidden = grad_hidden_near + grad_hidden_far
    grad_hidden_own = grad_own_near + grad_own_far

    media_gain_part = jnp.sum(grad_hidden * normed_media, (0, 1))
    grad_embedded = norm_back(grad_hidden * media_scale, normed_media, inv_media)
    table_part = jnp.dot(onehot.T, jnp.sum(grad_embedded, 1), precision=HIGHEST)

    query_grad = mm_tn(hidden_lat, query_sum)
    grad_lat = mm_nt(query_sum, query_weight)
    grad_lat = grad_lat + lax.dynamic_update_slice_in_dim(jnp.zeros_like(grad_lat), grad_hidden_own, first_row, 0)
    latent_gain_part = jnp.sum(grad_lat * normed_lat, 0)
    latents_part = norm_back(grad_lat * latent_scale, normed_lat, inv_lat)
    latents_part = latents_part + lax.dynamic_update_slice_in_dim(
        jnp.zeros_like(latents_part), residual, first_row, 0
    )
    smalls = jnp.concatenate(
        [
            latents_part,
            table_part,
            media_gain_part[None],
            latent_gain_part[None],
            feed_gain_part,
            jnp.zeros((pad, width), F32),
        ]
    ).astype(BF)
    smalls = smalls.T.reshape(grid.count, part, -1).at[grid.owners("cabz")].get(mode="promise_in_bounds")
    small_sum = grid.scatter_core_last(after(smalls, keyval_b)).T
    keyval_sum.to_a()
    keyval_sum.to_z()
    up_grad_t, down_grad = unpack_back(back)
    up_grad = up_grad_t.T
    keyval_grad = keyval_sum.result().T
    mixed_sums = mixed_sum.result()
    new_latents = (mixed + mixed_sums[:rows]).reshape(seq_here, own_rows, width)
    output_grad = mixed_sums[rows:]
    latents_grad = small_sum[:lat_rows]
    table_grad = small_sum[lat_rows : lat_rows + times]
    media_gain_grad, latent_gain_grad, feed_gain_grad = (small_sum[lat_rows + times + i] for i in range(3))
    return (
        new_latents,
        grad_embedded[:, None],
        latents_grad,
        table_grad,
        media_gain_grad,
        latent_gain_grad,
        feed_gain_grad,
        query_grad,
        keyval_grad,
        output_grad,
        up_grad,
        down_grad,
    )


def solution(mesh):
    grid = Grid(mesh.shape["seq"], mesh.shape["frame"])

    def run(*args):
        return local(grid, *args)

    return jax.shard_map(
        run,
        mesh=mesh,
        in_specs=(
            P("seq", "frame", None, None),
            P("seq"),
            P("seq", "frame"),
            P(None, BOTH),
            P(None, BOTH),
            P(BOTH),
            P(BOTH),
            P(BOTH),
            P(None, BOTH),
            P(None, BOTH),
            P(BOTH, None),
            P("seq", "frame"),
            P("frame", "seq"),
            P("seq", "frame", None),
        ),
        out_specs=(
            P("seq", "frame", None),
            P("seq", "frame", None, None),
            P(None, BOTH),
            P(None, BOTH),
            P(BOTH),
            P(BOTH),
            P(BOTH),
            P(None, BOTH),
            P(None, BOTH),
            P(BOTH, None),
            P("seq", "frame"),
            P("frame", "seq"),
        ),
        check_vma=False,
    )
```

time: 758 us -> 532 us (0.70)
  Pallas kernels: 0 us -> 134 us
  matrix products: 129 us -> 2.47 us
  local copies, waits for them, and re-layouts: 127 us -> 47.7 us
  other arithmetic: 125 us -> 58.1 us
  waiting for transfers between devices: 234 us -> 180 us
  starting transfers between devices: 130 us -> 99.2 us
    pallas_call x0 -> x13, Pallas kernels: none -> 134 us  [the longest x2 47.6 us: attend_back(): pl.pallas_call(functools.partial(attend_back_kernel, sizes), grid=(count...]
    dot_general x24 -> x0, matrix products: 116 us -> none  [the longest x22 113 us: ein(): return jnp.einsum(spec, a, b, preferred_element_type=F32)]
    ppermute x98 -> x72, waiting for transfers between devices: 234 us -> 179 us  [send(): return lax.ppermute(value, BOTH, perm)]
    another operation x36 -> x3, other arithmetic: 52.5 us -> 1.56 us  [the longest x12 36.4 us: gather(): v = jnp.stack([v, self.to_core(v)])]
    ppermute x98 -> x72, starting transfers between devices: 130 us -> 87.3 us  [send(): return lax.ppermute(value, BOTH, perm)]
    gather x15 -> x3, local copies, waits for them, and re-layouts: 46.1 us -> 3.82 us  [the longest x1 1.7 us: local(): query_t.at[query_places[:, None], :, frame_ids[None, :]]]
    convert_element_type x8 -> x21, other arithmetic: 3.19 us -> 32.6 us  [the longest x16 28.7 us: step(): self.sum(half, self.size).astype(BF)]
    select_n x15 -> x3, other arithmetic: 29 us -> 0.03 us  [the longest x1 0.02 us: local(): query_t.at[query_places[:, None], :, frame_ids[None, :]]]
  transfers between devices with their start and end apart: 98 -> 74, of which waited for: 40 -> 41; matrix products, arithmetic and copies ran while one was open for 48% -> 15% of each run, Pallas kernels for 0% -> 19%
where the time goes in v2:
time: 532 us; the launch traced here: 524 us
  waiting for transfers between devices  180 us (34%)
  Pallas kernels  134 us (25%)
  starting transfers between devices  99.2 us (19%)
  other arithmetic  58.1 us (11%)
  local copies, waits for them, and re-layouts  47.7 us (9%)
    ppermute x72, waiting for transfers between devices, send(): return lax.ppermute(value, BOTH, perm)  179 us
    ppermute x72, starting transfers between devices, send(): return lax.ppermute(value, BOTH, perm)  87.3 us
    pallas_call x2, Pallas kernels, attend_back(): pl.pallas_call(functools.partial(attend_back_kernel, sizes), grid=(count...  47.6 us
    convert_element_type x16, other arithmetic, step(): self.sum(half, self.size).astype(BF)  28.7 us
    pallas_call x1, Pallas kernels, attend(): pl.pallas_call(functools.partial(attend_kernel, (heads, group, seqs, lat,...  22.8 us
    pallas_call x2, Pallas kernels, feed(): pl.pallas_call(functools.partial(feed_kernel, count), in_specs=[whole(up....  18.5 us
    unnamed x133, local copies, waits for them, and re-layouts  16.9 us
    pallas_call x2, Pallas kernels, feed_rest(): pl.pallas_call(functools.partial(feed_rest_kernel, count), in_specs=[whol...  12.7 us
  transfers between devices with their start and end apart: 74, of which 41 were waited for; matrix products, arithmetic and copies ran while one was open for 15% of the time, Pallas kernels for 19%

profile of v2, /device:TPU:0, one launch (start us, length us, event | category | flops | bytes accessed | tf_op | source)
XLA Modules:
  0.0 524.2 jit_solution(7046377651702392705)
XLA Ops:
  18.2 10.3 %collective-permute-done.2 = bf16[1,96,1536]{2,1,0:T(8,128)(2,1)S(1)} collective-permute-done((bf16[1,96,1536]{2,1,0:T(8,128)(2,1)}, bf16[1,96,1536]{2,1,0:T(8,128)(2,1)S(1)}, u32[]{:S(2)}, u32[]{:S(2)}) %collective-permute-start.2) | collective-permute-done | bytes 294944 | tf_op jit(solution)/shard_map/ppermute | solution.py:73
  91.0 11.8 %collective-permute-done.19 = bf16[2,96,1536]{2,1,0:T(8,128)(2,1)S(1)} collective-permute-done((bf16[2,96,1536]{2,1,0:T(8,128)(2,1)S(1)}, bf16[2,96,1536]{2,1,0:T(8,128)(2,1)S(1)}, u32[]{:S(2)}, u32[]{:S(2)}) %collective-permute-start.19) | collective-permute-done | bytes 589856 | tf_op jit(solution)/shard_map/ppermute | solution.py:73
  111.8 5.9 %all-to-all-start = ((bf16[8,192,384]{2,1,0:T(8,128)(2,1)}), bf16[8,192,384]{2,1,0:T(8,128)(2,1)}, u32[]{:S(2)}, u32[]{:S(2)}) async-start(bf16[8,192,384]{2,1,0:T(8,128)(2,1)} %pad_maximum_fusion.2), calls=%async_computation | async-start | bytes 2359296 | tf_op jit(solution)/shard_map/all_to_all | solution.py:912
  118.3 22.8 %attend.1 = (bf16[1024,1536]{1,0:T(8,128)(2,1)}, f32[3,1024,256]{2,1,0:T(8,128)}, f32[1024,16]{1,0:T(8,128)}, f32[16,192,128]{2,1,0:T(8,128)}) custom-call(s32[32]{0:T(128)} %scatter_custom_fusion.order_ref, s32[3]{0:T(128)} %compare_convert_fusion.9.valid_ref, bf16[16,96,64]{2,1,0:T(8,128)(2,1)} %copy.76.query_ref, bf16[3,256,1536]{2,1,0:T(8,128)(2,1)} %fusion.8.media_ref, ...), custom_call_target="tpu_custom_call" | custom-call | flops 15000000512 | bytes 25000000 | tf_op jit(solution)/shard_map/attend/pallas_call | solution.py:305
  142.7 10.5 %collective-permute-start.27 = (bf16[4,96,1536]{2,1,0:T(8,128)(2,1)S(1)}, bf16[4,96,1536]{2,1,0:T(8,128)(2,1)}, u32[]{:S(2)}, u32[]{:S(2)}) collective-permute-start(bf16[4,96,1536]{2,1,0:T(8,128)(2,1)S(1)} %pad_maximum_fusion.1.refs_4_.refs_0_), channel_id=1, source_target_pairs={{0,1},{1,0},{2,3},{3,2},{4,5},{5,4},{6,7},{7,6},{8,9},{9,8},{10,11... | collective-permute-start | bytes 3538952 | tf_op jit(solution)/shard_map/ppermute | solution.py:73
  158.4 8.7 %collective-permute-start.30 = (bf16[4,96,1536]{2,1,0:T(8,128)(2,1)}, bf16[4,96,1536]{2,1,0:T(8,128)(2,1)}, u32[]{:S(2)}, u32[]{:S(2)}) collective-permute-start(bf16[4,96,1536]{2,1,0:T(8,128)(2,1)} %collective-permute-done.26.refs_7_.refs_3_), channel_id=1, source_target_pairs={{0,1},{1,0},{2,3},{3,2},{4,5},{5,4},{6,7},{7,6},{8,9},{9,8},{10,11... | collective-permute-start | bytes 3538952 | tf_op jit(solution)/shard_map/ppermute | solution.py:73
  180.0 7.1 %mixer.1 = (f32[48,1536]{1,0:T(8,128)S(1)}, f32[48,1536]{1,0:T(8,128)S(1)}, bf16[48,1536]{1,0:T(8,128)(2,1)S(1)}, f32[16,48,128]{2,1,0:T(8,128)S(1)}, bf16[48,1536]{1,0:T(8,128)(2,1)S(1)}) custom-call(s32[32]{0:T(128)S(1)} %copy-done.18, f32[16,1536]{1,0:T(8,128)S(1)} %constant_dynamic-slice_fusion.1.latent_ref, f32[1,1536]{1,0:T(1,128)S(1)} %get-tuple-element.250.gain_ref, ...), custom_call_target="tpu_custom_call" | custom-call | flops 2000000000 | bytes 8000000 | tf_op jit(solution)/shard_map/mixer/pallas_call | solution.py:370
  190.5 7.5 %collective-permute-done.31 = bf16[1,48,1536]{2,1,0:T(8,128)(2,1)S(1)} collective-permute-done((bf16[1,48,1536]{2,1,0:T(8,128)(2,1)S(1)}, bf16[1,48,1536]{2,1,0:T(8,128)(2,1)S(1)}, u32[]{:S(2)}, u32[]{:S(2)}) %collective-permute-start.31) | collective-permute-done | bytes 147488 | tf_op jit(solution)/shard_map/ppermute | solution.py:73
  198.8 8.0 %collective-permute-done.32 = bf16[2,48,1536]{2,1,0:T(8,128)(2,1)S(1)} collective-permute-done((bf16[2,48,1536]{2,1,0:T(8,128)(2,1)S(1)}, bf16[2,48,1536]{2,1,0:T(8,128)(2,1)S(1)}, u32[]{:S(2)}, u32[]{:S(2)}) %collective-permute-start.32) | collective-permute-done | bytes 294944 | tf_op jit(solution)/shard_map/ppermute | solution.py:73
  211.5 9.9 %collective-permute-done.34.refs_1_ = bf16[4,48,1536]{2,1,0:T(8,128)(2,1)S(1)} collective-permute-done((bf16[4,48,1536]{2,1,0:T(8,128)(2,1)S(1)}, bf16[4,48,1536]{2,1,0:T(8,128)(2,1)S(1)}, u32[]{:S(2)}, u32[]{:S(2)}) %collective-permute-start.34) | collective-permute-done | bytes 589856 | tf_op jit(solution)/shard_map/ppermute | solution.py:73
  223.3 7.8 %collective-permute-done.38.refs_3_ = bf16[4,48,1536]{2,1,0:T(8,128)(2,1)S(1)} collective-permute-done((bf16[4,48,1536]{2,1,0:T(8,128)(2,1)S(1)}, bf16[4,48,1536]{2,1,0:T(8,128)(2,1)S(1)}, u32[]{:S(2)}, u32[]{:S(2)}) %collective-permute-start.38) | collective-permute-done | bytes 589856 | tf_op jit(solution)/shard_map/ppermute | solution.py:73
  235.3 9.1 %feed.2 = (bf16[768,192]{1,0:T(8,128)(2,1)S(1)}, bf16[768,192]{1,0:T(8,128)(2,1)S(1)}, bf16[16,48,1536]{2,1,0:T(8,128)(2,1)}) custom-call(bf16[192,1536]{1,0:T(8,128)(2,1)S(1)} %copy-done.22, bf16[192,1536]{1,0:T(8,128)(2,1)S(1)} %copy-done.20, bf16[4,48,1536]{2,1,0:T(8,128)(2,1)S(1)} %collective-permute-done.33.refs_0_, ...), custom_call_target="tpu_custom_call" | custom-call | flops 5000000000 | bytes 8000000 | tf_op jit(solution)/shard_map/feed/pallas_call | solution.py:603
  247.8 9.4 %feed.3 = (bf16[768,192]{1,0:T(8,128)(2,1)S(1)}, bf16[768,192]{1,0:T(8,128)(2,1)S(1)}, bf16[16,48,1536]{2,1,0:T(8,128)(2,1)}) custom-call(bf16[192,1536]{1,0:T(8,128)(2,1)S(1)} %copy-done.22, bf16[192,1536]{1,0:T(8,128)(2,1)S(1)} %copy-done.20, bf16[4,48,1536]{2,1,0:T(8,128)(2,1)S(1)} %pad_maximum_fusion.5.refs_0_, ...), custom_call_target="tpu_custom_call" | custom-call | flops 5000000000 | bytes 8000000 | tf_op jit(solution)/shard_map/feed/pallas_call | solution.py:603
  260.5 6.9 %feed_rest.2 = (f32[192,1536]{1,0:T(8,128)S(1)}, f32[192,1536]{1,0:T(8,128)S(1)}, bf16[16,96,1536]{2,1,0:T(8,128)(2,1)}) custom-call(bf16[192,1536]{1,0:T(8,128)(2,1)S(1)} %copy-done.21, bf16[768,192]{1,0:T(8,128)(2,1)S(1)} %get-tuple-element.131.act_ref, bf16[768,192]{1,0:T(8,128)(2,1)S(1)} %get-tuple-element.133.grad_up_ref, ...), custom_call_target="tpu_custom_call" | custom-call | flops 5000000000 | bytes 8000000 | tf_op jit(solution)/shard_map/feed_rest/pallas_call | solution.py:647
  289.4 6.1 %collective-permute-done.44 = bf16[2,48,1536]{2,1,0:T(8,128)(2,1)S(1)} collective-permute-done((bf16[2,48,1536]{2,1,0:T(8,128)(2,1)S(1)}, bf16[2,48,1536]{2,1,0:T(8,128)(2,1)S(1)}, u32[]{:S(2)}, u32[]{:S(2)}) %collective-permute-start.44) | collective-permute-done | bytes 294944 | tf_op jit(solution)/shard_map/ppermute | solution.py:73
  308.1 6.3 %unmix.1 = (bf16[16,48,128]{2,1,0:T(8,128)(2,1)S(1)}, f32[48,1536]{1,0:T(8,128)}, bf16[48,1536]{1,0:T(8,128)(2,1)S(1)}, f32[1,1536]{1,0:T(1,128)S(1)}, f32[16,1536]{1,0:T(8,128)S(1)}) custom-call(s32[32]{0:T(128)S(1)} %copy-done.18, f32[48,1536]{1,0:T(8,128)S(1)} %add_bitcast_fusion.1.grad_feed_ref, f32[48,1536]{1,0:T(8,128)S(1)} %bitcast.110, ...), custom_call_target="tpu_custom_call" | custom-call | flops 2000000000 | bytes 8000000 | tf_op jit(solution)/shard_map/unmix/pallas_call | solution.py:433
  316.4 5.9 %collective-permute-done.47.refs_2_ = bf16[16,48,128]{2,1,0:T(8,128)(2,1)S(1)} collective-permute-done((bf16[16,48,128]{2,1,0:T(8,128)(2,1)S(1)}, bf16[16,48,128]{2,1,0:T(8,128)(2,1)S(1)}, u32[]{:S(2)}, u32[]{:S(2)}) %collective-permute-start.47) | collective-permute-done | bytes 196640 | tf_op jit(solution)/shard_map/ppermute | solution.py:73
  325.6 9.7 %output_part.1 = (bf16[16,96,1536]{2,1,0:T(8,128)(2,1)S(1)}, bf16[16,96,1536]{2,1,0:T(8,128)(2,1)S(1)}) custom-call(s32[32]{0:T(128)S(1)} %shift-left_add_fusion.place_ref, bf16[48,1536]{1,0:T(8,128)(2,1)S(1)} %copy-done.15, bf16[48,1536]{1,0:T(8,128)(2,1)S(1)} %get-tuple-element.151.low_ref, ...), custom_call_target="tpu_custom_call", output_to_operand_aliasing={{0}: (3, {}), {1}: (4, {})} | custom-call | flops 2000000000 | bytes 8000000 | tf_op jit(solution)/shard_map/output_part/pallas_call | solution.py:467
  339.4 6.0 %all-to-all-start.1 = ((bf16[8,192,384]{2,1,0:T(8,128)(2,1)}), bf16[8,192,384]{2,1,0:T(8,128)(2,1)S(1)}, u32[]{:S(2)}, u32[]{:S(2)}) async-start(bf16[8,192,384]{2,1,0:T(8,128)(2,1)} %pack_back.1), calls=%async_computation.1 | async-start | bytes 2359296 | tf_op jit(solution)/shard_map/all_to_all | solution.py:950
  345.4 23.7 %attend_back.2 = (bf16[16,96,1536]{2,1,0:T(8,128)(2,1)}, bf16[16,96,1536]{2,1,0:T(8,128)(2,1)}, bf16[32,48,64]{2,1,0:T(8,128)(2,1)}, f32[3,256,1536]{2,1,0:T(8,128)}, f32[16,1536]{1,0:T(8,128)}) custom-call(s32[32]{0:T(128)} %scatter_custom_fusion.order_ref, s32[32]{0:T(128)} %copy-done.19, s32[1]{0:T(128)} %bitcast.32.slot_ref, ...), custom_call_target="tpu_custom_call" | custom-call | flops 12000000000 | bytes 20000000 | tf_op jit(solution)/shard_map/attend_back/pallas_call | solution.py:773
  375.9 23.9 %attend_back.3 = (bf16[16,96,1536]{2,1,0:T(8,128)(2,1)}, bf16[16,96,1536]{2,1,0:T(8,128)(2,1)}, bf16[32,48,64]{2,1,0:T(8,128)(2,1)}, f32[3,256,1536]{2,1,0:T(8,128)}, f32[16,1536]{1,0:T(8,128)}) custom-call(s32[32]{0:T(128)} %scatter_custom_fusion.order_ref, s32[32]{0:T(128)} %copy-done.19, ...), custom_call_target="tpu_custom_call", output_to_operand_aliasing={{0}: (21, {}), {1}: (22, {})} | custom-call | flops 12000000000 | bytes 20000000 | tf_op jit(solution)/shard_map/attend_back/pallas_call | solution.py:773
  447.7 8.2 %collective-permute-done.60 = bf16[2,96,1536]{2,1,0:T(8,128)(2,1)} collective-permute-done((bf16[2,96,1536]{2,1,0:T(8,128)(2,1)}, bf16[2,96,1536]{2,1,0:T(8,128)(2,1)}, u32[]{:S(2)}, u32[]{:S(2)}) %collective-permute-start.60) | collective-permute-done | bytes 589856 | tf_op jit(solution)/shard_map/ppermute | solution.py:73
  459.8 7.9 %collective-permute-done.63 = bf16[8,96,1536]{2,1,0:T(8,128)(2,1)S(1)} collective-permute-done((bf16[8,96,1536]{2,1,0:T(8,128)(2,1)}, bf16[8,96,1536]{2,1,0:T(8,128)(2,1)S(1)}, u32[]{:S(2)}, u32[]{:S(2)}) %collective-permute-start.63) | collective-permute-done | bytes 2359328 | tf_op jit(solution)/shard_map/ppermute | solution.py:73
  509.7 12.0 %collective-permute-done.71 = bf16[1,96,1536]{2,1,0:T(8,128)(2,1)S(1)} collective-permute-done((bf16[1,96,1536]{2,1,0:T(8,128)(2,1)}, bf16[1,96,1536]{2,1,0:T(8,128)(2,1)S(1)}, u32[]{:S(2)}, u32[]{:S(2)}) %collective-permute-start.71) | collective-permute-done | bytes 294944 | tf_op jit(solution)/shard_map/ppermute | solution.py:73
  (396 shorter events, 276.7 us)
Async XLA Ops:
  38.5 15.7 %collective-permute-start.9 = (bf16[2,96,1536]{2,1,0:T(8,128)(2,1)S(1)}, bf16[2,96,1536]{2,1,0:T(8,128)(2,1)S(1)}, u32[]{:S(2)}, u32[]{:S(2)}) collective-permute-start(bf16[2,96,1536]{2,1,0:T(8,128)(2,1)S(1)} %pad_maximum_fusion.3), channel_id=1, source_target_pairs={{0,8},{1,9},{2,10},{3,11},{4,12},{5,13},{6,14},{7,15},{8,0},{9,1},... | collective-permute-start | bytes 1769480 | tf_op jit(solution)/shard_map/ppermute | solution.py:73
  55.4 32.2 %collective-permute-start.12 = (bf16[4,96,1536]{2,1,0:T(8,128)(2,1)}, bf16[4,96,1536]{2,1,0:T(8,128)(2,1)}, u32[]{:S(2)}, u32[]{:S(2)}) collective-permute-start(bf16[4,96,1536]{2,1,0:T(8,128)(2,1)} %pad_maximum_fusion.refs_0_.refs_7_), channel_id=1, source_target_pairs={{0,4},{1,3},{2,6},{3,1},{4,0},{5,7},{6,2},{7,5},{8,12},{9,11},{10,... | collective-permute-start | bytes 3538952 | tf_op jit(solution)/shard_map/ppermute | solution.py:73
  56.9 30.7 %collective-permute-start.13 = (bf16[4,96,1536]{2,1,0:T(8,128)(2,1)}, bf16[4,96,1536]{2,1,0:T(8,128)(2,1)}, u32[]{:S(2)}, u32[]{:S(2)}) collective-permute-start(bf16[4,96,1536]{2,1,0:T(8,128)(2,1)} %pad_maximum_fusion.refs_0_.refs_7_), channel_id=1, source_target_pairs={{0,2},{1,5},{2,0},{3,7},{4,6},{5,1},{6,4},{7,3},{8,10},{9,13},{10,... | collective-permute-start | bytes 3538952 | tf_op jit(solution)/shard_map/ppermute | solution.py:73
  71.1 15.3 %collective-permute-start.14 = (bf16[1,96,1536]{2,1,0:T(8,128)(2,1)}, bf16[1,96,1536]{2,1,0:T(8,128)(2,1)}, u32[]{:S(2)}, u32[]{:S(2)}) collective-permute-start(bf16[1,96,1536]{2,1,0:T(8,128)(2,1)} %bitcast.21), channel_id=1, source_target_pairs={{0,16},{1,17},{2,18},{3,19},{4,20},{5,21},{6,22},{7,23},{8,24},{9,... | collective-permute-start | bytes 884744 | tf_op jit(solution)/shard_map/ppermute | solution.py:73
  87.6 16.9 %collective-permute-start.15 = (bf16[4,96,1536]{2,1,0:T(8,128)(2,1)}, bf16[4,96,1536]{2,1,0:T(8,128)(2,1)}, u32[]{:S(2)}, u32[]{:S(2)}) collective-permute-start(bf16[4,96,1536]{2,1,0:T(8,128)(2,1)} %collective-permute-done.12.refs_1_.refs_8_), channel_id=1, source_target_pairs={{0,2},{1,5},{2,0},{3,7},{4,6},{5,1},{6,4},{7,3},{8,10},{9,13},{10,... | collective-permute-start | bytes 3538952 | tf_op jit(solution)/shard_map/ppermute | solution.py:73
  90.9 26.8 %collective-permute-start.16 = (bf16[4,96,1536]{2,1,0:T(8,128)(2,1)}, bf16[4,96,1536]{2,1,0:T(8,128)(2,1)}, u32[]{:S(2)}, u32[]{:S(2)}) collective-permute-start(bf16[4,96,1536]{2,1,0:T(8,128)(2,1)} %pad_maximum_fusion.refs_0_.refs_7_), channel_id=1, source_target_pairs={{0,1},{1,0},{2,3},{3,2},{4,5},{5,4},{6,7},{7,6},{8,9},{9,8},{10,11... | collective-permute-start | bytes 3538952 | tf_op jit(solution)/shard_map/ppermute | solution.py:73
  110.3 31.8 %collective-permute-start.24 = (bf16[4,96,1536]{2,1,0:T(8,128)(2,1)S(1)}, bf16[4,96,1536]{2,1,0:T(8,128)(2,1)S(1)}, u32[]{:S(2)}, u32[]{:S(2)}) collective-permute-start(bf16[4,96,1536]{2,1,0:T(8,128)(2,1)S(1)} %pad_maximum_fusion.1.refs_4_.refs_0_), channel_id=1, source_target_pairs={{0,4},{1,3},{2,6},{3,1},{4,0},{5,7},{6,2},{7,5},{8,12},{9,11},{10,... | collective-permute-start | bytes 3538952 | tf_op jit(solution)/shard_map/ppermute | solution.py:73
  111.8 57.1 %all-to-all-start = ((bf16[8,192,384]{2,1,0:T(8,128)(2,1)}), bf16[8,192,384]{2,1,0:T(8,128)(2,1)}, u32[]{:S(2)}, u32[]{:S(2)}) async-start(bf16[8,192,384]{2,1,0:T(8,128)(2,1)} %pad_maximum_fusion.2), calls=%async_computation | async-start | bytes 2359296 | tf_op jit(solution)/shard_map/all_to_all | solution.py:912
  117.7 24.4 %collective-permute-start.25 = (bf16[4,96,1536]{2,1,0:T(8,128)(2,1)S(1)}, bf16[4,96,1536]{2,1,0:T(8,128)(2,1)}, u32[]{:S(2)}, u32[]{:S(2)}) collective-permute-start(bf16[4,96,1536]{2,1,0:T(8,128)(2,1)S(1)} %pad_maximum_fusion.1.refs_4_.refs_0_), channel_id=1, source_target_pairs={{0,2},{1,5},{2,0},{3,7},{4,6},{5,1},{6,4},{7,3},{8,10},{9,13},{10,... | collective-permute-start | bytes 3538952 | tf_op jit(solution)/shard_map/ppermute | solution.py:73
  142.1 16.3 %collective-permute-start.26 = (bf16[4,96,1536]{2,1,0:T(8,128)(2,1)S(1)}, bf16[4,96,1536]{2,1,0:T(8,128)(2,1)}, u32[]{:S(2)}, u32[]{:S(2)}) collective-permute-start(bf16[4,96,1536]{2,1,0:T(8,128)(2,1)S(1)} %collective-permute-done.24.refs_5_.refs_1_), channel_id=1, source_target_pairs={{0,2},{1,5},{2,0},{3,7},{4,6},{5,1},{6,4},{7,3},{8,10},{9,13},{10,... | collective-permute-start | bytes 3538952 | tf_op jit(solution)/shard_map/ppermute | solution.py:73
  142.7 26.2 %collective-permute-start.27 = (bf16[4,96,1536]{2,1,0:T(8,128)(2,1)S(1)}, bf16[4,96,1536]{2,1,0:T(8,128)(2,1)}, u32[]{:S(2)}, u32[]{:S(2)}) collective-permute-start(bf16[4,96,1536]{2,1,0:T(8,128)(2,1)S(1)} %pad_maximum_fusion.1.refs_4_.refs_0_), channel_id=1, source_target_pairs={{0,1},{1,0},{2,3},{3,2},{4,5},{5,4},{6,7},{7,6},{8,9},{9,8},{10,11... | collective-permute-start | bytes 3538952 | tf_op jit(solution)/shard_map/ppermute | solution.py:73
  153.2 26.8 %collective-permute-start.28 = (bf16[4,96,1536]{2,1,0:T(8,128)(2,1)S(1)}, bf16[4,96,1536]{2,1,0:T(8,128)(2,1)}, u32[]{:S(2)}, u32[]{:S(2)}) collective-permute-start(bf16[4,96,1536]{2,1,0:T(8,128)(2,1)S(1)} %collective-permute-done.24.refs_5_.refs_1_), channel_id=1, source_target_pairs={{0,1},{1,0},{2,3},{3,2},{4,5},{5,4},{6,7},{7,6},{8,9},{9,8},{10,11... | collective-permute-start | bytes 3538952 | tf_op jit(solution)/shard_map/ppermute | solution.py:73
  153.2 26.8 %collective-permute-start.29 = (bf16[4,96,1536]{2,1,0:T(8,128)(2,1)}, bf16[4,96,1536]{2,1,0:T(8,128)(2,1)}, u32[]{:S(2)}, u32[]{:S(2)}) collective-permute-start(bf16[4,96,1536]{2,1,0:T(8,128)(2,1)} %collective-permute-done.25.refs_6_.refs_2_), channel_id=1, source_target_pairs={{0,1},{1,0},{2,3},{3,2},{4,5},{5,4},{6,7},{7,6},{8,9},{9,8},{10,11... | collective-permute-start | bytes 3538952 | tf_op jit(solution)/shard_map/ppermute | solution.py:73
  158.4 21.6 %collective-permute-start.30 = (bf16[4,96,1536]{2,1,0:T(8,128)(2,1)}, bf16[4,96,1536]{2,1,0:T(8,128)(2,1)}, u32[]{:S(2)}, u32[]{:S(2)}) collective-permute-start(bf16[4,96,1536]{2,1,0:T(8,128)(2,1)} %collective-permute-done.26.refs_7_.refs_3_), channel_id=1, source_target_pairs={{0,1},{1,0},{2,3},{3,2},{4,5},{5,4},{6,7},{7,6},{8,9},{9,8},{10,11... | collective-permute-start | bytes 3538952 | tf_op jit(solution)/shard_map/ppermute | solution.py:73
  247.4 22.0 %collective-permute-start.40 = (bf16[8,48,1536]{2,1,0:T(8,128)(2,1)}, bf16[8,48,1536]{2,1,0:T(8,128)(2,1)S(1)}, u32[]{:S(2)}, u32[]{:S(2)}) collective-permute-start(bf16[8,48,1536]{2,1,0:T(8,128)(2,1)} %get-tuple-element.242), channel_id=1, source_target_pairs={{0,1},{1,0},{2,3},{3,2},{4,5},{5,4},{6,7},{7,6},{8,9},{9,8},{10,11... | collective-permute-start | bytes 3538952 | tf_op jit(solution)/shard_map/ppermute | solution.py:73
  258.9 16.3 %collective-permute-start.42 = (bf16[8,48,1536]{2,1,0:T(8,128)(2,1)S(1)}, bf16[8,48,1536]{2,1,0:T(8,128)(2,1)S(1)}, u32[]{:S(2)}, u32[]{:S(2)}) collective-permute-start(bf16[8,48,1536]{2,1,0:T(8,128)(2,1)S(1)} %add_convert_fusion.4), channel_id=1, source_target_pairs={{0,2},{1,5},{2,0},{3,7},{4,6},{5,1},{6,4},{7,3},{8,10},{9,13},{10,... | collective-permute-start | bytes 3538952 | tf_op jit(solution)/shard_map/ppermute | solution.py:73
  338.9 30.2 %collective-permute-start.49 = (bf16[8,96,1536]{2,1,0:T(8,128)(2,1)}, bf16[8,96,1536]{2,1,0:T(8,128)(2,1)}, u32[]{:S(2)}, u32[]{:S(2)}) collective-permute-start(bf16[8,96,1536]{2,1,0:T(8,128)(2,1)} %get-tuple-element.240), channel_id=1, source_target_pairs={{0,1},{1,0},{2,3},{3,2},{4,5},{5,4},{6,7},{7,6},{8,9},{9,8},{10,11... | collective-permute-start | bytes 7077896 | tf_op jit(solution)/shard_map/ppermute | solution.py:73
  339.1 30.0 %collective-permute-start.50 = (bf16[8,96,1536]{2,1,0:T(8,128)(2,1)}, bf16[8,96,1536]{2,1,0:T(8,128)(2,1)}, u32[]{:S(2)}, u32[]{:S(2)}) collective-permute-start(bf16[8,96,1536]{2,1,0:T(8,128)(2,1)} %get-tuple-element.241), channel_id=1, source_target_pairs={{0,1},{1,0},{2,3},{3,2},{4,5},{5,4},{6,7},{7,6},{8,9},{9,8},{10,11... | collective-permute-start | bytes 7077896 | tf_op jit(solution)/shard_map/ppermute | solution.py:73
  339.4 35.0 %all-to-all-start.1 = ((bf16[8,192,384]{2,1,0:T(8,128)(2,1)}), bf16[8,192,384]{2,1,0:T(8,128)(2,1)S(1)}, u32[]{:S(2)}, u32[]{:S(2)}) async-start(bf16[8,192,384]{2,1,0:T(8,128)(2,1)} %pack_back.1), calls=%async_computation.1 | async-start | bytes 2359296 | tf_op jit(solution)/shard_map/all_to_all | solution.py:950
  374.4 32.6 %collective-permute-start.51 = (bf16[8,96,1536]{2,1,0:T(8,128)(2,1)}, bf16[8,96,1536]{2,1,0:T(8,128)(2,1)}, u32[]{:S(2)}, u32[]{:S(2)}) collective-permute-start(bf16[8,96,1536]{2,1,0:T(8,128)(2,1)} %add_convert_fusion.1), channel_id=1, source_target_pairs={{0,2},{1,5},{2,0},{3,7},{4,6},{5,1},{6,4},{7,3},{8,10},{9,13},{10,... | collective-permute-start | bytes 7077896 | tf_op jit(solution)/shard_map/ppermute | solution.py:73
  410.2 28.4 %collective-permute-start.52 = (bf16[4,96,1536]{2,1,0:T(8,128)(2,1)S(1)}, bf16[4,96,1536]{2,1,0:T(8,128)(2,1)S(1)}, u32[]{:S(2)}, u32[]{:S(2)}) collective-permute-start(bf16[4,96,1536]{2,1,0:T(8,128)(2,1)S(1)} %add_convert_fusion.3), channel_id=1, source_target_pairs={{0,4},{1,3},{2,6},{3,1},{4,0},{5,7},{6,2},{7,5},{8,12},{9,11},{10,... | collective-permute-start | bytes 3538952 | tf_op jit(solution)/shard_map/ppermute | solution.py:73
  438.6 29.1 %collective-permute-start.63 = (bf16[8,96,1536]{2,1,0:T(8,128)(2,1)}, bf16[8,96,1536]{2,1,0:T(8,128)(2,1)S(1)}, u32[]{:S(2)}, u32[]{:S(2)}) collective-permute-start(bf16[8,96,1536]{2,1,0:T(8,128)(2,1)} %add_convert_fusion), channel_id=1, source_target_pairs={{0,2},{1,5},{2,0},{3,7},{4,6},{5,1},{6,4},{7,3},{8,10},{9,13},{10,... | collective-permute-start | bytes 7077896 | tf_op jit(solution)/shard_map/ppermute | solution.py:73
  457.4 18.6 %collective-permute-start.61 = (bf16[1,96,1536]{2,1,0:T(8,128)(2,1)S(1)}, bf16[1,96,1536]{2,1,0:T(8,128)(2,1)S(1)}, u32[]{:S(2)}, u32[]{:S(2)}) collective-permute-start(bf16[1,96,1536]{2,1,0:T(8,128)(2,1)S(1)} %add_convert_fusion.9), channel_id=1, source_target_pairs={{0,16},{1,17},{2,18},{3,19},{4,20},{5,21},{6,22},{7,23},{8,24},{9,... | collective-permute-start | bytes 884744 | tf_op jit(solution)/shard_map/ppermute | solution.py:73
  470.7 16.8 %collective-permute-start.69 = (bf16[4,96,1536]{2,1,0:T(8,128)(2,1)S(1)}, bf16[4,96,1536]{2,1,0:T(8,128)(2,1)S(1)}, u32[]{:S(2)}, u32[]{:S(2)}) collective-permute-start(bf16[4,96,1536]{2,1,0:T(8,128)(2,1)S(1)} %add_convert_fusion.2), channel_id=1, source_target_pairs={{0,4},{1,3},{2,6},{3,1},{4,0},{5,7},{6,2},{7,5},{8,12},{9,11},{10,... | collective-permute-start | bytes 3538952 | tf_op jit(solution)/shard_map/ppermute | solution.py:73
  (113 other events, 1301.4 us)

commit v3 on v2

--- a/solution.py
+++ b/solution.py
@@ -154,12 +154,11 @@
 
 
 class Scatter:
-    def __init__(self, grid, send, *others):
+    def __init__(self, grid, low, high, *others):
         self.grid = grid
-        self.size = send.shape[0]
-        half = self.size // 2
-        send = after(send, others)
-        self.high, self.arrays = [grid.to_core(send[half:])], [grid.to_core(send[:half])]
+        self.size = 2 * low.shape[0]
+        low, high = after((low, high), others)
+        self.high, self.arrays = [grid.to_core(high)], [grid.to_core(low)]
 
     def keep(self, keep):
         half = self.size // 2
@@ -172,20 +171,21 @@
             arrays, lo, hi = self.high, 0, hi - lo
         return sum(p[lo:hi].astype(F32) for p in arrays)
 
-    def step(self, send, size, *others):
-        for k in reversed(self.grid.strides(size)):
+    def step(self, send, strides, *others):
+        for k in strides:
             half = self.size // 2
             self.arrays.append(send(after(self.sum(half, self.size).astype(BF), others), k))
             self.size = half
 
     def to_b(self, *others):
-        self.step(self.grid.to_b, self.grid.side, *others)
+        self.step(self.grid.to_b, self.grid.strides(self.grid.side)[::-1], *others)
 
     def to_a(self, *others):
-        self.step(self.grid.to_a, self.grid.side, *others)
-
-    def to_z(self, *others):
-        self.step(self.grid.to_z, self.grid.depth, *others)
+        self.step(self.grid.to_a, self.grid.strides(self.grid.side)[::-1], *others)
+
+    def to_z(self, *others, first=True, rest=True):
+        strides = self.grid.strides(self.grid.depth)[::-1]
+        self.step(self.grid.to_z, (strides[:1] if first else []) + (strides[1:] if rest else []), *others)
 
     def last(self):
         return self.arrays[-1]
@@ -209,17 +209,16 @@
     return copies
 
 
-def place_copy(place_ref, block, source_ref, keep_ref, send_ref, sem_ref):
-    half = keep_ref.shape[0]
+def place_copy(place_ref, block, source_ref, target_refs, sem_ref):
     place = place_ref[block]
-
-    @pl.when(place < half)
-    def _():
-        pltpu.make_async_copy(source_ref, keep_ref.at[place], sem_ref).start()
-
-    @pl.when(place >= half)
-    def _():
-        pltpu.make_async_copy(source_ref, send_ref.at[place - half], sem_ref).start()
+    first = 0
+    for target in target_refs:
+        index, size = place - first, target.shape[0]
+        first += size
+
+        @pl.when((index >= 0) & (index < size))
+        def _():
+            pltpu.make_async_copy(source_ref, target.at[index], sem_ref).start()
 
 
 def dot(a, b):
@@ -325,7 +324,7 @@
             pltpu.SemaphoreType.DMA((2 * heads,)),
         ],
         compiler_params=params(56),
-        cost_estimate=cost(15e9, 25e6),
+        cost_estimate=cost(2e9, 2e6),
         name="attend",
     )(order, valid, query_t, hidden_media, hidden_own, *parts)
 
@@ -443,36 +442,35 @@
 
 
 def output_part_kernel(groups, place_ref, context_ref, low_ref, *refs):
-    keep_ref, send_ref, out_ref, sem_ref = refs[-4:]
+    *targets, out_ref, sem_ref = refs[-5:]
     low = low_ref[...]
     per = out_ref.shape[0] // groups
     part = context_ref.shape[1] // groups
     rows = out_ref.shape[1]
-    last = pl.ds(keep_ref.shape[1] - rows, rows)
-    keep_rows, send_rows = keep_ref.at[:, last], send_ref.at[:, last]
+    targets = [t.at[:, pl.ds(t.shape[1] - rows, rows)] for t in targets]
     for g in range(groups):
         value = mm_tn(context_ref[:, g * part : (g + 1) * part], low).astype(BF)
         out_ref[g * per : (g + 1) * per] = value.reshape((per,) + out_ref.shape[1:])
         for i in range(g * per, (g + 1) * per):
-            place_copy(place_ref, i, out_ref.at[i], keep_rows, send_rows, sem_ref.at[i])
+            place_copy(place_ref, i, out_ref.at[i], targets, sem_ref.at[i])
     for i in range(out_ref.shape[0]):
-        pltpu.make_async_copy(out_ref.at[i], keep_rows.at[0], sem_ref.at[i]).wait()
+        pltpu.make_async_copy(out_ref.at[i], targets[0].at[0], sem_ref.at[i]).wait()
 
 
 def output_part_of(place, context, low, *halves):
     width = low.shape[1]
     count = place.shape[0]
     block = context.shape[1] // count
-    shapes = [h.shape for h in halves] or [(count // 2, block, width)] * 2
+    shapes = [h.shape for h in halves] or [(n, block, width) for n in (count // 2, count // 4, count // 4)]
     return pl.pallas_call(
         functools.partial(output_part_kernel, 4),
         in_specs=[SMEM, whole(context.shape), whole(low.shape)] + [ANYWHERE] * len(halves),
-        out_specs=[ANYWHERE, ANYWHERE],
+        out_specs=[ANYWHERE] * 3,
         out_shape=[jax.ShapeDtypeStruct(shape, BF) for shape in shapes],
-        input_output_aliases={3: 0, 4: 1} if halves else {},
+        input_output_aliases={3: 0, 4: 1, 5: 2} if halves else {},
         scratch_shapes=[pltpu.VMEM((count, block, width), BF), pltpu.SemaphoreType.DMA((count,))],
         compiler_params=params(32),
-        cost_estimate=cost(2e9, 8e6),
+        cost_estimate=cost(1e9, 2e6),
         name="output_part",
     )(place, context, low, *halves)
 
@@ -567,7 +565,9 @@
 
 def feed_kernel(part_count, up_ref, down_ref, *refs):
     feed, grad = refs[:part_count], refs[part_count : 2 * part_count]
-    act_ref, grad_up_ref, out_ref, feed_st, grad_st, out_st, feed_sem, grad_sem, out_sem = refs[2 * part_count :]
+    act_ref, grad_up_ref, *out_refs = refs[2 * part_count : -6]
+    feed_st, grad_st, out_st, feed_sem, grad_sem, out_sem = refs[-6:]
+    each = part_count // len(out_refs)
     n, per, width = feed[0].shape
     chunk = n * per
     feeds, grads = loads(feed, per, feed_st, feed_sem), loads(grad, per, grad_st, grad_sem)
@@ -576,11 +576,12 @@
         start(grads[i])
     up, down = up_ref[...], down_ref[...]
     outs = []
-    for i in range(part_count):
+    each, n, chunk = each // 2, 2 * n, 2 * chunk
+    for i in range(part_count // 2):
         at = slice(i * n, (i + 1) * n)
-        wait(feeds[i])
+        wait(feeds[2 * i] + feeds[2 * i + 1])
         pre = mm_nt(feed_st[at].reshape(chunk, width), up)
-        wait(grads[i])
+        wait(grads[2 * i] + grads[2 * i + 1])
         grad_act = mm_nt(grad_st[at].reshape(chunk, width), down)
         cdf = 0.5 * (1.0 + lax.erf(pre * ROOT_HALF))
         slope = cdf + pre * (jnp.exp(-0.5 * pre * pre) * DENSITY)
@@ -588,12 +589,13 @@
         grad_up = (grad_act * slope).astype(BF)
         grad_up_ref[i * chunk : (i + 1) * chunk, :] = grad_up
         out_st[at] = dot(grad_up, up).astype(BF).reshape(n, per, width)
-        outs.append(pltpu.make_async_copy(out_st.at[pl.ds(i * n, n)], out_ref.at[pl.ds(i * n, n)], out_sem.at[i]))
+        to = out_refs[i // each].at[pl.ds(i % each * n, n)]
+        outs.append(pltpu.make_async_copy(out_st.at[pl.ds(i * n, n)], to, out_sem.at[i]))
         outs[i].start()
     wait(outs)
 
 
-def feed(up, down, feed_parts, grad_parts):
+def feed(up, down, feed_parts, grad_parts, splits):
     hid, width = up.shape
     count = len(feed_parts)
     n, per, _ = feed_parts[0].shape
@@ -603,8 +605,9 @@
     return pl.pallas_call(
         functools.partial(feed_kernel, count),
         in_specs=[whole(up.shape), whole(down.shape)] + [ANYWHERE] * (2 * count),
-        out_specs=[whole((rows, hid))] * 2 + [ANYWHERE],
-        out_shape=[jax.ShapeDtypeStruct((rows, hid), BF)] * 2 + [jax.ShapeDtypeStruct((count * n, per, width), BF)],
+        out_specs=[whole((rows, hid))] * 2 + [ANYWHERE] * splits,
+        out_shape=[jax.ShapeDtypeStruct((rows, hid), BF)] * 2
+        + [jax.ShapeDtypeStruct((count * n // splits, per, width), BF)] * splits,
         scratch_shapes=[store] * 3 + [sems] * 3,
         compiler_params=params(48),
         cost_estimate=cost(5e9, 8e6),
@@ -614,7 +617,9 @@
 
 def feed_rest_kernel(part_count, down_ref, act_ref, grad_up_ref, *refs):
     feed, grad = refs[:part_count], refs[part_count : 2 * part_count]
-    up_grad_ref, down_grad_ref, out_ref, feed_st, grad_st, out_st, feed_sem, grad_sem, out_sem = refs[2 * part_count :]
+    up_grad_ref, down_grad_ref, *out_refs = refs[2 * part_count : -6]
+    feed_st, grad_st, out_st, feed_sem, grad_sem, out_sem = refs[-6:]
+    each = part_count // len(out_refs)
     n, per, width = feed[0].shape
     chunk = n * per
     feeds, grads = loads(feed, per, feed_st, feed_sem), loads(grad, per, grad_st, grad_sem)
@@ -628,7 +633,8 @@
         at = slice(i * n, (i + 1) * n)
         act = act_ref[i * chunk : (i + 1) * chunk, :]
         out_st[at] = dot(act, down).astype(BF).reshape(n, per, width)
-        outs.append(pltpu.make_async_copy(out_st.at[pl.ds(i * n, n)], out_ref.at[pl.ds(i * n, n), first], out_sem.at[i]))
+        to = out_refs[i // each].at[pl.ds(i % each * n, n), first]
+        outs.append(pltpu.make_async_copy(out_st.at[pl.ds(i * n, n)], to, out_sem.at[i]))
         outs[i].start()
     for i in range(part_count):
         wait(feeds[i])
@@ -638,7 +644,7 @@
     wait(outs)
 
 
-def feed_rest(down, act, grad_up, feed_parts, grad_parts, spare):
+def feed_rest(down, act, grad_up, feed_parts, grad_parts, spare, splits):
     hid, width = down.shape
     count = len(feed_parts)
     n, per, _ = feed_parts[0].shape
@@ -647,9 +653,9 @@
     return pl.pallas_call(
         functools.partial(feed_rest_kernel, count),
         in_specs=[whole(down.shape), whole(act.shape), whole(grad_up.shape)] + [ANYWHERE] * (2 * count),
-        out_specs=[whole((hid, width))] * 2 + [ANYWHERE],
+        out_specs=[whole((hid, width))] * 2 + [ANYWHERE] * splits,
         out_shape=[jax.ShapeDtypeStruct((hid, width), F32)] * 2
-        + [jax.ShapeDtypeStruct((count * n, per + spare, width), BF)],
+        + [jax.ShapeDtypeStruct((count * n // splits, per + spare, width), BF)] * splits,
         scratch_shapes=[store] * 3 + [sems] * 3,
         compiler_params=params(48),
         cost_estimate=cost(5e9, 8e6),
@@ -665,7 +671,8 @@
     refs = refs[piece_count + 3 + part_count :]
     (
         keep_ref,
-        send_ref,
+        low_ref,
+        high_ref,
         query_part_ref,
         grad_media_ref,
         grad_own_ref,
@@ -677,7 +684,7 @@
         key_mix_ref,
         sem_ref,
         out_sem_ref,
-    ) = refs[-13:]
+    ) = refs[-14:]
     step = pl.program_id(0)
     head_dim = weight_ref.shape[1]
     own_rows = own_ref.shape[0]
@@ -757,11 +764,13 @@
         out_ref[2 * j + 1] = mm_tn(grad_ref[j, :, :head_dim], mix_ref[j]).astype(BF)
         for i in range(2):
             slot = 2 * j + i
-            place_copy(place_ref, first + h + i * heads, out_ref.at[slot], keep_ref, send_ref, out_sem_ref.at[slot])
+            place_copy(
+                place_ref, first + h + i * heads, out_ref.at[slot], (keep_ref, low_ref, high_ref), out_sem_ref.at[slot]
+            )
     pl.when(step == pl.num_programs(0) - 1)(out_wait)
 
 
-def attend_back(order, place, slot, query_t, hidden_media, hidden_own, pieces, folded, scores, own_scores, parts, factor, first, count, *halves):
+def attend_back(order, place, slot, query_t, hidden_media, hidden_own, pieces, folded, scores, own_scores, parts, factor, first, count, work, *halves):
     heads, head_dim, lat = query_t.shape
     seqs, patches, width = hidden_media.shape
     group = 4
@@ -784,13 +793,15 @@
         out_specs=[
             ANYWHERE,
             ANYWHERE,
+            ANYWHERE,
             whole((2 * heads, head_dim // 2, lat)),
             whole(hidden_media.shape),
             whole(hidden_own.shape),
         ],
         out_shape=[
             jax.ShapeDtypeStruct((heads, head_dim, width), BF),
-            jax.ShapeDtypeStruct((heads, head_dim, width), BF),
+            jax.ShapeDtypeStruct((heads // 2, head_dim, width), BF),
+            jax.ShapeDtypeStruct((heads // 2, head_dim, width), BF),
             jax.ShapeDtypeStruct((2 * heads, head_dim // 2, lat), BF),
             jax.ShapeDtypeStruct(hidden_media.shape, F32),
             jax.ShapeDtypeStruct(hidden_own.shape, F32),
@@ -805,9 +816,9 @@
             pltpu.SemaphoreType.DMA((2 * heads,)),
             pltpu.SemaphoreType.DMA((2 * group,)),
         ],
-        input_output_aliases={position: 0, position + 1: 1} if halves else {},
+        input_output_aliases={position: 0, position + 1: 1, position + 2: 2} if halves else {},
         compiler_params=params(60),
-        cost_estimate=cost(12e9, 20e6),
+        cost_estimate=cost(work, 20e6),
         name="attend_back",
     )(order, place, slot, query_t, hidden_media, hidden_own, *pieces, folded, scores, own_scores, *parts, *halves)
 
@@ -847,12 +858,13 @@
     else:
         order = place = jnp.arange(2 * HEADS, dtype=jnp.int32)
 
-    def scatter_order(keep, send):
+    quarters = (grid.count // 2, grid.count // 2 + grid.count // 4)
+
+    def scatter_order(parts):
         if aligned:
-            return keep, send
-        v = jnp.concatenate([keep, send]).reshape(grid.count, -1, keep.shape[-1])
-        v = v.at[owners].get(mode="promise_in_bounds")
-        return v[: grid.count // 2], v[grid.count // 2 :]
+            return parts
+        v = jnp.concatenate(parts).reshape(grid.count, -1, parts[0].shape[-1])
+        return jnp.split(v.at[owners].get(mode="promise_in_bounds"), quarters)
 
     def aligned_parts(parts):
         if aligned:
@@ -867,10 +879,10 @@
     small = grid.gather(packed.T[None], "z")
     first, *rest = grid.strides(grid.depth)
     keyval_z = grid.step(after(keyval_weight.T, small)[None], "z", first)
-    small = after(small, keyval_z)
+    small = grid.gather(after(small, keyval_z), "ab")
     for k in rest:
         keyval_z = grid.step(keyval_z, "z", k)
-    small = grid.gather(small, "abc").at[places].get(mode="promise_in_bounds")
+    small = grid.gather(after(small, keyval_z), "c").at[places].get(mode="promise_in_bounds")
     small = small.reshape(width, -1).T.astype(F32)
     lat_float = small[:lat_rows]
     table_all = small[lat_rows : lat_rows + times]
@@ -895,34 +907,36 @@
     lat_own = lax.dynamic_slice_in_dim(lat_float, first_row, own_rows, 0)
     query_own = mm_tn(query_weight, hidden_lat.T).astype(BF)
     frame_ids = jnp.arange(grid.frame, dtype=jnp.int32) ^ slot
-    query_t = after(grid.gather(query_own[None], "cab"), keyval_z)
-    query_t = grid.gather(query_t, "z")
+    query_z = grid.gather(query_own[None], "cz")
     first, *rest = grid.strides(grid.depth)
-    mixed_first = grid.step(after(jnp.concatenate([output_weight, grad_out.astype(BF)]), query_t)[None], "z", first)
+    mixed_first = grid.step(after(jnp.concatenate([output_weight, grad_out.astype(BF)]), query_z)[None], "z", first)
     mixed_z = mixed_first
     for k in rest:
         mixed_z = grid.step(mixed_z, "z", k)
-    query_t = query_t.reshape(grid.count, part, grid.frame, own_rows)
-    query_places = grid.places("cabz")
+    query_all = grid.gather(query_z, "ab")
+    query_t = query_all.reshape(grid.count, part, grid.frame, own_rows)
+    query_places = grid.places("czab")
     query_t = query_t.at[query_places[:, None], :, frame_ids[None, :]].get(mode="promise_in_bounds")
     query_t = query_t.transpose(0, 2, 1, 3).reshape(HEADS, head_dim, lat_rows)
-    keyval_ab = grid.gather_ab(keyval_z, query_t, mixed_first)
-    keyval_parts = aligned_parts(grid.gather_core(keyval_ab, mixed_z))
+    keyval_ab = grid.gather_ab(keyval_z)
+    early = (mixed_z, hidden_media, hidden_own, query_t, feed_got)
+    keyval_parts = aligned_parts(grid.gather_core(keyval_ab, *early))
     mixed_z = after(mixed_z, keyval_ab)
-    feed_got = lax.all_to_all(after(feed_got, mixed_z), "seq", 0, 0)
     folded, media_scores, own_scores, context_parts = attend(
         order, is_valid, query_t, hidden_media, hidden_own, keyval_parts, factor
     )
     context_parts = context_parts.reshape(HEADS, seq_here, grid.frame, own_rows, LANES)
     pieces = [context_parts[:, :, k].reshape(HEADS, rows, LANES).astype(BF) for k in range(grid.frame)]
-    pieces = after(pieces, feed_got)
     pieces = [pieces[0]] + [grid.to_frame(pieces[k], k) for k in range(1, grid.frame)]
-    mixed_parts = grid.gather_core(grid.gather_ab(mixed_z, folded))
+    feed_got = lax.all_to_all(after(feed_got, folded), "seq", 0, 0)
+    mixed_ab = grid.gather_ab(mixed_z, folded)
+    mixed_parts = grid.gather_core(mixed_ab, pieces)
     if aligned:
         output_parts, grad_parts = mixed_parts, mixed_parts
     else:
         output_parts = aligned_parts([p[:, :part] for p in mixed_parts])
         grad_parts = [p[:, part:] for p in mixed_parts]
+    pieces[0] = after(pieces[0], feed_got)
     mixed, normed_feed, hidden_feed, context, context_low = mixer(
         order, lat_own, feed_scale, pieces, output_parts, head_dim
     )
@@ -931,15 +945,15 @@
     feed_parts = grid.gather_core(grid.gather_ab(grid.gather(hidden_feed[None], "z"), up_t))
     half = len(feed_parts) // 2
     far, near = (feed_parts[half:], grad_parts[half:]), (feed_parts[:half], grad_parts[:half])
-    far_act, far_grad_up, send = feed(up_t, down_w, *far)
-    grad_sum = Scatter(grid, send)
-    near_act, near_grad_up, keep = feed(up_t, down_w, *after(near, send))
+    far_act, far_grad_up, low, high = feed(up_t, down_w, *far, 2)
+    grad_sum = Scatter(grid, low, high)
+    near_act, near_grad_up, keep = feed(up_t, down_w, *after(near, high), 1)
     grad_sum.keep(keep)
     grad_sum.to_b()
     spare = part if aligned else 0
-    far_up, far_down, send = feed_rest(down_w, far_act, after(far_grad_up, keep), *far, spare)
-    near_up, near_down, keep = feed_rest(down_w, near_act, after(near_grad_up, send), *near, spare)
-    grad_sum.to_a(send)
+    far_up, far_down, low, high = feed_rest(down_w, far_act, after(far_grad_up, keep), *far, spare, 2)
+    near_up, near_down, keep = feed_rest(down_w, near_act, after(near_grad_up, high), *near, spare, 1)
+    grad_sum.to_a(high)
     grad_sum.to_z(keep)
     back = pack_back(grid.seq, far_up, far_down, near_up, near_down)
     grad_feed = after(grad_sum.result(), back)
@@ -948,47 +962,52 @@
     )
     messages = [message] + [grid.to_frame(message, k) for k in range(1, grid.frame)]
     back = lax.all_to_all(after(back, message), "seq", 0, 0)
+    output_context = after(context_low, messages)
     if aligned:
-        keep, send = output_part_of(place, after(context_low, messages), grad_mixed_low, keep, send)
+        keep, low, high = output_part_of(place, output_context, grad_mixed_low, keep, low, high)
     else:
-        out_keep, out_send = scatter_order(*output_part_of(place, context_low, grad_mixed_low))
-        keep, send = jnp.concatenate([keep, out_keep], 1), jnp.concatenate([send, out_send], 1)
-    mixed_sum = Scatter(grid, send)
+        pairs = zip((keep, low, high), scatter_order(output_part_of(place, output_context, grad_mixed_low)))
+        keep, low, high = (jnp.concatenate(pair, 1) for pair in pairs)
+    mixed_sum = Scatter(grid, low, high)
     mixed_sum.keep(keep)
     messages = after(messages, keep)
 
-    def back_half(messages, first, *halves):
-        return attend_back(
+    def back_heads(first, count, work, *parts):
+        *parts, query_part, grad_media, grad_own = attend_back(
             order, place, slot.reshape(1), query_t, hidden_media, hidden_own, messages, folded, media_scores, own_scores,
-            keyval_parts, factor, first, HEADS // 2, *halves,
+            keyval_parts, factor, first, count, work, *parts,
         )
-
-    keep, send, query_near, grad_hidden_near, grad_own_near = back_half(messages, 0)
-    keep, send = after((keep, send), mixed_sum.arrays[0])
-    mixed_sum.to_b(send, back)
-    keep, send, query_far, grad_hidden_far, grad_own_far = back_half(messages, HEADS // 2, keep, send)
-    keep, send = scatter_order(keep, send)
-    keyval_sum = Scatter(grid, send)
-    keyval_sum.keep(keep)
-    half = grid.count // 2
-    query_part = query_near + query_far
+        return parts, (query_part, grad_media, grad_own)
+
+    quarter = HEADS // 4
+    parts, sums = back_heads(0, quarter, 2e9)
+    parts = after(parts, mixed_sum.high, mixed_sum.arrays)
+    mixed_sum.to_b(parts, back)
+    parts, more = back_heads(quarter, 2 * quarter, 40e9, *parts)
+    sums = [sums, more]
+    parts = after(parts, mixed_sum.last())
+    mixed_sum.to_a(parts)
+    parts, more = back_heads(3 * quarter, quarter, 30e9, *parts)
+    sums.append(more)
+    query_part = sums[0][0] + sums[1][0] + sums[2][0]
     if not aligned:
         query_part = query_part.reshape(grid.count, part, lat_rows).at[owners].get(mode="promise_in_bounds")
-    query_part = after(query_part, mixed_sum.last())
-    query_sum = Scatter(grid, query_part[half:])
-    query_sum.keep(query_part[:half])
-    mixed_sum.to_a(send)
+    query_keep, low, high = jnp.split(after(query_part, mixed_sum.last()), quarters)
+    query_sum = Scatter(grid, low, high)
+    query_sum.keep(query_keep)
+    keep, low, high = scatter_order(parts)
+    keyval_sum = Scatter(grid, low, high, query_sum.high)
+    keyval_sum.keep(keep)
     query_sum.to_b()
+    keyval_sum.to_b(query_sum.last())
     query_sum.to_a()
-    keyval_sum.to_b(query_sum.last(), mixed_sum.last())
     keyval_b = keyval_sum.last()
     query_sum.to_z(keyval_sum.arrays[0])
     query_sum = query_sum.result().T.astype(BF)
-    mixed_sum.to_z(query_sum)
-    grad_hidden_near = after(grad_hidden_near, keyval_sum.arrays[0])
+    mixed_sum.to_z(keyval_sum.high)
+    sums = after(sums, keyval_sum.high)
+    grad_hidden, grad_hidden_own = (sums[0][i] + sums[1][i] + sums[2][i] for i in (1, 2))
     back = after(back, keyval_b)
-    grad_hidden = grad_hidden_near + grad_hidden_far
-    grad_hidden_own = grad_own_near + grad_own_far
 
     media_gain_part = jnp.sum(grad_hidden * normed_media, (0, 1))
     grad_embedded = norm_back(grad_hidden * media_scale, normed_media, inv_media)
@@ -1012,10 +1031,10 @@
             jnp.zeros((pad, width), F32),
         ]
     ).astype(BF)
+    keyval_sum.to_a()
+    keyval_sum.to_z()
     smalls = smalls.T.reshape(grid.count, part, -1).at[grid.owners("cabz")].get(mode="promise_in_bounds")
     small_sum = grid.scatter_core_last(after(smalls, keyval_b)).T
-    keyval_sum.to_a()
-    keyval_sum.to_z()
     up_grad_t, down_grad = unpack_back(back)
     up_grad = up_grad_t.T
     keyval_grad = keyval_sum.result().T

time: 532 us -> 510 us (0.959)
  starting transfers between devices: 99.2 us -> 76.8 us
  waiting for transfers between devices: 180 us -> 174 us
    ppermute x72, waiting for transfers between devices: 179 us -> 156 us  [send(): return lax.ppermute(value, BOTH, perm)]
    ppermute x72, starting transfers between devices: 87.3 us -> 67.5 us  [send(): return lax.ppermute(value, BOTH, perm)]
    slice x5 -> x0, local copies, waits for them, and re-layouts: 10.8 us -> none  [the longest x3 5.69 us: __init__(): send[:half]]
    all_to_all x1, waiting for transfers between devices: 0.01 us -> 8.91 us  [local(): feed_got = lax.all_to_all(after(feed_got, folded), 'seq', 0, 0)]
    all_to_all x1, waiting for transfers between devices: 0.79 us -> 8.97 us  [local(): back = lax.all_to_all(after(back, message), 'seq', 0, 0)]
    pallas_call x2 -> x3, Pallas kernels: 47.6 us -> 54.6 us  [attend_back(): pl.pallas_call(functools.partial(attend_back_kernel, sizes), grid=(count...]
    unnamed x133 -> x165, local copies, waits for them, and re-layouts: 16.9 us -> 22.6 us
  transfers between devices with their start and end apart: 74 -> 74, of which waited for: 41 -> 40; matrix products, arithmetic and copies ran while one was open for 15% -> 15% of each run, Pallas kernels for 19% -> 22%
where the time goes in v3:
time: 510 us; the launch traced here: 502 us
  waiting for transfers between devices  174 us (34%)
  Pallas kernels  138 us (27%)
  starting transfers between devices  76.8 us (15%)
  other arithmetic  62.9 us (12%)
  local copies, waits for them, and re-layouts  44.6 us (9%)
    ppermute x72, waiting for transfers between devices, send(): return lax.ppermute(value, BOTH, perm)  156 us
    ppermute x72, starting transfers between devices, send(): return lax.ppermute(value, BOTH, perm)  67.5 us
    pallas_call x3, Pallas kernels, attend_back(): pl.pallas_call(functools.partial(attend_back_kernel, sizes), grid=(count...  54.6 us
    convert_element_type x16, other arithmetic, step(): self.sum(half, self.size).astype(BF)  27.3 us
    pallas_call x1, Pallas kernels, attend(): pl.pallas_call(functools.partial(attend_kernel, (heads, group, seqs, lat,...  22.7 us
    unnamed x165, local copies, waits for them, and re-layouts  22.6 us
    pallas_call x2, Pallas kernels, feed(): pl.pallas_call(functools.partial(feed_kernel, count), in_specs=[whole(up....  17.2 us
    pallas_call x2, Pallas kernels, feed_rest(): pl.pallas_call(functools.partial(feed_rest_kernel, count), in_specs=[whol...  13.2 us
  transfers between devices with their start and end apart: 74, of which 40 were waited for; matrix products, arithmetic and copies ran while one was open for 15% of the time, Pallas kernels for 22%

profile of v3, /device:TPU:0, one launch (start us, length us, event | category | flops | bytes accessed | tf_op | source)
XLA Modules:
  0.0 502.3 jit_solution(12251210102042445450)
XLA Ops:
  18.3 10.3 %collective-permute-done.2 = bf16[1,96,1536]{2,1,0:T(8,128)(2,1)S(1)} collective-permute-done((bf16[1,96,1536]{2,1,0:T(8,128)(2,1)}, bf16[1,96,1536]{2,1,0:T(8,128)(2,1)S(1)}, u32[]{:S(2)}, u32[]{:S(2)}) %collective-permute-start.2) | collective-permute-done | bytes 294944 | tf_op jit(solution)/shard_map/ppermute | solution.py:73
  77.5 6.7 %collective-permute-done.18 = bf16[1,96,1536]{2,1,0:T(8,128)(2,1)S(1)} collective-permute-done((bf16[1,96,1536]{2,1,0:T(8,128)(2,1)S(1)}, bf16[1,96,1536]{2,1,0:T(8,128)(2,1)S(1)}, u32[]{:S(2)}, u32[]{:S(2)}) %collective-permute-start.18) | collective-permute-done | bytes 294944 | tf_op jit(solution)/shard_map/ppermute | solution.py:73
  107.6 22.7 %attend.1 = (bf16[1024,1536]{1,0:T(8,128)(2,1)}, f32[3,1024,256]{2,1,0:T(8,128)}, f32[1024,16]{1,0:T(8,128)}, f32[16,192,128]{2,1,0:T(8,128)}) custom-call(s32[32]{0:T(128)} %scatter_custom_fusion.order_ref, s32[3]{0:T(128)} %compare_convert_fusion.9.valid_ref, bf16[16,96,64]{2,1,0:T(8,128)(2,1)} %copy.94.query_ref, bf16[3,256,1536]{2,1,0:T(8,128)(2,1)} %fusion.8.media_ref, ...), custom_call_target="tpu_custom_call" | custom-call | flops 2000000000 | bytes 2000000 | tf_op jit(solution)/shard_map/attend/pallas_call | solution.py:304
  140.4 12.5 %collective-permute-done.22.refs_2_ = bf16[16,48,128]{2,1,0:T(8,128)(2,1)S(1)} collective-permute-done((bf16[16,48,128]{2,1,0:T(8,128)(2,1)S(1)}, bf16[16,48,128]{2,1,0:T(8,128)(2,1)S(1)}, u32[]{:S(2)}, u32[]{:S(2)}) %collective-permute-start.22) | collective-permute-done | bytes 196640 | tf_op jit(solution)/shard_map/ppermute | solution.py:73
  156.4 8.9 %all-to-all-done.got_ref = bf16[8,192,384]{2,1,0:T(8,128)(2,1)} async-done(((bf16[8,192,384]{2,1,0:T(8,128)(2,1)}), bf16[8,192,384]{2,1,0:T(8,128)(2,1)}, u32[]{:S(2)}, u32[]{:S(2)}) %all-to-all-start) | async-done | bytes 1179680 | tf_op jit(solution)/shard_map/all_to_all | solution.py:931
  168.2 7.1 %mixer.1 = (f32[48,1536]{1,0:T(8,128)S(1)}, f32[48,1536]{1,0:T(8,128)S(1)}, bf16[48,1536]{1,0:T(8,128)(2,1)S(1)}, f32[16,48,128]{2,1,0:T(8,128)S(1)}, bf16[48,1536]{1,0:T(8,128)(2,1)S(1)}) custom-call(s32[32]{0:T(128)S(1)} %copy-done.24, f32[16,1536]{1,0:T(8,128)S(1)} %constant_dynamic-slice_fusion.1.latent_ref, f32[1,1536]{1,0:T(1,128)S(1)} %get-tuple-element.296.gain_ref, ...), custom_call_target="tpu_custom_call" | custom-call | flops 2000000000 | bytes 8000000 | tf_op jit(solution)/shard_map/mixer/pallas_call | solution.py:369
  175.4 9.0 %collective-permute-done.31 = bf16[1,48,1536]{2,1,0:T(8,128)(2,1)S(1)} collective-permute-done((bf16[1,48,1536]{2,1,0:T(8,128)(2,1)S(1)}, bf16[1,48,1536]{2,1,0:T(8,128)(2,1)S(1)}, u32[]{:S(2)}, u32[]{:S(2)}) %collective-permute-start.31) | collective-permute-done | bytes 147488 | tf_op jit(solution)/shard_map/ppermute | solution.py:73
  184.5 8.5 %collective-permute-done.32 = bf16[2,48,1536]{2,1,0:T(8,128)(2,1)S(1)} collective-permute-done((bf16[2,48,1536]{2,1,0:T(8,128)(2,1)S(1)}, bf16[2,48,1536]{2,1,0:T(8,128)(2,1)S(1)}, u32[]{:S(2)}, u32[]{:S(2)}) %collective-permute-start.32) | collective-permute-done | bytes 294944 | tf_op jit(solution)/shard_map/ppermute | solution.py:73
  197.8 9.9 %collective-permute-done.34.refs_1_ = bf16[4,48,1536]{2,1,0:T(8,128)(2,1)S(1)} collective-permute-done((bf16[4,48,1536]{2,1,0:T(8,128)(2,1)S(1)}, bf16[4,48,1536]{2,1,0:T(8,128)(2,1)S(1)}, u32[]{:S(2)}, u32[]{:S(2)}) %collective-permute-start.34) | collective-permute-done | bytes 589856 | tf_op jit(solution)/shard_map/ppermute | solution.py:73
  209.7 7.8 %collective-permute-done.38.refs_3_ = bf16[4,48,1536]{2,1,0:T(8,128)(2,1)S(1)} collective-permute-done((bf16[4,48,1536]{2,1,0:T(8,128)(2,1)S(1)}, bf16[4,48,1536]{2,1,0:T(8,128)(2,1)S(1)}, u32[]{:S(2)}, u32[]{:S(2)}) %collective-permute-start.38) | collective-permute-done | bytes 589856 | tf_op jit(solution)/shard_map/ppermute | solution.py:73
  221.6 8.7 %feed.2 = (bf16[768,192]{1,0:T(8,128)(2,1)S(1)}, bf16[768,192]{1,0:T(8,128)(2,1)S(1)}, bf16[8,48,1536]{2,1,0:T(8,128)(2,1)S(1)}, bf16[8,48,1536]{2,1,0:T(8,128)(2,1)}) custom-call(bf16[192,1536]{1,0:T(8,128)(2,1)S(1)} %copy-done.28, bf16[192,1536]{1,0:T(8,128)(2,1)S(1)} %copy-done.26, bf16[4,48,1536]{2,1,0:T(8,128)(2,1)S(1)} %collective-permute-done.33.refs_0_, ...), custom_call_target="tpu_custom_call" | custom-call | flops 5000000000 | bytes 8000000 | tf_op jit(solution)/shard_map/feed/pallas_call | solution.py:605
  230.9 8.5 %feed.3 = (bf16[768,192]{1,0:T(8,128)(2,1)S(1)}, bf16[768,192]{1,0:T(8,128)(2,1)S(1)}, bf16[16,48,1536]{2,1,0:T(8,128)(2,1)}) custom-call(bf16[192,1536]{1,0:T(8,128)(2,1)S(1)} %copy-done.28, bf16[192,1536]{1,0:T(8,128)(2,1)S(1)} %copy-done.26, bf16[4,48,1536]{2,1,0:T(8,128)(2,1)S(1)} %pad_maximum_fusion.5.refs_0_, ...), custom_call_target="tpu_custom_call" | custom-call | flops 5000000000 | bytes 8000000 | tf_op jit(solution)/shard_map/feed/pallas_call | solution.py:605
  242.7 6.6 %feed_rest.2 = (f32[192,1536]{1,0:T(8,128)S(1)}, f32[192,1536]{1,0:T(8,128)S(1)}, bf16[8,96,1536]{2,1,0:T(8,128)(2,1)}, bf16[8,96,1536]{2,1,0:T(8,128)(2,1)}) custom-call(bf16[192,1536]{1,0:T(8,128)(2,1)S(1)} %copy-done.27, bf16[768,192]{1,0:T(8,128)(2,1)S(1)} %get-tuple-element.158.act_ref, bf16[768,192]{1,0:T(8,128)(2,1)S(1)} %get-tuple-element.160.grad_up_ref, ...), custom_call_target="tpu_custom_call" | custom-call | flops 5000000000 | bytes 8000000 | tf_op jit(solution)/shard_map/feed_rest/pallas_call | solution.py:653
  251.5 5.9 %collective-permute-done.42 = bf16[8,48,1536]{2,1,0:T(8,128)(2,1)S(1)} collective-permute-done((bf16[8,48,1536]{2,1,0:T(8,128)(2,1)S(1)}, bf16[8,48,1536]{2,1,0:T(8,128)(2,1)S(1)}, u32[]{:S(2)}, u32[]{:S(2)}) %collective-permute-start.42) | collective-permute-done | bytes 1179680 | tf_op jit(solution)/shard_map/ppermute | solution.py:73
  261.0 6.5 %feed_rest.3 = (f32[192,1536]{1,0:T(8,128)S(1)}, f32[192,1536]{1,0:T(8,128)S(1)}, bf16[16,96,1536]{2,1,0:T(8,128)(2,1)}) custom-call(bf16[192,1536]{1,0:T(8,128)(2,1)S(1)} %copy-done.27, bf16[768,192]{1,0:T(8,128)(2,1)S(1)} %get-tuple-element.163.act_ref, bf16[768,192]{1,0:T(8,128)(2,1)S(1)} %get-tuple-element.165.grad_up_ref, ...), custom_call_target="tpu_custom_call" | custom-call | flops 5000000000 | bytes 8000000 | tf_op jit(solution)/shard_map/feed_rest/pallas_call | solution.py:653
  271.3 6.7 %collective-permute-done.44 = bf16[2,48,1536]{2,1,0:T(8,128)(2,1)S(1)} collective-permute-done((bf16[2,48,1536]{2,1,0:T(8,128)(2,1)S(1)}, bf16[2,48,1536]{2,1,0:T(8,128)(2,1)S(1)}, u32[]{:S(2)}, u32[]{:S(2)}) %collective-permute-start.44) | collective-permute-done | bytes 294944 | tf_op jit(solution)/shard_map/ppermute | solution.py:73
  290.3 6.3 %unmix.1 = (bf16[16,48,128]{2,1,0:T(8,128)(2,1)S(1)}, f32[48,1536]{1,0:T(8,128)}, bf16[48,1536]{1,0:T(8,128)(2,1)S(1)}, f32[1,1536]{1,0:T(1,128)S(1)}, f32[16,1536]{1,0:T(8,128)S(1)}) custom-call(s32[32]{0:T(128)S(1)} %copy-done.24, f32[48,1536]{1,0:T(8,128)S(1)} %add_bitcast_fusion.1.grad_feed_ref, f32[48,1536]{1,0:T(8,128)S(1)} %bitcast.112, ...), custom_call_target="tpu_custom_call" | custom-call | flops 2000000000 | bytes 8000000 | tf_op jit(solution)/shard_map/unmix/pallas_call | solution.py:432
  299.1 5.8 %collective-permute-done.47.refs_2_ = bf16[16,48,128]{2,1,0:T(8,128)(2,1)S(1)} collective-permute-done((bf16[16,48,128]{2,1,0:T(8,128)(2,1)S(1)}, bf16[16,48,128]{2,1,0:T(8,128)(2,1)S(1)}, u32[]{:S(2)}, u32[]{:S(2)}) %collective-permute-start.47) | collective-permute-done | bytes 196640 | tf_op jit(solution)/shard_map/ppermute | solution.py:73
  308.4 6.8 %output_part.1 = (bf16[16,96,1536]{2,1,0:T(8,128)(2,1)S(1)}, bf16[8,96,1536]{2,1,0:T(8,128)(2,1)}, bf16[8,96,1536]{2,1,0:T(8,128)(2,1)}) custom-call(s32[32]{0:T(128)S(1)} %shift-left_add_fusion.place_ref, bf16[48,1536]{1,0:T(8,128)(2,1)S(1)} %copy-done.21, ...), custom_call_target="tpu_custom_call", output_to_operand_aliasing={{0}: (3, {}), {1}: (4, {}), {2}: (5, {})} | custom-call | flops 1000000000 | bytes 2000000 | tf_op jit(solution)/shard_map/output_part/pallas_call | solution.py:465
  321.9 15.1 %attend_back.3 = (bf16[16,96,1536]{2,1,0:T(8,128)(2,1)}, bf16[8,96,1536]{2,1,0:T(8,128)(2,1)}, bf16[8,96,1536]{2,1,0:T(8,128)(2,1)}, bf16[32,48,64]{2,1,0:T(8,12...) custom-call(s32[32]{0:T(128)} %scatter_custom_fusion.order_ref, s32[32]{0:T(128)} %copy-done.25, ...), custom_call_target="tpu_custom_call" | custom-call | flops 2000000000 | bytes 20000000 | tf_op jit(solution)/shard_map/attend_back/pallas_call | solution.py:782
  341.6 9.0 %all-to-all-done.1.got_ref = bf16[8,192,384]{2,1,0:T(8,128)(2,1)S(1)} async-done(((bf16[8,192,384]{2,1,0:T(8,128)(2,1)}), bf16[8,192,384]{2,1,0:T(8,128)(2,1)S(1)}, u32[]{:S(2)}, u32[]{:S(2)}) %all-to-all-start.1) | async-done | bytes 1179680 | tf_op jit(solution)/shard_map/all_to_all | solution.py:964
  352.2 24.3 %attend_back.4 = (bf16[16,96,1536]{2,1,0:T(8,128)(2,1)}, bf16[8,96,1536]{2,1,0:T(8,128)(2,1)}, bf16[8,96,1536]{2,1,0:T(8,128)(2,1)}, bf16[32,48,64]{2,1,0:T(8,12...) custom-call(s32[32]{0:T(128)} %scatter_custom_fusion.order_ref, ...), custom_call_target="tpu_custom_call", output_to_operand_aliasing={{0}: (21, {}), {1}: (22, {}), {2}: (23, {})} | custom-call | flops 40000000000 | bytes 20000000 | tf_op jit(solution)/shard_map/attend_back/pallas_call | solution.py:782
  383.7 15.2 %attend_back.5 = (bf16[16,96,1536]{2,1,0:T(8,128)(2,1)}, bf16[8,96,1536]{2,1,0:T(8,128)(2,1)}, bf16[8,96,1536]{2,1,0:T(8,128)(2,1)}, bf16[32,48,64]{2,1,0:T(8,12...) custom-call(s32[32]{0:T(128)} %scatter_custom_fusion.order_ref, ...), custom_call_target="tpu_custom_call", output_to_operand_aliasing={{0}: (21, {}), {1}: (22, {}), {2}: (23, {})} | custom-call | flops 30000001024 | bytes 20000000 | tf_op jit(solution)/shard_map/attend_back/pallas_call | solution.py:782
  488.3 11.3 %collective-permute-done.71 = bf16[1,96,1536]{2,1,0:T(8,128)(2,1)S(1)} collective-permute-done((bf16[1,96,1536]{2,1,0:T(8,128)(2,1)S(1)}, bf16[1,96,1536]{2,1,0:T(8,128)(2,1)S(1)}, u32[]{:S(2)}, u32[]{:S(2)}) %collective-permute-start.71) | collective-permute-done | bytes 294944 | tf_op jit(solution)/shard_map/ppermute | solution.py:73
  (428 shorter events, 259.6 us)
Async XLA Ops:
  47.1 28.4 %collective-permute-start.12 = (bf16[4,96,1536]{2,1,0:T(8,128)(2,1)}, bf16[4,96,1536]{2,1,0:T(8,128)(2,1)}, u32[]{:S(2)}, u32[]{:S(2)}) collective-permute-start(bf16[4,96,1536]{2,1,0:T(8,128)(2,1)} %pad_maximum_fusion.refs_0_.refs_7_), channel_id=1, source_target_pairs={{0,4},{1,3},{2,6},{3,1},{4,0},{5,7},{6,2},{7,5},{8,12},{9,11},{10,... | collective-permute-start | bytes 3538952 | tf_op jit(solution)/shard_map/ppermute | solution.py:73
  48.7 27.1 %collective-permute-start.13 = (bf16[4,96,1536]{2,1,0:T(8,128)(2,1)}, bf16[4,96,1536]{2,1,0:T(8,128)(2,1)}, u32[]{:S(2)}, u32[]{:S(2)}) collective-permute-start(bf16[4,96,1536]{2,1,0:T(8,128)(2,1)} %pad_maximum_fusion.refs_0_.refs_7_), channel_id=1, source_target_pairs={{0,2},{1,5},{2,0},{3,7},{4,6},{5,1},{6,4},{7,3},{8,10},{9,13},{10,... | collective-permute-start | bytes 3538952 | tf_op jit(solution)/shard_map/ppermute | solution.py:73
  50.2 52.0 %collective-permute-start.15 = (bf16[4,96,1536]{2,1,0:T(8,128)(2,1)}, bf16[4,96,1536]{2,1,0:T(8,128)(2,1)}, u32[]{:S(2)}, u32[]{:S(2)}) collective-permute-start(bf16[4,96,1536]{2,1,0:T(8,128)(2,1)} %pad_maximum_fusion.refs_0_.refs_7_), channel_id=1, source_target_pairs={{0,1},{1,0},{2,3},{3,2},{4,5},{5,4},{6,7},{7,6},{8,9},{9,8},{10,11... | collective-permute-start | bytes 3538952 | tf_op jit(solution)/shard_map/ppermute | solution.py:73
  75.8 25.8 %collective-permute-start.14 = (bf16[4,96,1536]{2,1,0:T(8,128)(2,1)}, bf16[4,96,1536]{2,1,0:T(8,128)(2,1)}, u32[]{:S(2)}, u32[]{:S(2)}) collective-permute-start(bf16[4,96,1536]{2,1,0:T(8,128)(2,1)} %collective-permute-done.12.refs_1_.refs_8_), channel_id=1, source_target_pairs={{0,2},{1,5},{2,0},{3,7},{4,6},{5,1},{6,4},{7,3},{8,10},{9,13},{10,... | collective-permute-start | bytes 3538952 | tf_op jit(solution)/shard_map/ppermute | solution.py:73
  84.3 15.5 %collective-permute-start.19 = (bf16[2,96,1536]{2,1,0:T(8,128)(2,1)S(1)}, bf16[2,96,1536]{2,1,0:T(8,128)(2,1)}, u32[]{:S(2)}, u32[]{:S(2)}) collective-permute-start(bf16[2,96,1536]{2,1,0:T(8,128)(2,1)S(1)} %pad_maximum_fusion.4), channel_id=1, source_target_pairs={{0,8},{1,9},{2,10},{3,11},{4,12},{5,13},{6,14},{7,15},{8,0},{9,1},... | collective-permute-start | bytes 1769480 | tf_op jit(solution)/shard_map/ppermute | solution.py:73
  101.6 28.7 %collective-permute-start.24 = (bf16[4,96,1536]{2,1,0:T(8,128)(2,1)S(1)}, bf16[4,96,1536]{2,1,0:T(8,128)(2,1)S(1)}, u32[]{:S(2)}, u32[]{:S(2)}) collective-permute-start(bf16[4,96,1536]{2,1,0:T(8,128)(2,1)S(1)} %pad_maximum_fusion.1.refs_4_.refs_0_), channel_id=1, source_target_pairs={{0,4},{1,3},{2,6},{3,1},{4,0},{5,7},{6,2},{7,5},{8,12},{9,11},{10,... | collective-permute-start | bytes 3538952 | tf_op jit(solution)/shard_map/ppermute | solution.py:73
  102.2 28.2 %collective-permute-start.25 = (bf16[4,96,1536]{2,1,0:T(8,128)(2,1)S(1)}, bf16[4,96,1536]{2,1,0:T(8,128)(2,1)}, u32[]{:S(2)}, u32[]{:S(2)}) collective-permute-start(bf16[4,96,1536]{2,1,0:T(8,128)(2,1)S(1)} %pad_maximum_fusion.1.refs_4_.refs_0_), channel_id=1, source_target_pairs={{0,2},{1,5},{2,0},{3,7},{4,6},{5,1},{6,4},{7,3},{8,10},{9,13},{10,... | collective-permute-start | bytes 3538952 | tf_op jit(solution)/shard_map/ppermute | solution.py:73
  130.3 24.0 %collective-permute-start.26 = (bf16[4,96,1536]{2,1,0:T(8,128)(2,1)S(1)}, bf16[4,96,1536]{2,1,0:T(8,128)(2,1)}, u32[]{:S(2)}, u32[]{:S(2)}) collective-permute-start(bf16[4,96,1536]{2,1,0:T(8,128)(2,1)S(1)} %collective-permute-done.24.refs_5_.refs_1_), channel_id=1, source_target_pairs={{0,2},{1,5},{2,0},{3,7},{4,6},{5,1},{6,4},{7,3},{8,10},{9,13},{10,... | collective-permute-start | bytes 3538952 | tf_op jit(solution)/shard_map/ppermute | solution.py:73
  130.9 34.4 %all-to-all-start = ((bf16[8,192,384]{2,1,0:T(8,128)(2,1)}), bf16[8,192,384]{2,1,0:T(8,128)(2,1)}, u32[]{:S(2)}, u32[]{:S(2)}) async-start(bf16[8,192,384]{2,1,0:T(8,128)(2,1)} %pad_maximum_fusion.2), calls=%async_computation | async-start | bytes 2359296 | tf_op jit(solution)/shard_map/all_to_all | solution.py:931
  138.0 14.9 %collective-permute-start.22 = (bf16[16,48,128]{2,1,0:T(8,128)(2,1)S(1)}, bf16[16,48,128]{2,1,0:T(8,128)(2,1)S(1)}, u32[]{:S(2)}, u32[]{:S(2)}) collective-permute-start(bf16[16,48,128]{2,1,0:T(8,128)(2,1)S(1)} %bitcast.144), channel_id=1, source_target_pairs={{0,2},{1,3},{2,0},{3,1},{4,6},{5,7},{6,4},{7,5},{8,10},{9,11},{10,... | collective-permute-start | bytes 589832 | tf_op jit(solution)/shard_map/ppermute | solution.py:73
  139.9 25.5 %collective-permute-start.27 = (bf16[4,96,1536]{2,1,0:T(8,128)(2,1)S(1)}, bf16[4,96,1536]{2,1,0:T(8,128)(2,1)}, u32[]{:S(2)}, u32[]{:S(2)}) collective-permute-start(bf16[4,96,1536]{2,1,0:T(8,128)(2,1)S(1)} %pad_maximum_fusion.1.refs_4_.refs_0_), channel_id=1, source_target_pairs={{0,1},{1,0},{2,3},{3,2},{4,5},{5,4},{6,7},{7,6},{8,9},{9,8},{10,11... | collective-permute-start | bytes 3538952 | tf_op jit(solution)/shard_map/ppermute | solution.py:73
  140.2 25.1 %collective-permute-start.28 = (bf16[4,96,1536]{2,1,0:T(8,128)(2,1)S(1)}, bf16[4,96,1536]{2,1,0:T(8,128)(2,1)}, u32[]{:S(2)}, u32[]{:S(2)}) collective-permute-start(bf16[4,96,1536]{2,1,0:T(8,128)(2,1)S(1)} %collective-permute-done.24.refs_5_.refs_1_), channel_id=1, source_target_pairs={{0,1},{1,0},{2,3},{3,2},{4,5},{5,4},{6,7},{7,6},{8,9},{9,8},{10,11... | collective-permute-start | bytes 3538952 | tf_op jit(solution)/shard_map/ppermute | solution.py:73
  230.5 20.9 %collective-permute-start.40 = (bf16[8,48,1536]{2,1,0:T(8,128)(2,1)S(1)}, bf16[8,48,1536]{2,1,0:T(8,128)(2,1)}, u32[]{:S(2)}, u32[]{:S(2)}) collective-permute-start(bf16[8,48,1536]{2,1,0:T(8,128)(2,1)S(1)} %get-tuple-element.147), channel_id=1, source_target_pairs={{0,1},{1,0},{2,3},{3,2},{4,5},{5,4},{6,7},{7,6},{8,9},{9,8},{10,11... | collective-permute-start | bytes 3538952 | tf_op jit(solution)/shard_map/ppermute | solution.py:73
  241.1 16.3 %collective-permute-start.42 = (bf16[8,48,1536]{2,1,0:T(8,128)(2,1)S(1)}, bf16[8,48,1536]{2,1,0:T(8,128)(2,1)S(1)}, u32[]{:S(2)}, u32[]{:S(2)}) collective-permute-start(bf16[8,48,1536]{2,1,0:T(8,128)(2,1)S(1)} %add_convert_fusion.4), channel_id=1, source_target_pairs={{0,2},{1,5},{2,0},{3,7},{4,6},{5,1},{6,4},{7,3},{8,10},{9,13},{10,... | collective-permute-start | bytes 3538952 | tf_op jit(solution)/shard_map/ppermute | solution.py:73
  317.4 19.6 %collective-permute-start.49 = (bf16[8,96,1536]{2,1,0:T(8,128)(2,1)}, bf16[8,96,1536]{2,1,0:T(8,128)(2,1)}, u32[]{:S(2)}, u32[]{:S(2)}) collective-permute-start(bf16[8,96,1536]{2,1,0:T(8,128)(2,1)} %get-tuple-element.182), channel_id=1, source_target_pairs={{0,1},{1,0},{2,3},{3,2},{4,5},{5,4},{6,7},{7,6},{8,9},{9,8},{10,11... | collective-permute-start | bytes 7077896 | tf_op jit(solution)/shard_map/ppermute | solution.py:73
  317.4 19.6 %collective-permute-start.50 = (bf16[8,96,1536]{2,1,0:T(8,128)(2,1)}, bf16[8,96,1536]{2,1,0:T(8,128)(2,1)}, u32[]{:S(2)}, u32[]{:S(2)}) collective-permute-start(bf16[8,96,1536]{2,1,0:T(8,128)(2,1)} %get-tuple-element.184), channel_id=1, source_target_pairs={{0,1},{1,0},{2,3},{3,2},{4,5},{5,4},{6,7},{7,6},{8,9},{9,8},{10,11... | collective-permute-start | bytes 7077896 | tf_op jit(solution)/shard_map/ppermute | solution.py:73
  317.9 32.7 %all-to-all-start.1 = ((bf16[8,192,384]{2,1,0:T(8,128)(2,1)}), bf16[8,192,384]{2,1,0:T(8,128)(2,1)S(1)}, u32[]{:S(2)}, u32[]{:S(2)}) async-start(bf16[8,192,384]{2,1,0:T(8,128)(2,1)} %pack_back.1), calls=%async_computation.1 | async-start | bytes 2359296 | tf_op jit(solution)/shard_map/all_to_all | solution.py:964
  350.6 29.2 %collective-permute-start.51 = (bf16[8,96,1536]{2,1,0:T(8,128)(2,1)}, bf16[8,96,1536]{2,1,0:T(8,128)(2,1)}, u32[]{:S(2)}, u32[]{:S(2)}) collective-permute-start(bf16[8,96,1536]{2,1,0:T(8,128)(2,1)} %add_convert_fusion.1), channel_id=1, source_target_pairs={{0,2},{1,5},{2,0},{3,7},{4,6},{5,1},{6,4},{7,3},{8,10},{9,13},{10,... | collective-permute-start | bytes 7077896 | tf_op jit(solution)/shard_map/ppermute | solution.py:73
  382.2 17.9 %collective-permute-start.52 = (bf16[4,96,1536]{2,1,0:T(8,128)(2,1)S(1)}, bf16[4,96,1536]{2,1,0:T(8,128)(2,1)S(1)}, u32[]{:S(2)}, u32[]{:S(2)}) collective-permute-start(bf16[4,96,1536]{2,1,0:T(8,128)(2,1)S(1)} %add_convert_fusion.3), channel_id=1, source_target_pairs={{0,4},{1,3},{2,6},{3,1},{4,0},{5,7},{6,2},{7,5},{8,12},{9,11},{10,... | collective-permute-start | bytes 3538952 | tf_op jit(solution)/shard_map/ppermute | solution.py:73
  401.6 15.2 %collective-permute-start.60 = (bf16[8,96,1536]{2,1,0:T(8,128)(2,1)}, bf16[8,96,1536]{2,1,0:T(8,128)(2,1)}, u32[]{:S(2)}, u32[]{:S(2)}) collective-permute-start(bf16[8,96,1536]{2,1,0:T(8,128)(2,1)} %get-tuple-element.227), channel_id=1, source_target_pairs={{0,1},{1,0},{2,3},{3,2},{4,5},{5,4},{6,7},{7,6},{8,9},{9,8},{10,11... | collective-permute-start | bytes 7077896 | tf_op jit(solution)/shard_map/ppermute | solution.py:73
  415.1 30.2 %collective-permute-start.63 = (bf16[8,96,1536]{2,1,0:T(8,128)(2,1)S(1)}, bf16[8,96,1536]{2,1,0:T(8,128)(2,1)}, u32[]{:S(2)}, u32[]{:S(2)}) collective-permute-start(bf16[8,96,1536]{2,1,0:T(8,128)(2,1)S(1)} %add_convert_fusion), channel_id=1, source_target_pairs={{0,2},{1,5},{2,0},{3,7},{4,6},{5,1},{6,4},{7,3},{8,10},{9,13},{10,... | collective-permute-start | bytes 7077896 | tf_op jit(solution)/shard_map/ppermute | solution.py:73
  443.4 15.2 %collective-permute-start.56 = (bf16[1,96,1536]{2,1,0:T(8,128)(2,1)S(1)}, bf16[1,96,1536]{2,1,0:T(8,128)(2,1)S(1)}, u32[]{:S(2)}, u32[]{:S(2)}) collective-permute-start(bf16[1,96,1536]{2,1,0:T(8,128)(2,1)S(1)} %add_convert_fusion.9), channel_id=1, source_target_pairs={{0,16},{1,17},{2,18},{3,19},{4,20},{5,21},{6,22},{7,23},{8,24},{9,... | collective-permute-start | bytes 884744 | tf_op jit(solution)/shard_map/ppermute | solution.py:73
  448.7 18.5 %collective-permute-start.69 = (bf16[4,96,1536]{2,1,0:T(8,128)(2,1)S(1)}, bf16[4,96,1536]{2,1,0:T(8,128)(2,1)S(1)}, u32[]{:S(2)}, u32[]{:S(2)}) collective-permute-start(bf16[4,96,1536]{2,1,0:T(8,128)(2,1)S(1)} %add_convert_fusion.2), channel_id=1, source_target_pairs={{0,4},{1,3},{2,6},{3,1},{4,0},{5,7},{6,2},{7,5},{8,12},{9,11},{10,... | collective-permute-start | bytes 3538952 | tf_op jit(solution)/shard_map/ppermute | solution.py:73
  465.0 14.7 %collective-permute-start.67 = (bf16[2,48,72]{2,1,0:T(8,128)(2,1)S(1)}, bf16[2,48,72]{2,1,0:T(8,128)(2,1)S(1)}, u32[]{:S(2)}, u32[]{:S(2)}) collective-permute-start(bf16[2,48,72]{2,1,0:T(8,128)(2,1)S(1)} %slice.601), channel_id=1, source_target_pairs={{0,4},{1,3},{2,6},{3,1},{4,0},{5,7},{6,2},{7,5},{8,12},{9,11},{10,... | collective-permute-start | bytes 41480 | tf_op jit(solution)/shard_map/ppermute | solution.py:73
  (126 other events, 1333.5 us)

commit v4 on v3

--- a/solution.py
+++ b/solution.py
@@ -380,8 +380,8 @@
             jax.ShapeDtypeStruct((rows, heads * head_dim), BF),
         ],
         scratch_shapes=[pltpu.VMEM((count, block, width), BF), pltpu.SemaphoreType.DMA((count,))],
-        compiler_params=params(32),
-        cost_estimate=cost(2e9, 8e6),
+        compiler_params=params(60),
+        cost_estimate=cost(1e6, 1e6),
         name="mixer",
     )(order, latent_own, gain, *pieces, *parts)
 
@@ -435,7 +435,7 @@
         out_specs=[whole(shape) for shape, _ in shapes],
         out_shape=[jax.ShapeDtypeStruct(*item) for item in shapes],
         scratch_shapes=[pltpu.VMEM((count, block, width), BF), pltpu.SemaphoreType.DMA((count,))],
-        compiler_params=params(32),
+        compiler_params=params(60),
         cost_estimate=cost(2e9, 8e6),
         name="unmix",
     )(order, *arrays, *parts)
@@ -469,7 +469,7 @@
         out_shape=[jax.ShapeDtypeStruct(shape, BF) for shape in shapes],
         input_output_aliases={3: 0, 4: 1, 5: 2} if halves else {},
         scratch_shapes=[pltpu.VMEM((count, block, width), BF), pltpu.SemaphoreType.DMA((count,))],
-        compiler_params=params(32),
+        compiler_params=params(60),
         cost_estimate=cost(1e9, 2e6),
         name="output_part",
     )(place, context, low, *halves)
@@ -609,7 +609,7 @@
         out_shape=[jax.ShapeDtypeStruct((rows, hid), BF)] * 2
         + [jax.ShapeDtypeStruct((count * n // splits, per, width), BF)] * splits,
         scratch_shapes=[store] * 3 + [sems] * 3,
-        compiler_params=params(48),
+        compiler_params=params(60),
         cost_estimate=cost(5e9, 8e6),
         name="feed",
     )(up, down, *feed_parts, *grad_parts)
@@ -624,8 +624,8 @@
     chunk = n * per
     feeds, grads = loads(feed, per, feed_st, feed_sem), loads(grad, per, grad_st, grad_sem)
     for i in range(part_count):
+        start(grads[i])
         start(feeds[i])
-        start(grads[i])
     down = down_ref[...]
     first = pl.ds(0, per)
     outs = []
@@ -703,7 +703,8 @@
                 head = block & (heads - 1)
                 here = (head >= first) & (head < first + count)
                 to = jnp.where(here, head - first + jnp.where(block >= heads, count, 0), 0)
-                loads_here.append((here, pltpu.make_async_copy(part.at[k], weight_ref.at[to], sem_ref.at[n])))
+                copy = pltpu.make_async_copy(part.at[k], weight_ref.at[to], sem_ref.at[n])
+                loads_here.append((here, copy))
         for here, c in loads_here:
             pl.when(here)(c.start)
         grad_media_ref[...] = jnp.zeros_like(grad_media_ref)
@@ -729,6 +730,7 @@
     own = own_ref[...]
     own_scores = own_score_ref[...]
     key_mix = jnp.zeros(queries.shape, F32)
+    own_sum = jnp.zeros(own_scores.shape, F32)
     for s in range(seqs):
         media = media_ref[s]
         lifted = gp_ref[s]
@@ -740,12 +742,15 @@
         ds = (probs * (mm_nt(lifted, media) - row_term)).astype(BF)
         own_ds = (own_probs * (mm_nt(lifted, own) - row_term)).astype(BF)
         probs, own_probs = probs.astype(BF), own_probs.astype(BF)
-        key_mix = key_mix + dot(ds, media) + dot(own_ds, own)
+        key_mix = key_mix + dot(ds, media)
+        own_sum = own_sum + own_ds.astype(F32)
         mix = (dot(probs, media) + dot(own_probs, own)).astype(BF)
         for j in range(group):
             mix_ref[j, s * lat : (s + 1) * lat, :] = mix[j * lat : (j + 1) * lat, :]
-        grad_media_ref[s] += mm_tn(ds, queries) + mm_tn(probs, lifted)
-        grad_own_ref[...] += mm_tn(own_ds, queries) + mm_tn(own_probs, lifted)
+        pair = jnp.concatenate([queries, lifted])
+        grad_media_ref[s] += mm_tn(jnp.concatenate([ds, probs]), pair)
+        grad_own_ref[...] += mm_tn(jnp.concatenate([own_ds, own_probs]), pair)
+    key_mix = key_mix + dot(own_sum.astype(BF), own)
     key_mix_ref[...] = (key_mix * factor).astype(BF)
     per = query_part_ref.shape[0] // heads
     pl.when(step > 0)(out_wait)
@@ -908,12 +913,13 @@
     query_own = mm_tn(query_weight, hidden_lat.T).astype(BF)
     frame_ids = jnp.arange(grid.frame, dtype=jnp.int32) ^ slot
     query_z = grid.gather(query_own[None], "cz")
+    query_a = grid.gather(query_z, "a")
     first, *rest = grid.strides(grid.depth)
     mixed_first = grid.step(after(jnp.concatenate([output_weight, grad_out.astype(BF)]), query_z)[None], "z", first)
     mixed_z = mixed_first
     for k in rest:
-        mixed_z = grid.step(mixed_z, "z", k)
-    query_all = grid.gather(query_z, "ab")
+        mixed_z = grid.step(after(mixed_z, query_a), "z", k)
+    query_all = grid.gather(query_a, "b")
     query_t = query_all.reshape(grid.count, part, grid.frame, own_rows)
     query_places = grid.places("czab")
     query_t = query_t.at[query_places[:, None], :, frame_ids[None, :]].get(mode="promise_in_bounds")
@@ -936,13 +942,12 @@
     else:
         output_parts = aligned_parts([p[:, :part] for p in mixed_parts])
         grad_parts = [p[:, part:] for p in mixed_parts]
-    pieces[0] = after(pieces[0], feed_got)
     mixed, normed_feed, hidden_feed, context, context_low = mixer(
         order, lat_own, feed_scale, pieces, output_parts, head_dim
     )
 
     up_t, down_w = unpack_feed(feed_got)
-    feed_parts = grid.gather_core(grid.gather_ab(grid.gather(hidden_feed[None], "z"), up_t))
+    feed_parts = grid.gather_core(grid.gather_ab(grid.gather(after(hidden_feed, feed_got)[None], "z"), up_t))
     half = len(feed_parts) // 2
     far, near = (feed_parts[half:], grad_parts[half:]), (feed_parts[:half], grad_parts[:half])
     far_act, far_grad_up, low, high = feed(up_t, down_w, *far, 2)

time: 510 us -> 502 us (0.984)
  waiting for transfers between devices: 174 us -> 161 us
  starting transfers between devices: 76.8 us -> 85 us
    all_to_all x1, waiting for transfers between devices: 8.91 us -> 0.01 us  [local(): feed_got = lax.all_to_all(after(feed_got, folded), 'seq', 0, 0)]
    ppermute x72, starting transfers between devices: 67.5 us -> 73.3 us  [send(): return lax.ppermute(value, BOTH, perm)]
    ppermute x72, waiting for transfers between devices: 156 us -> 151 us  [send(): return lax.ppermute(value, BOTH, perm)]
    unnamed x165 -> x178, local copies, waits for them, and re-layouts: 22.6 us -> 19.5 us
  transfers between devices with their start and end apart: 74 -> 74, of which waited for: 40 -> 39; matrix products, arithmetic and copies ran while one was open for 15% -> 17% of each run, Pallas kernels for 22% -> 23%
where the time goes in v4:
time: 502 us; the launch traced here: 494 us
  waiting for transfers between devices  161 us (32%)
  Pallas kernels  133 us (26%)
  starting transfers between devices  85 us (17%)
  other arithmetic  65.2 us (13%)
  local copies, waits for them, and re-layouts  43.8 us (9%)
    ppermute x72, waiting for transfers between devices, send(): return lax.ppermute(value, BOTH, perm)  151 us
    ppermute x72, starting transfers between devices, send(): return lax.ppermute(value, BOTH, perm)  73.3 us
    pallas_call x3, Pallas kernels, attend_back(): pl.pallas_call(functools.partial(attend_back_kernel, sizes), grid=(count...  53 us
    convert_element_type x16, other arithmetic, step(): self.sum(half, self.size).astype(BF)  26.9 us
    pallas_call x1, Pallas kernels, attend(): pl.pallas_call(functools.partial(attend_kernel, (heads, group, seqs, lat,...  22.8 us
    unnamed x178, local copies, waits for them, and re-layouts  19.5 us
    pallas_call x2, Pallas kernels, feed(): pl.pallas_call(functools.partial(feed_kernel, count), in_specs=[whole(up....  18.4 us
    pallas_call x2, Pallas kernels, feed_rest(): pl.pallas_call(functools.partial(feed_rest_kernel, count), in_specs=[whol...  11.3 us
  transfers between devices with their start and end apart: 74, of which 39 were waited for; matrix products, arithmetic and copies ran while one was open for 17% of the time, Pallas kernels for 23%

profile of v4, /device:TPU:0, one launch (start us, length us, event | category | flops | bytes accessed | tf_op | source)
XLA Modules:
  0.0 494.5 jit_solution(13961539503774303317)
XLA Ops:
  18.9 9.6 %collective-permute-done.2 = bf16[1,96,1536]{2,1,0:T(8,128)(2,1)S(1)} collective-permute-done((bf16[1,96,1536]{2,1,0:T(8,128)(2,1)}, bf16[1,96,1536]{2,1,0:T(8,128)(2,1)S(1)}, u32[]{:S(2)}, u32[]{:S(2)}) %collective-permute-start.2) | collective-permute-done | bytes 294944 | tf_op jit(solution)/shard_map/ppermute | solution.py:73
  78.5 5.7 %collective-permute-done.18 = bf16[1,96,1536]{2,1,0:T(8,128)(2,1)S(1)} collective-permute-done((bf16[1,96,1536]{2,1,0:T(8,128)(2,1)S(1)}, bf16[1,96,1536]{2,1,0:T(8,128)(2,1)S(1)}, u32[]{:S(2)}, u32[]{:S(2)}) %collective-permute-start.18) | collective-permute-done | bytes 294944 | tf_op jit(solution)/shard_map/ppermute | solution.py:73
  86.8 7.5 %collective-permute-done.11 = bf16[16,48,64]{2,1,0:T(8,128)(2,1)S(1)} collective-permute-done((bf16[16,48,64]{2,1,0:T(8,128)(2,1)}, bf16[16,48,64]{2,1,0:T(8,128)(2,1)S(1)}, u32[]{:S(2)}, u32[]{:S(2)}) %collective-permute-start.11) | collective-permute-done | bytes 98336 | tf_op jit(solution)/shard_map/ppermute | solution.py:73
  107.5 22.8 %attend.1 = (bf16[1024,1536]{1,0:T(8,128)(2,1)}, f32[3,1024,256]{2,1,0:T(8,128)}, f32[1024,16]{1,0:T(8,128)}, f32[16,192,128]{2,1,0:T(8,128)}) custom-call(s32[32]{0:T(128)} %scatter_custom_fusion.order_ref, s32[3]{0:T(128)} %compare_convert_fusion.9.valid_ref, bf16[16,96,64]{2,1,0:T(8,128)(2,1)} %copy.94.query_ref, bf16[3,256,1536]{2,1,0:T(8,128)(2,1)} %fusion.8.media_ref, ...), custom_call_target="tpu_custom_call" | custom-call | flops 2000000000 | bytes 2000000 | tf_op jit(solution)/shard_map/attend/pallas_call | solution.py:304
  131.5 6.7 %all-to-all-start = ((bf16[8,192,384]{2,1,0:T(8,128)(2,1)}), bf16[8,192,384]{2,1,0:T(8,128)(2,1)S(1)}, u32[]{:S(2)}, u32[]{:S(2)}) async-start(bf16[8,192,384]{2,1,0:T(8,128)(2,1)} %pad_maximum_fusion.1), calls=%async_computation | async-start | bytes 2359296 | tf_op jit(solution)/shard_map/all_to_all | solution.py:937
  143.0 10.0 %collective-permute-done.22.refs_2_ = bf16[16,48,128]{2,1,0:T(8,128)(2,1)S(1)} collective-permute-done((bf16[16,48,128]{2,1,0:T(8,128)(2,1)S(1)}, bf16[16,48,128]{2,1,0:T(8,128)(2,1)S(1)}, u32[]{:S(2)}, u32[]{:S(2)}) %collective-permute-start.22) | collective-permute-done | bytes 196640 | tf_op jit(solution)/shard_map/ppermute | solution.py:73
  161.0 7.6 %mixer.1 = (f32[48,1536]{1,0:T(8,128)}, f32[48,1536]{1,0:T(8,128)}, bf16[48,1536]{1,0:T(8,128)(2,1)}, f32[16,48,128]{2,1,0:T(8,128)}, bf16[48,1536]{1,0:T(8,128)(2,1)}) custom-call(s32[32]{0:T(128)} %scatter_custom_fusion.order_ref, f32[16,1536]{1,0:T(8,128)} %constant_dynamic-slice_fusion.1.latent_ref, f32[1,1536]{1,0:T(1,128)} %get-tuple-element.298.gain_ref, ...), custom_call_target="tpu_custom_call" | custom-call | flops 1000000 | bytes 1000000 | tf_op jit(solution)/shard_map/mixer/pallas_call | solution.py:369
  172.3 7.4 %collective-permute-done.31 = bf16[1,48,1536]{2,1,0:T(8,128)(2,1)S(1)} collective-permute-done((bf16[1,48,1536]{2,1,0:T(8,128)(2,1)}, bf16[1,48,1536]{2,1,0:T(8,128)(2,1)S(1)}, u32[]{:S(2)}, u32[]{:S(2)}) %collective-permute-start.31) | collective-permute-done | bytes 147488 | tf_op jit(solution)/shard_map/ppermute | solution.py:73
  181.5 7.6 %collective-permute-done.32 = bf16[2,48,1536]{2,1,0:T(8,128)(2,1)S(1)} collective-permute-done((bf16[2,48,1536]{2,1,0:T(8,128)(2,1)S(1)}, bf16[2,48,1536]{2,1,0:T(8,128)(2,1)S(1)}, u32[]{:S(2)}, u32[]{:S(2)}) %collective-permute-start.32) | collective-permute-done | bytes 294944 | tf_op jit(solution)/shard_map/ppermute | solution.py:73
  196.6 9.9 %collective-permute-done.34.refs_1_ = bf16[4,48,1536]{2,1,0:T(8,128)(2,1)S(1)} collective-permute-done((bf16[4,48,1536]{2,1,0:T(8,128)(2,1)S(1)}, bf16[4,48,1536]{2,1,0:T(8,128)(2,1)S(1)}, u32[]{:S(2)}, u32[]{:S(2)}) %collective-permute-start.34) | collective-permute-done | bytes 589856 | tf_op jit(solution)/shard_map/ppermute | solution.py:73
  208.0 8.4 %collective-permute-done.38.refs_3_ = bf16[4,48,1536]{2,1,0:T(8,128)(2,1)S(1)} collective-permute-done((bf16[4,48,1536]{2,1,0:T(8,128)(2,1)S(1)}, bf16[4,48,1536]{2,1,0:T(8,128)(2,1)S(1)}, u32[]{:S(2)}, u32[]{:S(2)}) %collective-permute-start.38) | collective-permute-done | bytes 589856 | tf_op jit(solution)/shard_map/ppermute | solution.py:73
  219.3 9.2 %feed.2 = (bf16[768,192]{1,0:T(8,128)(2,1)}, bf16[768,192]{1,0:T(8,128)(2,1)}, bf16[8,48,1536]{2,1,0:T(8,128)(2,1)}, bf16[8,48,1536]{2,1,0:T(8,128)(2,1)}) custom-call(bf16[192,1536]{1,0:T(8,128)(2,1)} %get-tuple-element.142.up_ref, bf16[192,1536]{1,0:T(8,128)(2,1)} %get-tuple-element.143.down_ref, bf16[4,48,1536]{2,1,0:T(8,128)(2,1)} %copy-done.14, ...), custom_call_target="tpu_custom_call" | custom-call | flops 5000000000 | bytes 8000000 | tf_op jit(solution)/shard_map/feed/pallas_call | solution.py:605
  229.1 9.2 %feed.3 = (bf16[768,192]{1,0:T(8,128)(2,1)}, bf16[768,192]{1,0:T(8,128)(2,1)}, bf16[16,48,1536]{2,1,0:T(8,128)(2,1)}) custom-call(bf16[192,1536]{1,0:T(8,128)(2,1)} %get-tuple-element.142.up_ref, bf16[192,1536]{1,0:T(8,128)(2,1)} %get-tuple-element.143.down_ref, bf16[4,48,1536]{2,1,0:T(8,128)(2,1)} %copy-done.5, bf16[4,48,1536]{2,1,0:T(8,128)(2,1)} %copy-done.7, ...), custom_call_target="tpu_custom_call" | custom-call | flops 5000000000 | bytes 8000000 | tf_op jit(solution)/shard_map/feed/pallas_call | solution.py:605
  241.1 5.4 %feed_rest.2 = (f32[192,1536]{1,0:T(8,128)S(1)}, f32[192,1536]{1,0:T(8,128)S(1)}, bf16[8,96,1536]{2,1,0:T(8,128)(2,1)}, bf16[8,96,1536]{2,1,0:T(8,128)(2,1)}) custom-call(bf16[192,1536]{1,0:T(8,128)(2,1)S(1)} %copy-done.11, bf16[768,192]{1,0:T(8,128)(2,1)S(1)} %copy-done.24, bf16[768,192]{1,0:T(8,128)(2,1)S(1)} %copy-done.25, ...), custom_call_target="tpu_custom_call" | custom-call | flops 5000000000 | bytes 8000000 | tf_op jit(solution)/shard_map/feed_rest/pallas_call | solution.py:653
  248.7 7.6 %collective-permute-done.42 = bf16[8,48,1536]{2,1,0:T(8,128)(2,1)S(1)} collective-permute-done((bf16[8,48,1536]{2,1,0:T(8,128)(2,1)S(1)}, bf16[8,48,1536]{2,1,0:T(8,128)(2,1)S(1)}, u32[]{:S(2)}, u32[]{:S(2)}) %collective-permute-start.42) | collective-permute-done | bytes 1179680 | tf_op jit(solution)/shard_map/ppermute | solution.py:73
  259.8 5.8 %feed_rest.3 = (f32[192,1536]{1,0:T(8,128)S(1)}, f32[192,1536]{1,0:T(8,128)S(1)}, bf16[16,96,1536]{2,1,0:T(8,128)(2,1)}) custom-call(bf16[192,1536]{1,0:T(8,128)(2,1)S(1)} %copy-done.11, bf16[768,192]{1,0:T(8,128)(2,1)S(1)} %copy-done.22, bf16[768,192]{1,0:T(8,128)(2,1)S(1)} %copy-done.23, bf16[4,48,1536]{2,1,0:T(8,128)(2,1)S(1)} %copy-done.6, ...), custom_call_target="tpu_custom_call" | custom-call | flops 5000000000 | bytes 8000000 | tf_op jit(solution)/shard_map/feed_rest/pallas_call | solution.py:653
  269.9 6.6 %collective-permute-done.44 = bf16[2,48,1536]{2,1,0:T(8,128)(2,1)S(1)} collective-permute-done((bf16[2,48,1536]{2,1,0:T(8,128)(2,1)S(1)}, bf16[2,48,1536]{2,1,0:T(8,128)(2,1)S(1)}, u32[]{:S(2)}, u32[]{:S(2)}) %collective-permute-start.44) | collective-permute-done | bytes 294944 | tf_op jit(solution)/shard_map/ppermute | solution.py:73
  288.1 6.6 %unmix.1 = (bf16[16,48,128]{2,1,0:T(8,128)(2,1)}, f32[48,1536]{1,0:T(8,128)}, bf16[48,1536]{1,0:T(8,128)(2,1)}, f32[1,1536]{1,0:T(1,128)}, f32[16,1536]{1,0:T(8,128)}) custom-call(s32[32]{0:T(128)} %scatter_custom_fusion.order_ref, f32[48,1536]{1,0:T(8,128)} %add_bitcast_fusion.1.grad_feed_ref, f32[48,1536]{1,0:T(8,128)} %bitcast.117, ...), custom_call_target="tpu_custom_call" | custom-call | flops 2000000000 | bytes 8000000 | tf_op jit(solution)/shard_map/unmix/pallas_call | solution.py:432
  297.2 5.6 %collective-permute-done.47.refs_2_ = bf16[16,48,128]{2,1,0:T(8,128)(2,1)S(1)} collective-permute-done((bf16[16,48,128]{2,1,0:T(8,128)(2,1)}, bf16[16,48,128]{2,1,0:T(8,128)(2,1)S(1)}, u32[]{:S(2)}, u32[]{:S(2)}) %collective-permute-start.47) | collective-permute-done | bytes 196640 | tf_op jit(solution)/shard_map/ppermute | solution.py:73
  315.6 14.8 %attend_back.3 = (bf16[16,96,1536]{2,1,0:T(8,128)(2,1)}, bf16[8,96,1536]{2,1,0:T(8,128)(2,1)}, bf16[8,96,1536]{2,1,0:T(8,128)(2,1)}, bf16[32,48,64]{2,1,0:T(8,12...) custom-call(s32[32]{0:T(128)} %scatter_custom_fusion.order_ref, s32[32]{0:T(128)} %shift-left_add_fusion.place_ref, ...), custom_call_target="tpu_custom_call" | custom-call | flops 2000000000 | bytes 20000000 | tf_op jit(solution)/shard_map/attend_back/pallas_call | solution.py:787
  334.9 9.6 %all-to-all-done.1.got_ref = bf16[8,192,384]{2,1,0:T(8,128)(2,1)S(1)} async-done(((bf16[8,192,384]{2,1,0:T(8,128)(2,1)}), bf16[8,192,384]{2,1,0:T(8,128)(2,1)S(1)}, u32[]{:S(2)}, u32[]{:S(2)}) %all-to-all-start.1) | async-done | bytes 1179680 | tf_op jit(solution)/shard_map/all_to_all | solution.py:969
  345.2 23.3 %attend_back.4 = (bf16[16,96,1536]{2,1,0:T(8,128)(2,1)}, bf16[8,96,1536]{2,1,0:T(8,128)(2,1)}, bf16[8,96,1536]{2,1,0:T(8,128)(2,1)}, bf16[32,48,64]{2,1,0:T(8,12...) custom-call(s32[32]{0:T(128)} %scatter_custom_fusion.order_ref, ...), custom_call_target="tpu_custom_call", output_to_operand_aliasing={{0}: (21, {}), {1}: (22, {}), {2}: (23, {})} | custom-call | flops 40000000000 | bytes 20000000 | tf_op jit(solution)/shard_map/attend_back/pallas_call | solution.py:787
  377.6 14.9 %attend_back.5 = (bf16[16,96,1536]{2,1,0:T(8,128)(2,1)}, bf16[8,96,1536]{2,1,0:T(8,128)(2,1)}, bf16[8,96,1536]{2,1,0:T(8,128)(2,1)}, bf16[32,48,64]{2,1,0:T(8,12...) custom-call(s32[32]{0:T(128)} %scatter_custom_fusion.order_ref, ...), custom_call_target="tpu_custom_call", output_to_operand_aliasing={{0}: (21, {}), {1}: (22, {}), {2}: (23, {})} | custom-call | flops 30000001024 | bytes 20000000 | tf_op jit(solution)/shard_map/attend_back/pallas_call | solution.py:787
  481.4 10.3 %collective-permute-done.71 = bf16[1,96,1536]{2,1,0:T(8,128)(2,1)S(1)} collective-permute-done((bf16[1,96,1536]{2,1,0:T(8,128)(2,1)S(1)}, bf16[1,96,1536]{2,1,0:T(8,128)(2,1)S(1)}, u32[]{:S(2)}, u32[]{:S(2)}) %collective-permute-start.71) | collective-permute-done | bytes 294944 | tf_op jit(solution)/shard_map/ppermute | solution.py:73
  (440 shorter events, 259.8 us)
Async XLA Ops:
  29.5 14.3 %collective-permute-start.5 = (bf16[2,96,1536]{2,1,0:T(8,128)(2,1)S(1)}, bf16[2,96,1536]{2,1,0:T(8,128)(2,1)}, u32[]{:S(2)}, u32[]{:S(2)}) collective-permute-start(bf16[2,96,1536]{2,1,0:T(8,128)(2,1)S(1)} %pad_maximum_fusion.2), channel_id=1, source_target_pairs={{0,8},{1,9},{2,10},{3,11},{4,12},{5,13},{6,14},{7,15},{8,0},{9,1},... | collective-permute-start | bytes 1769480 | tf_op jit(solution)/shard_map/ppermute | solution.py:73
  46.1 28.4 %collective-permute-start.12 = (bf16[4,96,1536]{2,1,0:T(8,128)(2,1)}, bf16[4,96,1536]{2,1,0:T(8,128)(2,1)}, u32[]{:S(2)}, u32[]{:S(2)}) collective-permute-start(bf16[4,96,1536]{2,1,0:T(8,128)(2,1)} %pad_maximum_fusion.refs_0_.refs_7_), channel_id=1, source_target_pairs={{0,4},{1,3},{2,6},{3,1},{4,0},{5,7},{6,2},{7,5},{8,12},{9,11},{10,... | collective-permute-start | bytes 3538952 | tf_op jit(solution)/shard_map/ppermute | solution.py:73
  47.7 28.1 %collective-permute-start.13 = (bf16[4,96,1536]{2,1,0:T(8,128)(2,1)}, bf16[4,96,1536]{2,1,0:T(8,128)(2,1)}, u32[]{:S(2)}, u32[]{:S(2)}) collective-permute-start(bf16[4,96,1536]{2,1,0:T(8,128)(2,1)} %pad_maximum_fusion.refs_0_.refs_7_), channel_id=1, source_target_pairs={{0,2},{1,5},{2,0},{3,7},{4,6},{5,1},{6,4},{7,3},{8,10},{9,13},{10,... | collective-permute-start | bytes 3538952 | tf_op jit(solution)/shard_map/ppermute | solution.py:73
  49.2 52.8 %collective-permute-start.15 = (bf16[4,96,1536]{2,1,0:T(8,128)(2,1)}, bf16[4,96,1536]{2,1,0:T(8,128)(2,1)}, u32[]{:S(2)}, u32[]{:S(2)}) collective-permute-start(bf16[4,96,1536]{2,1,0:T(8,128)(2,1)} %pad_maximum_fusion.refs_0_.refs_7_), channel_id=1, source_target_pairs={{0,1},{1,0},{2,3},{3,2},{4,5},{5,4},{6,7},{7,6},{8,9},{9,8},{10,11... | collective-permute-start | bytes 3538952 | tf_op jit(solution)/shard_map/ppermute | solution.py:73
  69.7 14.6 %collective-permute-start.18 = (bf16[1,96,1536]{2,1,0:T(8,128)(2,1)S(1)}, bf16[1,96,1536]{2,1,0:T(8,128)(2,1)S(1)}, u32[]{:S(2)}, u32[]{:S(2)}) collective-permute-start(bf16[1,96,1536]{2,1,0:T(8,128)(2,1)S(1)} %bitcast.122), channel_id=1, source_target_pairs={{0,16},{1,17},{2,18},{3,19},{4,20},{5,21},{6,22},{7,23},{8,24},{9,... | collective-permute-start | bytes 884744 | tf_op jit(solution)/shard_map/ppermute | solution.py:73
  75.8 25.6 %collective-permute-start.14 = (bf16[4,96,1536]{2,1,0:T(8,128)(2,1)}, bf16[4,96,1536]{2,1,0:T(8,128)(2,1)S(1)}, u32[]{:S(2)}, u32[]{:S(2)}) collective-permute-start(bf16[4,96,1536]{2,1,0:T(8,128)(2,1)} %collective-permute-done.12.refs_1_.refs_8_), channel_id=1, source_target_pairs={{0,2},{1,5},{2,0},{3,7},{4,6},{5,1},{6,4},{7,3},{8,10},{9,13},{10,... | collective-permute-start | bytes 3538952 | tf_op jit(solution)/shard_map/ppermute | solution.py:73
  85.3 14.4 %collective-permute-start.19 = (bf16[2,96,1536]{2,1,0:T(8,128)(2,1)S(1)}, bf16[2,96,1536]{2,1,0:T(8,128)(2,1)}, u32[]{:S(2)}, u32[]{:S(2)}) collective-permute-start(bf16[2,96,1536]{2,1,0:T(8,128)(2,1)S(1)} %pad_maximum_fusion.3), channel_id=1, source_target_pairs={{0,8},{1,9},{2,10},{3,11},{4,12},{5,13},{6,14},{7,15},{8,0},{9,1},... | collective-permute-start | bytes 1769480 | tf_op jit(solution)/shard_map/ppermute | solution.py:73
  101.5 28.8 %collective-permute-start.24 = (bf16[4,96,1536]{2,1,0:T(8,128)(2,1)S(1)}, bf16[4,96,1536]{2,1,0:T(8,128)(2,1)}, u32[]{:S(2)}, u32[]{:S(2)}) collective-permute-start(bf16[4,96,1536]{2,1,0:T(8,128)(2,1)S(1)} %constant_dynamic-update-slice_fusion.11.refs_4_.refs_0_), channel_id=1, source_target_pairs={{0,4},{1,3},{2,6},{3,1},{4,0},{5,7},{6,2},{7,5},{8,12},{9,11},{10,... | collective-permute-start | bytes 3538952 | tf_op jit(solution)/shard_map/ppermute | solution.py:73
  102.0 28.2 %collective-permute-start.25 = (bf16[4,96,1536]{2,1,0:T(8,128)(2,1)S(1)}, bf16[4,96,1536]{2,1,0:T(8,128)(2,1)}, u32[]{:S(2)}, u32[]{:S(2)}) collective-permute-start(bf16[4,96,1536]{2,1,0:T(8,128)(2,1)S(1)} %constant_dynamic-update-slice_fusion.11.refs_4_.refs_0_), channel_id=1, source_target_pairs={{0,2},{1,5},{2,0},{3,7},{4,6},{5,1},{6,4},{7,3},{8,10},{9,13},{10,... | collective-permute-start | bytes 3538952 | tf_op jit(solution)/shard_map/ppermute | solution.py:73
  130.2 23.6 %collective-permute-start.26 = (bf16[4,96,1536]{2,1,0:T(8,128)(2,1)}, bf16[4,96,1536]{2,1,0:T(8,128)(2,1)}, u32[]{:S(2)}, u32[]{:S(2)}) collective-permute-start(bf16[4,96,1536]{2,1,0:T(8,128)(2,1)} %collective-permute-done.24.refs_5_.refs_1_), channel_id=1, source_target_pairs={{0,2},{1,5},{2,0},{3,7},{4,6},{5,1},{6,4},{7,3},{8,10},{9,13},{10,... | collective-permute-start | bytes 3538952 | tf_op jit(solution)/shard_map/ppermute | solution.py:73
  131.5 37.0 %all-to-all-start = ((bf16[8,192,384]{2,1,0:T(8,128)(2,1)}), bf16[8,192,384]{2,1,0:T(8,128)(2,1)S(1)}, u32[]{:S(2)}, u32[]{:S(2)}) async-start(bf16[8,192,384]{2,1,0:T(8,128)(2,1)} %pad_maximum_fusion.1), calls=%async_computation | async-start | bytes 2359296 | tf_op jit(solution)/shard_map/all_to_all | solution.py:937
  142.5 14.3 %collective-permute-start.27 = (bf16[4,96,1536]{2,1,0:T(8,128)(2,1)S(1)}, bf16[4,96,1536]{2,1,0:T(8,128)(2,1)S(1)}, u32[]{:S(2)}, u32[]{:S(2)}) collective-permute-start(bf16[4,96,1536]{2,1,0:T(8,128)(2,1)S(1)} %constant_dynamic-update-slice_fusion.11.refs_4_.refs_0_), channel_id=1, source_target_pairs={{0,1},{1,0},{2,3},{3,2},{4,5},{5,4},{6,7},{7,6},{8,9},{9,8},{10,11... | collective-permute-start | bytes 3538952 | tf_op jit(solution)/shard_map/ppermute | solution.py:73
  142.8 15.1 %collective-permute-start.28 = (bf16[4,96,1536]{2,1,0:T(8,128)(2,1)}, bf16[4,96,1536]{2,1,0:T(8,128)(2,1)S(1)}, u32[]{:S(2)}, u32[]{:S(2)}) collective-permute-start(bf16[4,96,1536]{2,1,0:T(8,128)(2,1)} %collective-permute-done.24.refs_5_.refs_1_), channel_id=1, source_target_pairs={{0,1},{1,0},{2,3},{3,2},{4,5},{5,4},{6,7},{7,6},{8,9},{9,8},{10,11... | collective-permute-start | bytes 3538952 | tf_op jit(solution)/shard_map/ppermute | solution.py:73
  190.1 16.4 %collective-permute-start.34 = (bf16[4,48,1536]{2,1,0:T(8,128)(2,1)S(1)}, bf16[4,48,1536]{2,1,0:T(8,128)(2,1)S(1)}, u32[]{:S(2)}, u32[]{:S(2)}) collective-permute-start(bf16[4,48,1536]{2,1,0:T(8,128)(2,1)S(1)} %pad_maximum_fusion.4.refs_0_), channel_id=1, source_target_pairs={{0,4},{1,3},{2,6},{3,1},{4,0},{5,7},{6,2},{7,5},{8,12},{9,11},{10,... | collective-permute-start | bytes 1769480 | tf_op jit(solution)/shard_map/ppermute | solution.py:73
  228.7 20.0 %collective-permute-start.40 = (bf16[8,48,1536]{2,1,0:T(8,128)(2,1)}, bf16[8,48,1536]{2,1,0:T(8,128)(2,1)}, u32[]{:S(2)}, u32[]{:S(2)}) collective-permute-start(bf16[8,48,1536]{2,1,0:T(8,128)(2,1)} %get-tuple-element.149), channel_id=1, source_target_pairs={{0,1},{1,0},{2,3},{3,2},{4,5},{5,4},{6,7},{7,6},{8,9},{9,8},{10,11... | collective-permute-start | bytes 3538952 | tf_op jit(solution)/shard_map/ppermute | solution.py:73
  240.0 16.3 %collective-permute-start.42 = (bf16[8,48,1536]{2,1,0:T(8,128)(2,1)S(1)}, bf16[8,48,1536]{2,1,0:T(8,128)(2,1)S(1)}, u32[]{:S(2)}, u32[]{:S(2)}) collective-permute-start(bf16[8,48,1536]{2,1,0:T(8,128)(2,1)S(1)} %add_convert_fusion.4), channel_id=1, source_target_pairs={{0,2},{1,5},{2,0},{3,7},{4,6},{5,1},{6,4},{7,3},{8,10},{9,13},{10,... | collective-permute-start | bytes 3538952 | tf_op jit(solution)/shard_map/ppermute | solution.py:73
  310.1 20.3 %collective-permute-start.49 = (bf16[8,96,1536]{2,1,0:T(8,128)(2,1)}, bf16[8,96,1536]{2,1,0:T(8,128)(2,1)}, u32[]{:S(2)}, u32[]{:S(2)}) collective-permute-start(bf16[8,96,1536]{2,1,0:T(8,128)(2,1)} %get-tuple-element.184), channel_id=1, source_target_pairs={{0,1},{1,0},{2,3},{3,2},{4,5},{5,4},{6,7},{7,6},{8,9},{9,8},{10,11... | collective-permute-start | bytes 7077896 | tf_op jit(solution)/shard_map/ppermute | solution.py:73
  310.5 19.9 %collective-permute-start.50 = (bf16[8,96,1536]{2,1,0:T(8,128)(2,1)}, bf16[8,96,1536]{2,1,0:T(8,128)(2,1)}, u32[]{:S(2)}, u32[]{:S(2)}) collective-permute-start(bf16[8,96,1536]{2,1,0:T(8,128)(2,1)} %get-tuple-element.186), channel_id=1, source_target_pairs={{0,1},{1,0},{2,3},{3,2},{4,5},{5,4},{6,7},{7,6},{8,9},{9,8},{10,11... | collective-permute-start | bytes 7077896 | tf_op jit(solution)/shard_map/ppermute | solution.py:73
  310.7 33.8 %all-to-all-start.1 = ((bf16[8,192,384]{2,1,0:T(8,128)(2,1)}), bf16[8,192,384]{2,1,0:T(8,128)(2,1)S(1)}, u32[]{:S(2)}, u32[]{:S(2)}) async-start(bf16[8,192,384]{2,1,0:T(8,128)(2,1)} %pack_back.1), calls=%async_computation.1 | async-start | bytes 2359296 | tf_op jit(solution)/shard_map/all_to_all | solution.py:969
  344.5 29.2 %collective-permute-start.51 = (bf16[8,96,1536]{2,1,0:T(8,128)(2,1)}, bf16[8,96,1536]{2,1,0:T(8,128)(2,1)}, u32[]{:S(2)}, u32[]{:S(2)}) collective-permute-start(bf16[8,96,1536]{2,1,0:T(8,128)(2,1)} %add_convert_fusion.1), channel_id=1, source_target_pairs={{0,2},{1,5},{2,0},{3,7},{4,6},{5,1},{6,4},{7,3},{8,10},{9,13},{10,... | collective-permute-start | bytes 7077896 | tf_op jit(solution)/shard_map/ppermute | solution.py:73
  376.1 17.6 %collective-permute-start.52 = (bf16[4,96,1536]{2,1,0:T(8,128)(2,1)S(1)}, bf16[4,96,1536]{2,1,0:T(8,128)(2,1)S(1)}, u32[]{:S(2)}, u32[]{:S(2)}) collective-permute-start(bf16[4,96,1536]{2,1,0:T(8,128)(2,1)S(1)} %add_convert_fusion.3), channel_id=1, source_target_pairs={{0,4},{1,3},{2,6},{3,1},{4,0},{5,7},{6,2},{7,5},{8,12},{9,11},{10,... | collective-permute-start | bytes 3538952 | tf_op jit(solution)/shard_map/ppermute | solution.py:73
  408.8 30.3 %collective-permute-start.63 = (bf16[8,96,1536]{2,1,0:T(8,128)(2,1)S(1)}, bf16[8,96,1536]{2,1,0:T(8,128)(2,1)}, u32[]{:S(2)}, u32[]{:S(2)}) collective-permute-start(bf16[8,96,1536]{2,1,0:T(8,128)(2,1)S(1)} %add_convert_fusion), channel_id=1, source_target_pairs={{0,2},{1,5},{2,0},{3,7},{4,6},{5,1},{6,4},{7,3},{8,10},{9,13},{10,... | collective-permute-start | bytes 7077896 | tf_op jit(solution)/shard_map/ppermute | solution.py:73
  437.5 15.1 %collective-permute-start.56 = (bf16[1,96,1536]{2,1,0:T(8,128)(2,1)S(1)}, bf16[1,96,1536]{2,1,0:T(8,128)(2,1)S(1)}, u32[]{:S(2)}, u32[]{:S(2)}) collective-permute-start(bf16[1,96,1536]{2,1,0:T(8,128)(2,1)S(1)} %add_convert_fusion.9), channel_id=1, source_target_pairs={{0,16},{1,17},{2,18},{3,19},{4,20},{5,21},{6,22},{7,23},{8,24},{9,... | collective-permute-start | bytes 884744 | tf_op jit(solution)/shard_map/ppermute | solution.py:73
  442.5 17.7 %collective-permute-start.69 = (bf16[4,96,1536]{2,1,0:T(8,128)(2,1)S(1)}, bf16[4,96,1536]{2,1,0:T(8,128)(2,1)S(1)}, u32[]{:S(2)}, u32[]{:S(2)}) collective-permute-start(bf16[4,96,1536]{2,1,0:T(8,128)(2,1)S(1)} %add_convert_fusion.2), channel_id=1, source_target_pairs={{0,4},{1,3},{2,6},{3,1},{4,0},{5,7},{6,2},{7,5},{8,12},{9,11},{10,... | collective-permute-start | bytes 3538952 | tf_op jit(solution)/shard_map/ppermute | solution.py:73
  (132 other events, 1213.2 us)

commit v5 on v4

--- a/solution.py
+++ b/solution.py
@@ -689,12 +689,7 @@
     head_dim = weight_ref.shape[1]
     own_rows = own_ref.shape[0]
 
-    def out_wait():
-        for slot in range(2 * group):
-            pltpu.make_async_copy(out_ref.at[slot], keep_ref.at[0], out_sem_ref.at[slot]).wait()
-
-    @pl.when(step == 0)
-    def _():
+    def weight_loads():
         loads_here = []
         for part in parts:
             for k in range(part.shape[0]):
@@ -704,14 +699,25 @@
                 here = (head >= first) & (head < first + count)
                 to = jnp.where(here, head - first + jnp.where(block >= heads, count, 0), 0)
                 copy = pltpu.make_async_copy(part.at[k], weight_ref.at[to], sem_ref.at[n])
-                loads_here.append((here, copy))
-        for here, c in loads_here:
-            pl.when(here)(c.start)
+                loads_here.append((here, block >= heads, copy))
+        return loads_here
+
+    def out_wait():
+        for slot in range(2 * group):
+            pltpu.make_async_copy(out_ref.at[slot], keep_ref.at[0], out_sem_ref.at[slot]).wait()
+
+    @pl.when(step == 0)
+    def _():
+        loads_here = weight_loads()
+        for here, value, c in loads_here:
+            pl.when(here & value)(c.start)
+        for here, value, c in loads_here:
+            pl.when(here & ~value)(c.start)
         grad_media_ref[...] = jnp.zeros_like(grad_media_ref)
         grad_own_ref[...] = jnp.zeros_like(grad_own_ref)
         query_part_ref[...] = jnp.zeros_like(query_part_ref)
-        for here, c in loads_here:
-            pl.when(here)(c.wait)
+        for here, value, c in loads_here:
+            pl.when(here & value)(c.wait)
 
     columns = []
     for j in range(group):
@@ -754,6 +760,12 @@
     key_mix_ref[...] = (key_mix * factor).astype(BF)
     per = query_part_ref.shape[0] // heads
     pl.when(step > 0)(out_wait)
+
+    @pl.when(step == 0)
+    def _():
+        for here, value, c in weight_loads():
+            pl.when(here & ~value)(c.wait)
+
     for j in range(group):
         h = step * group + j
         mixed = key_mix_ref[j * lat : (j + 1) * lat, :]

time: 502 us -> 503 us (level)
  no operation moved by 1% of the time
where the time goes in v5:
time: 503 us; the launch traced here: 495 us
  waiting for transfers between devices  162 us (32%)
  Pallas kernels  132 us (26%)
  starting transfers between devices  84.9 us (17%)
  other arithmetic  65.2 us (13%)
  local copies, waits for them, and re-layouts  43.8 us (9%)
    ppermute x72, waiting for transfers between devices, send(): return lax.ppermute(value, BOTH, perm)  152 us
    ppermute x72, starting transfers between devices, send(): return lax.ppermute(value, BOTH, perm)  73.3 us
    pallas_call x3, Pallas kernels, attend_back(): pl.pallas_call(functools.partial(attend_back_kernel, sizes), grid=(count...  52.1 us
    convert_element_type x16, other arithmetic, step(): self.sum(half, self.size).astype(BF)  26.9 us
    pallas_call x1, Pallas kernels, attend(): pl.pallas_call(functools.partial(attend_kernel, (heads, group, seqs, lat,...  22.8 us
    unnamed x178, local copies, waits for them, and re-layouts  19.5 us
    pallas_call x2, Pallas kernels, feed(): pl.pallas_call(functools.partial(feed_kernel, count), in_specs=[whole(up....  18.4 us
    pallas_call x2, Pallas kernels, feed_rest(): pl.pallas_call(functools.partial(feed_rest_kernel, count), in_specs=[whol...  11.3 us
  transfers between devices with their start and end apart: 74, of which 39 were waited for; matrix products, arithmetic and copies ran while one was open for 17% of the time, Pallas kernels for 23%

profile of v5, /device:TPU:0, one launch (start us, length us, event | category | flops | bytes accessed | tf_op | source)
XLA Modules:
  0.0 494.9 jit_solution(1533764050893802572)
XLA Ops:
  18.9 9.6 %collective-permute-done.2 = bf16[1,96,1536]{2,1,0:T(8,128)(2,1)S(1)} collective-permute-done((bf16[1,96,1536]{2,1,0:T(8,128)(2,1)}, bf16[1,96,1536]{2,1,0:T(8,128)(2,1)S(1)}, u32[]{:S(2)}, u32[]{:S(2)}) %collective-permute-start.2) | collective-permute-done | bytes 294944 | tf_op jit(solution)/shard_map/ppermute | solution.py:73
  78.5 5.7 %collective-permute-done.18 = bf16[1,96,1536]{2,1,0:T(8,128)(2,1)S(1)} collective-permute-done((bf16[1,96,1536]{2,1,0:T(8,128)(2,1)S(1)}, bf16[1,96,1536]{2,1,0:T(8,128)(2,1)S(1)}, u32[]{:S(2)}, u32[]{:S(2)}) %collective-permute-start.18) | collective-permute-done | bytes 294944 | tf_op jit(solution)/shard_map/ppermute | solution.py:73
  86.8 7.5 %collective-permute-done.11 = bf16[16,48,64]{2,1,0:T(8,128)(2,1)S(1)} collective-permute-done((bf16[16,48,64]{2,1,0:T(8,128)(2,1)}, bf16[16,48,64]{2,1,0:T(8,128)(2,1)S(1)}, u32[]{:S(2)}, u32[]{:S(2)}) %collective-permute-start.11) | collective-permute-done | bytes 98336 | tf_op jit(solution)/shard_map/ppermute | solution.py:73
  107.5 22.8 %attend.1 = (bf16[1024,1536]{1,0:T(8,128)(2,1)}, f32[3,1024,256]{2,1,0:T(8,128)}, f32[1024,16]{1,0:T(8,128)}, f32[16,192,128]{2,1,0:T(8,128)}) custom-call(s32[32]{0:T(128)} %scatter_custom_fusion.order_ref, s32[3]{0:T(128)} %compare_convert_fusion.9.valid_ref, bf16[16,96,64]{2,1,0:T(8,128)(2,1)} %copy.94.query_ref, bf16[3,256,1536]{2,1,0:T(8,128)(2,1)} %fusion.8.media_ref, ...), custom_call_target="tpu_custom_call" | custom-call | flops 2000000000 | bytes 2000000 | tf_op jit(solution)/shard_map/attend/pallas_call | solution.py:304
  131.5 6.7 %all-to-all-start = ((bf16[8,192,384]{2,1,0:T(8,128)(2,1)}), bf16[8,192,384]{2,1,0:T(8,128)(2,1)S(1)}, u32[]{:S(2)}, u32[]{:S(2)}) async-start(bf16[8,192,384]{2,1,0:T(8,128)(2,1)} %pad_maximum_fusion.1), calls=%async_computation | async-start | bytes 2359296 | tf_op jit(solution)/shard_map/all_to_all | solution.py:949
  143.0 10.0 %collective-permute-done.22.refs_2_ = bf16[16,48,128]{2,1,0:T(8,128)(2,1)S(1)} collective-permute-done((bf16[16,48,128]{2,1,0:T(8,128)(2,1)S(1)}, bf16[16,48,128]{2,1,0:T(8,128)(2,1)S(1)}, u32[]{:S(2)}, u32[]{:S(2)}) %collective-permute-start.22) | collective-permute-done | bytes 196640 | tf_op jit(solution)/shard_map/ppermute | solution.py:73
  161.0 7.6 %mixer.1 = (f32[48,1536]{1,0:T(8,128)}, f32[48,1536]{1,0:T(8,128)}, bf16[48,1536]{1,0:T(8,128)(2,1)}, f32[16,48,128]{2,1,0:T(8,128)}, bf16[48,1536]{1,0:T(8,128)(2,1)}) custom-call(s32[32]{0:T(128)} %scatter_custom_fusion.order_ref, f32[16,1536]{1,0:T(8,128)} %constant_dynamic-slice_fusion.1.latent_ref, f32[1,1536]{1,0:T(1,128)} %get-tuple-element.298.gain_ref, ...), custom_call_target="tpu_custom_call" | custom-call | flops 1000000 | bytes 1000000 | tf_op jit(solution)/shard_map/mixer/pallas_call | solution.py:369
  172.3 7.4 %collective-permute-done.31 = bf16[1,48,1536]{2,1,0:T(8,128)(2,1)S(1)} collective-permute-done((bf16[1,48,1536]{2,1,0:T(8,128)(2,1)}, bf16[1,48,1536]{2,1,0:T(8,128)(2,1)S(1)}, u32[]{:S(2)}, u32[]{:S(2)}) %collective-permute-start.31) | collective-permute-done | bytes 147488 | tf_op jit(solution)/shard_map/ppermute | solution.py:73
  181.5 7.6 %collective-permute-done.32 = bf16[2,48,1536]{2,1,0:T(8,128)(2,1)S(1)} collective-permute-done((bf16[2,48,1536]{2,1,0:T(8,128)(2,1)S(1)}, bf16[2,48,1536]{2,1,0:T(8,128)(2,1)S(1)}, u32[]{:S(2)}, u32[]{:S(2)}) %collective-permute-start.32) | collective-permute-done | bytes 294944 | tf_op jit(solution)/shard_map/ppermute | solution.py:73
  196.6 9.9 %collective-permute-done.34.refs_1_ = bf16[4,48,1536]{2,1,0:T(8,128)(2,1)S(1)} collective-permute-done((bf16[4,48,1536]{2,1,0:T(8,128)(2,1)S(1)}, bf16[4,48,1536]{2,1,0:T(8,128)(2,1)S(1)}, u32[]{:S(2)}, u32[]{:S(2)}) %collective-permute-start.34) | collective-permute-done | bytes 589856 | tf_op jit(solution)/shard_map/ppermute | solution.py:73
  208.0 8.4 %collective-permute-done.38.refs_3_ = bf16[4,48,1536]{2,1,0:T(8,128)(2,1)S(1)} collective-permute-done((bf16[4,48,1536]{2,1,0:T(8,128)(2,1)S(1)}, bf16[4,48,1536]{2,1,0:T(8,128)(2,1)S(1)}, u32[]{:S(2)}, u32[]{:S(2)}) %collective-permute-start.38) | collective-permute-done | bytes 589856 | tf_op jit(solution)/shard_map/ppermute | solution.py:73
  219.3 9.2 %feed.2 = (bf16[768,192]{1,0:T(8,128)(2,1)}, bf16[768,192]{1,0:T(8,128)(2,1)}, bf16[8,48,1536]{2,1,0:T(8,128)(2,1)}, bf16[8,48,1536]{2,1,0:T(8,128)(2,1)}) custom-call(bf16[192,1536]{1,0:T(8,128)(2,1)} %get-tuple-element.142.up_ref, bf16[192,1536]{1,0:T(8,128)(2,1)} %get-tuple-element.143.down_ref, bf16[4,48,1536]{2,1,0:T(8,128)(2,1)} %copy-done.14, ...), custom_call_target="tpu_custom_call" | custom-call | flops 5000000000 | bytes 8000000 | tf_op jit(solution)/shard_map/feed/pallas_call | solution.py:605
  229.1 9.2 %feed.3 = (bf16[768,192]{1,0:T(8,128)(2,1)}, bf16[768,192]{1,0:T(8,128)(2,1)}, bf16[16,48,1536]{2,1,0:T(8,128)(2,1)}) custom-call(bf16[192,1536]{1,0:T(8,128)(2,1)} %get-tuple-element.142.up_ref, bf16[192,1536]{1,0:T(8,128)(2,1)} %get-tuple-element.143.down_ref, bf16[4,48,1536]{2,1,0:T(8,128)(2,1)} %copy-done.5, bf16[4,48,1536]{2,1,0:T(8,128)(2,1)} %copy-done.7, ...), custom_call_target="tpu_custom_call" | custom-call | flops 5000000000 | bytes 8000000 | tf_op jit(solution)/shard_map/feed/pallas_call | solution.py:605
  248.7 7.6 %collective-permute-done.42 = bf16[8,48,1536]{2,1,0:T(8,128)(2,1)S(1)} collective-permute-done((bf16[8,48,1536]{2,1,0:T(8,128)(2,1)S(1)}, bf16[8,48,1536]{2,1,0:T(8,128)(2,1)S(1)}, u32[]{:S(2)}, u32[]{:S(2)}) %collective-permute-start.42) | collective-permute-done | bytes 1179680 | tf_op jit(solution)/shard_map/ppermute | solution.py:73
  259.8 5.8 %feed_rest.3 = (f32[192,1536]{1,0:T(8,128)S(1)}, f32[192,1536]{1,0:T(8,128)S(1)}, bf16[16,96,1536]{2,1,0:T(8,128)(2,1)}) custom-call(bf16[192,1536]{1,0:T(8,128)(2,1)S(1)} %copy-done.11, bf16[768,192]{1,0:T(8,128)(2,1)S(1)} %copy-done.22, bf16[768,192]{1,0:T(8,128)(2,1)S(1)} %copy-done.23, bf16[4,48,1536]{2,1,0:T(8,128)(2,1)S(1)} %copy-done.6, ...), custom_call_target="tpu_custom_call" | custom-call | flops 5000000000 | bytes 8000000 | tf_op jit(solution)/shard_map/feed_rest/pallas_call | solution.py:653
  269.9 6.6 %collective-permute-done.44 = bf16[2,48,1536]{2,1,0:T(8,128)(2,1)S(1)} collective-permute-done((bf16[2,48,1536]{2,1,0:T(8,128)(2,1)S(1)}, bf16[2,48,1536]{2,1,0:T(8,128)(2,1)S(1)}, u32[]{:S(2)}, u32[]{:S(2)}) %collective-permute-start.44) | collective-permute-done | bytes 294944 | tf_op jit(solution)/shard_map/ppermute | solution.py:73
  288.1 6.6 %unmix.1 = (bf16[16,48,128]{2,1,0:T(8,128)(2,1)}, f32[48,1536]{1,0:T(8,128)}, bf16[48,1536]{1,0:T(8,128)(2,1)}, f32[1,1536]{1,0:T(1,128)}, f32[16,1536]{1,0:T(8,128)}) custom-call(s32[32]{0:T(128)} %scatter_custom_fusion.order_ref, f32[48,1536]{1,0:T(8,128)} %add_bitcast_fusion.1.grad_feed_ref, f32[48,1536]{1,0:T(8,128)} %bitcast.117, ...), custom_call_target="tpu_custom_call" | custom-call | flops 2000000000 | bytes 8000000 | tf_op jit(solution)/shard_map/unmix/pallas_call | solution.py:432
  297.2 5.6 %collective-permute-done.47.refs_2_ = bf16[16,48,128]{2,1,0:T(8,128)(2,1)S(1)} collective-permute-done((bf16[16,48,128]{2,1,0:T(8,128)(2,1)}, bf16[16,48,128]{2,1,0:T(8,128)(2,1)S(1)}, u32[]{:S(2)}, u32[]{:S(2)}) %collective-permute-start.47) | collective-permute-done | bytes 196640 | tf_op jit(solution)/shard_map/ppermute | solution.py:73
  315.6 14.6 %attend_back.3 = (bf16[16,96,1536]{2,1,0:T(8,128)(2,1)}, bf16[8,96,1536]{2,1,0:T(8,128)(2,1)}, bf16[8,96,1536]{2,1,0:T(8,128)(2,1)}, bf16[32,48,64]{2,1,0:T(8,12...) custom-call(s32[32]{0:T(128)} %scatter_custom_fusion.order_ref, s32[32]{0:T(128)} %shift-left_add_fusion.place_ref, ...), custom_call_target="tpu_custom_call" | custom-call | flops 2000000000 | bytes 20000000 | tf_op jit(solution)/shard_map/attend_back/pallas_call | solution.py:799
  334.7 9.8 %all-to-all-done.1.got_ref = bf16[8,192,384]{2,1,0:T(8,128)(2,1)S(1)} async-done(((bf16[8,192,384]{2,1,0:T(8,128)(2,1)}), bf16[8,192,384]{2,1,0:T(8,128)(2,1)S(1)}, u32[]{:S(2)}, u32[]{:S(2)}) %all-to-all-start.1) | async-done | bytes 1179680 | tf_op jit(solution)/shard_map/all_to_all | solution.py:981
  345.2 22.8 %attend_back.4 = (bf16[16,96,1536]{2,1,0:T(8,128)(2,1)}, bf16[8,96,1536]{2,1,0:T(8,128)(2,1)}, bf16[8,96,1536]{2,1,0:T(8,128)(2,1)}, bf16[32,48,64]{2,1,0:T(8,12...) custom-call(s32[32]{0:T(128)} %scatter_custom_fusion.order_ref, ...), custom_call_target="tpu_custom_call", output_to_operand_aliasing={{0}: (21, {}), {1}: (22, {}), {2}: (23, {})} | custom-call | flops 40000000000 | bytes 20000000 | tf_op jit(solution)/shard_map/attend_back/pallas_call | solution.py:799
  368.0 5.7 %collective-permute-done.51 = bf16[8,96,1536]{2,1,0:T(8,128)(2,1)} collective-permute-done((bf16[8,96,1536]{2,1,0:T(8,128)(2,1)}, bf16[8,96,1536]{2,1,0:T(8,128)(2,1)}, u32[]{:S(2)}, u32[]{:S(2)}) %collective-permute-start.51) | collective-permute-done | bytes 2359328 | tf_op jit(solution)/shard_map/ppermute | solution.py:73
  377.6 14.7 %attend_back.5 = (bf16[16,96,1536]{2,1,0:T(8,128)(2,1)}, bf16[8,96,1536]{2,1,0:T(8,128)(2,1)}, bf16[8,96,1536]{2,1,0:T(8,128)(2,1)}, bf16[32,48,64]{2,1,0:T(8,12...) custom-call(s32[32]{0:T(128)} %scatter_custom_fusion.order_ref, ...), custom_call_target="tpu_custom_call", output_to_operand_aliasing={{0}: (21, {}), {1}: (22, {}), {2}: (23, {})} | custom-call | flops 30000001024 | bytes 20000000 | tf_op jit(solution)/shard_map/attend_back/pallas_call | solution.py:799
  481.1 11.0 %collective-permute-done.71 = bf16[1,96,1536]{2,1,0:T(8,128)(2,1)S(1)} collective-permute-done((bf16[1,96,1536]{2,1,0:T(8,128)(2,1)S(1)}, bf16[1,96,1536]{2,1,0:T(8,128)(2,1)S(1)}, u32[]{:S(2)}, u32[]{:S(2)}) %collective-permute-start.71) | collective-permute-done | bytes 294944 | tf_op jit(solution)/shard_map/ppermute | solution.py:73
  (440 shorter events, 260.1 us)
Async XLA Ops:
  46.1 28.4 %collective-permute-start.12 = (bf16[4,96,1536]{2,1,0:T(8,128)(2,1)}, bf16[4,96,1536]{2,1,0:T(8,128)(2,1)}, u32[]{:S(2)}, u32[]{:S(2)}) collective-permute-start(bf16[4,96,1536]{2,1,0:T(8,128)(2,1)} %pad_maximum_fusion.refs_0_.refs_7_), channel_id=1, source_target_pairs={{0,4},{1,3},{2,6},{3,1},{4,0},{5,7},{6,2},{7,5},{8,12},{9,11},{10,... | collective-permute-start | bytes 3538952 | tf_op jit(solution)/shard_map/ppermute | solution.py:73
  47.7 28.1 %collective-permute-start.13 = (bf16[4,96,1536]{2,1,0:T(8,128)(2,1)}, bf16[4,96,1536]{2,1,0:T(8,128)(2,1)}, u32[]{:S(2)}, u32[]{:S(2)}) collective-permute-start(bf16[4,96,1536]{2,1,0:T(8,128)(2,1)} %pad_maximum_fusion.refs_0_.refs_7_), channel_id=1, source_target_pairs={{0,2},{1,5},{2,0},{3,7},{4,6},{5,1},{6,4},{7,3},{8,10},{9,13},{10,... | collective-permute-start | bytes 3538952 | tf_op jit(solution)/shard_map/ppermute | solution.py:73
  49.2 52.8 %collective-permute-start.15 = (bf16[4,96,1536]{2,1,0:T(8,128)(2,1)}, bf16[4,96,1536]{2,1,0:T(8,128)(2,1)}, u32[]{:S(2)}, u32[]{:S(2)}) collective-permute-start(bf16[4,96,1536]{2,1,0:T(8,128)(2,1)} %pad_maximum_fusion.refs_0_.refs_7_), channel_id=1, source_target_pairs={{0,1},{1,0},{2,3},{3,2},{4,5},{5,4},{6,7},{7,6},{8,9},{9,8},{10,11... | collective-permute-start | bytes 3538952 | tf_op jit(solution)/shard_map/ppermute | solution.py:73
  69.7 14.6 %collective-permute-start.18 = (bf16[1,96,1536]{2,1,0:T(8,128)(2,1)S(1)}, bf16[1,96,1536]{2,1,0:T(8,128)(2,1)S(1)}, u32[]{:S(2)}, u32[]{:S(2)}) collective-permute-start(bf16[1,96,1536]{2,1,0:T(8,128)(2,1)S(1)} %bitcast.122), channel_id=1, source_target_pairs={{0,16},{1,17},{2,18},{3,19},{4,20},{5,21},{6,22},{7,23},{8,24},{9,... | collective-permute-start | bytes 884744 | tf_op jit(solution)/shard_map/ppermute | solution.py:73
  75.8 25.6 %collective-permute-start.14 = (bf16[4,96,1536]{2,1,0:T(8,128)(2,1)}, bf16[4,96,1536]{2,1,0:T(8,128)(2,1)S(1)}, u32[]{:S(2)}, u32[]{:S(2)}) collective-permute-start(bf16[4,96,1536]{2,1,0:T(8,128)(2,1)} %collective-permute-done.12.refs_1_.refs_8_), channel_id=1, source_target_pairs={{0,2},{1,5},{2,0},{3,7},{4,6},{5,1},{6,4},{7,3},{8,10},{9,13},{10,... | collective-permute-start | bytes 3538952 | tf_op jit(solution)/shard_map/ppermute | solution.py:73
  85.3 14.4 %collective-permute-start.19 = (bf16[2,96,1536]{2,1,0:T(8,128)(2,1)S(1)}, bf16[2,96,1536]{2,1,0:T(8,128)(2,1)}, u32[]{:S(2)}, u32[]{:S(2)}) collective-permute-start(bf16[2,96,1536]{2,1,0:T(8,128)(2,1)S(1)} %pad_maximum_fusion.3), channel_id=1, source_target_pairs={{0,8},{1,9},{2,10},{3,11},{4,12},{5,13},{6,14},{7,15},{8,0},{9,1},... | collective-permute-start | bytes 1769480 | tf_op jit(solution)/shard_map/ppermute | solution.py:73
  101.5 28.8 %collective-permute-start.24 = (bf16[4,96,1536]{2,1,0:T(8,128)(2,1)S(1)}, bf16[4,96,1536]{2,1,0:T(8,128)(2,1)}, u32[]{:S(2)}, u32[]{:S(2)}) collective-permute-start(bf16[4,96,1536]{2,1,0:T(8,128)(2,1)S(1)} %constant_dynamic-update-slice_fusion.11.refs_4_.refs_0_), channel_id=1, source_target_pairs={{0,4},{1,3},{2,6},{3,1},{4,0},{5,7},{6,2},{7,5},{8,12},{9,11},{10,... | collective-permute-start | bytes 3538952 | tf_op jit(solution)/shard_map/ppermute | solution.py:73
  102.0 28.2 %collective-permute-start.25 = (bf16[4,96,1536]{2,1,0:T(8,128)(2,1)S(1)}, bf16[4,96,1536]{2,1,0:T(8,128)(2,1)}, u32[]{:S(2)}, u32[]{:S(2)}) collective-permute-start(bf16[4,96,1536]{2,1,0:T(8,128)(2,1)S(1)} %constant_dynamic-update-slice_fusion.11.refs_4_.refs_0_), channel_id=1, source_target_pairs={{0,2},{1,5},{2,0},{3,7},{4,6},{5,1},{6,4},{7,3},{8,10},{9,13},{10,... | collective-permute-start | bytes 3538952 | tf_op jit(solution)/shard_map/ppermute | solution.py:73
  130.2 23.6 %collective-permute-start.26 = (bf16[4,96,1536]{2,1,0:T(8,128)(2,1)}, bf16[4,96,1536]{2,1,0:T(8,128)(2,1)}, u32[]{:S(2)}, u32[]{:S(2)}) collective-permute-start(bf16[4,96,1536]{2,1,0:T(8,128)(2,1)} %collective-permute-done.24.refs_5_.refs_1_), channel_id=1, source_target_pairs={{0,2},{1,5},{2,0},{3,7},{4,6},{5,1},{6,4},{7,3},{8,10},{9,13},{10,... | collective-permute-start | bytes 3538952 | tf_op jit(solution)/shard_map/ppermute | solution.py:73
  131.5 37.0 %all-to-all-start = ((bf16[8,192,384]{2,1,0:T(8,128)(2,1)}), bf16[8,192,384]{2,1,0:T(8,128)(2,1)S(1)}, u32[]{:S(2)}, u32[]{:S(2)}) async-start(bf16[8,192,384]{2,1,0:T(8,128)(2,1)} %pad_maximum_fusion.1), calls=%async_computation | async-start | bytes 2359296 | tf_op jit(solution)/shard_map/all_to_all | solution.py:949
  142.8 15.1 %collective-permute-start.28 = (bf16[4,96,1536]{2,1,0:T(8,128)(2,1)}, bf16[4,96,1536]{2,1,0:T(8,128)(2,1)S(1)}, u32[]{:S(2)}, u32[]{:S(2)}) collective-permute-start(bf16[4,96,1536]{2,1,0:T(8,128)(2,1)} %collective-permute-done.24.refs_5_.refs_1_), channel_id=1, source_target_pairs={{0,1},{1,0},{2,3},{3,2},{4,5},{5,4},{6,7},{7,6},{8,9},{9,8},{10,11... | collective-permute-start | bytes 3538952 | tf_op jit(solution)/shard_map/ppermute | solution.py:73
  190.1 16.4 %collective-permute-start.34 = (bf16[4,48,1536]{2,1,0:T(8,128)(2,1)S(1)}, bf16[4,48,1536]{2,1,0:T(8,128)(2,1)S(1)}, u32[]{:S(2)}, u32[]{:S(2)}) collective-permute-start(bf16[4,48,1536]{2,1,0:T(8,128)(2,1)S(1)} %pad_maximum_fusion.4.refs_0_), channel_id=1, source_target_pairs={{0,4},{1,3},{2,6},{3,1},{4,0},{5,7},{6,2},{7,5},{8,12},{9,11},{10,... | collective-permute-start | bytes 1769480 | tf_op jit(solution)/shard_map/ppermute | solution.py:73
  228.7 20.0 %collective-permute-start.40 = (bf16[8,48,1536]{2,1,0:T(8,128)(2,1)}, bf16[8,48,1536]{2,1,0:T(8,128)(2,1)}, u32[]{:S(2)}, u32[]{:S(2)}) collective-permute-start(bf16[8,48,1536]{2,1,0:T(8,128)(2,1)} %get-tuple-element.149), channel_id=1, source_target_pairs={{0,1},{1,0},{2,3},{3,2},{4,5},{5,4},{6,7},{7,6},{8,9},{9,8},{10,11... | collective-permute-start | bytes 3538952 | tf_op jit(solution)/shard_map/ppermute | solution.py:73
  240.0 16.3 %collective-permute-start.42 = (bf16[8,48,1536]{2,1,0:T(8,128)(2,1)S(1)}, bf16[8,48,1536]{2,1,0:T(8,128)(2,1)S(1)}, u32[]{:S(2)}, u32[]{:S(2)}) collective-permute-start(bf16[8,48,1536]{2,1,0:T(8,128)(2,1)S(1)} %add_convert_fusion.4), channel_id=1, source_target_pairs={{0,2},{1,5},{2,0},{3,7},{4,6},{5,1},{6,4},{7,3},{8,10},{9,13},{10,... | collective-permute-start | bytes 3538952 | tf_op jit(solution)/shard_map/ppermute | solution.py:73
  310.1 20.0 %collective-permute-start.49 = (bf16[8,96,1536]{2,1,0:T(8,128)(2,1)}, bf16[8,96,1536]{2,1,0:T(8,128)(2,1)}, u32[]{:S(2)}, u32[]{:S(2)}) collective-permute-start(bf16[8,96,1536]{2,1,0:T(8,128)(2,1)} %get-tuple-element.184), channel_id=1, source_target_pairs={{0,1},{1,0},{2,3},{3,2},{4,5},{5,4},{6,7},{7,6},{8,9},{9,8},{10,11... | collective-permute-start | bytes 7077896 | tf_op jit(solution)/shard_map/ppermute | solution.py:73
  310.5 19.7 %collective-permute-start.50 = (bf16[8,96,1536]{2,1,0:T(8,128)(2,1)}, bf16[8,96,1536]{2,1,0:T(8,128)(2,1)}, u32[]{:S(2)}, u32[]{:S(2)}) collective-permute-start(bf16[8,96,1536]{2,1,0:T(8,128)(2,1)} %get-tuple-element.186), channel_id=1, source_target_pairs={{0,1},{1,0},{2,3},{3,2},{4,5},{5,4},{6,7},{7,6},{8,9},{9,8},{10,11... | collective-permute-start | bytes 7077896 | tf_op jit(solution)/shard_map/ppermute | solution.py:73
  310.7 33.8 %all-to-all-start.1 = ((bf16[8,192,384]{2,1,0:T(8,128)(2,1)}), bf16[8,192,384]{2,1,0:T(8,128)(2,1)S(1)}, u32[]{:S(2)}, u32[]{:S(2)}) async-start(bf16[8,192,384]{2,1,0:T(8,128)(2,1)} %pack_back.1), calls=%async_computation.1 | async-start | bytes 2359296 | tf_op jit(solution)/shard_map/all_to_all | solution.py:981
  344.5 29.2 %collective-permute-start.51 = (bf16[8,96,1536]{2,1,0:T(8,128)(2,1)}, bf16[8,96,1536]{2,1,0:T(8,128)(2,1)}, u32[]{:S(2)}, u32[]{:S(2)}) collective-permute-start(bf16[8,96,1536]{2,1,0:T(8,128)(2,1)} %add_convert_fusion.1), channel_id=1, source_target_pairs={{0,2},{1,5},{2,0},{3,7},{4,6},{5,1},{6,4},{7,3},{8,10},{9,13},{10,... | collective-permute-start | bytes 7077896 | tf_op jit(solution)/shard_map/ppermute | solution.py:73
  376.1 17.4 %collective-permute-start.52 = (bf16[4,96,1536]{2,1,0:T(8,128)(2,1)S(1)}, bf16[4,96,1536]{2,1,0:T(8,128)(2,1)S(1)}, u32[]{:S(2)}, u32[]{:S(2)}) collective-permute-start(bf16[4,96,1536]{2,1,0:T(8,128)(2,1)S(1)} %add_convert_fusion.3), channel_id=1, source_target_pairs={{0,4},{1,3},{2,6},{3,1},{4,0},{5,7},{6,2},{7,5},{8,12},{9,11},{10,... | collective-permute-start | bytes 3538952 | tf_op jit(solution)/shard_map/ppermute | solution.py:73
  408.6 30.3 %collective-permute-start.63 = (bf16[8,96,1536]{2,1,0:T(8,128)(2,1)S(1)}, bf16[8,96,1536]{2,1,0:T(8,128)(2,1)}, u32[]{:S(2)}, u32[]{:S(2)}) collective-permute-start(bf16[8,96,1536]{2,1,0:T(8,128)(2,1)S(1)} %add_convert_fusion), channel_id=1, source_target_pairs={{0,2},{1,5},{2,0},{3,7},{4,6},{5,1},{6,4},{7,3},{8,10},{9,13},{10,... | collective-permute-start | bytes 7077896 | tf_op jit(solution)/shard_map/ppermute | solution.py:73
  437.3 15.1 %collective-permute-start.56 = (bf16[1,96,1536]{2,1,0:T(8,128)(2,1)S(1)}, bf16[1,96,1536]{2,1,0:T(8,128)(2,1)S(1)}, u32[]{:S(2)}, u32[]{:S(2)}) collective-permute-start(bf16[1,96,1536]{2,1,0:T(8,128)(2,1)S(1)} %add_convert_fusion.9), channel_id=1, source_target_pairs={{0,16},{1,17},{2,18},{3,19},{4,20},{5,21},{6,22},{7,23},{8,24},{9,... | collective-permute-start | bytes 884744 | tf_op jit(solution)/shard_map/ppermute | solution.py:73
  442.2 17.0 %collective-permute-start.69 = (bf16[4,96,1536]{2,1,0:T(8,128)(2,1)S(1)}, bf16[4,96,1536]{2,1,0:T(8,128)(2,1)S(1)}, u32[]{:S(2)}, u32[]{:S(2)}) collective-permute-start(bf16[4,96,1536]{2,1,0:T(8,128)(2,1)S(1)} %add_convert_fusion.2), channel_id=1, source_target_pairs={{0,4},{1,3},{2,6},{3,1},{4,0},{5,7},{6,2},{7,5},{8,12},{9,11},{10,... | collective-permute-start | bytes 3538952 | tf_op jit(solution)/shard_map/ppermute | solution.py:73
  461.7 14.6 %collective-permute-start.70 = (bf16[2,96,1536]{2,1,0:T(8,128)(2,1)}, bf16[2,96,1536]{2,1,0:T(8,128)(2,1)}, u32[]{:S(2)}, u32[]{:S(2)}) collective-permute-start(bf16[2,96,1536]{2,1,0:T(8,128)(2,1)} %add_convert_fusion.5), channel_id=1, source_target_pairs={{0,8},{1,9},{2,10},{3,11},{4,12},{5,13},{6,14},{7,15},{8,0},{9,1},... | collective-permute-start | bytes 1769480 | tf_op jit(solution)/shard_map/ppermute | solution.py:73
  477.8 14.4 %collective-permute-start.71 = (bf16[1,96,1536]{2,1,0:T(8,128)(2,1)S(1)}, bf16[1,96,1536]{2,1,0:T(8,128)(2,1)S(1)}, u32[]{:S(2)}, u32[]{:S(2)}) collective-permute-start(bf16[1,96,1536]{2,1,0:T(8,128)(2,1)S(1)} %add_convert_fusion.8), channel_id=1, source_target_pairs={{0,16},{1,17},{2,18},{3,19},{4,20},{5,21},{6,22},{7,23},{8,24},{9,... | collective-permute-start | bytes 884744 | tf_op jit(solution)/shard_map/ppermute | solution.py:73
  (132 other events, 1214.0 us)
